TPU v7x, 32 devices: a whole 2x2x4 slice. The times are simulated.
32 devices in a mesh: dp: 8 (over y, x, core), tensor: 4 (over z).
Axes of the slice: x: 2, y: 2, z: 4, core: 2. Of those that a mesh axis runs over, the one named last changes fastest.
Arguments:
- gate_pre: bfloat16 [4096, 3584], P('dp', 'tensor'), may hold values from -6 to 6
- up_pre: bfloat16 [4096, 3584], P('dp', 'tensor'), may hold values from -6 to 6
- down_weight: bfloat16 [3584, 4096], P('tensor'), may hold values from -0.09375 to 0.09375
- grad_out: bfloat16 [4096, 4096], P(('dp', 'tensor')), may hold values from -6 to 6
Outputs:
- ffn_out: bfloat16 [4096, 4096], P(('dp', 'tensor'))
- grad_gate: bfloat16 [4096, 3584], P('dp', 'tensor')
- grad_up: bfloat16 [4096, 3584], P('dp', 'tensor')
- grad_down: float32 [3584, 4096], P('tensor', 'dp')
All inputs are finite; a program needn't handle non-finite values.
Results may differ from a plain program's by a relative error of at most 0.017.
Values may be sent and summed in bfloat16 or wider, within the bound.
No kernel may reach another device: no remote copies, remote signals or barrier semaphores. Data moves between devices by JAX's collectives and lax.ppermute only.
A program may use at most 128 MiB of HBM per device.

v0:
```python
import math

import jax
import jax.numpy as jnp
from jax import lax
from jax.sharding import PartitionSpec as P


def body(gate_pre, up_pre, down_weight, grad_out):
    gate_val = gate_pre.astype(jnp.float32)
    up_val = up_pre.astype(jnp.float32)
    sigmoid_gate = jax.nn.sigmoid(gate_val)
    activated = gate_val * sigmoid_gate
    hidden = (activated * up_val).astype(jnp.bfloat16)
    replica_rows = hidden.shape[0]
    grad_scale = 1.0 / math.sqrt(replica_rows * lax.axis_size("dp"))
    hidden_rows = hidden
    ffn_out = lax.psum_scatter(
        jnp.dot(hidden_rows, down_weight, preferred_element_type=jnp.float32).astype(jnp.bfloat16),
        "tensor",
        scatter_dimension=0,
        tiled=True,
    )
    piece = lax.all_gather(grad_out, "tensor", axis=0, tiled=True)
    product = jnp.einsum("td,fd->tf", piece, down_weight, preferred_element_type=jnp.float32)
    hidden_grad = product
    hidden_rows = hidden
    weight_grad = jnp.einsum("tf,td->fd", hidden_rows, piece, preferred_element_type=jnp.float32)
    hidden_grad, weight_grad = (hidden_grad, weight_grad)
    grad_down = lax.psum_scatter(
        (weight_grad * grad_scale).astype(jnp.bfloat16), "dp", scatter_dimension=1, tiled=True
    ).astype(jnp.float32)
    grad_gate = (
        hidden_grad * up_val * sigmoid_gate * (1.0 + gate_val * (1.0 - sigmoid_gate))
    ).astype(jnp.bfloat16)
    grad_up = (hidden_grad * activated).astype(jnp.bfloat16)
    return (ffn_out, grad_gate, grad_up, grad_down)


def solution(mesh):
    return jax.shard_map(
        body,
        mesh=mesh,
        in_specs=(
            P("dp", "tensor"),
            P("dp", "tensor"),
            P("tensor", None),
            P(("dp", "tensor"), None),
        ),
        out_specs=(
            P(("dp", "tensor"), None),
            P("dp", "tensor"),
            P("dp", "tensor"),
            P("tensor", "dp"),
        ),
        check_vma=False,
    )
```

profile of v0, /device:TPU:12, one launch (start us, length us, event | category | flops | bytes accessed | tf_op | source)
XLA Modules:
  0.0 253.3 jit_solution(4457046848337273817)
XLA Ops:
  7.2 0.0 all-gather.2.cloned.1.call-start
  7.2 0.7 all-gather.2.cloned.1.call-update
  7.9 0.0 reduce-scatter.5.cloned.1.call-start
  7.9 81.1 %all-gather.2.cloned.1.call-done = bf16[512,4096]{1,0:T(8,128)(2,1)} async-done(((bf16[128,4096]{1,0:T(8,128)(2,1)}), bf16[512,4096]{1,0:T(8,128)(2,1)}) %all-gather.2.cloned.1.call-update) | async-done | bytes 4194320 | tf_op jit(solution)/shard_map/all_gather | solution.py:24
  89.0 9.8 %multiply_convert_fusion = bf16[896,4096]{1,0:T(8,128)(2,1)} fusion(bf16[512,4096]{1,0:T(8,128)(2,1)} %all-gather.2.cloned.1.call-done, bf16[512,896]{1,0:T(8,128)(2,1)} %param.5, bf16[512,896]{1,0:T(8,128)(2,1)} %param.4), kind=kOutput, calls=%fused_computation | convolution fusion | flops 3769106432 | bytes 13369344 | tf_op jit(solution)/shard_map/tf,td->fd/dot_general | solution.py:28
  98.9 0.0 copy-start
  98.9 0.0 copy-start.1
  98.9 0.0 reduce-scatter.5.cloned.1.call-update
  98.9 0.0 reduce-scatter.3.cloned.1.call-start
  99.0 1.1 copy-done
  100.1 0.3 copy-done.1
  100.3 9.2 %convolution_convert_fusion = bf16[512,4096]{1,0:T(8,128)(2,1)} fusion(bf16[896,4096]{1,0:T(8,128)(2,1)} %param.6, bf16[512,896]{1,0:T(8,128)(2,1)S(1)} %copy-done, bf16[512,896]{1,0:T(8,128)(2,1)S(1)} %copy-done.1), kind=kOutput, calls=%fused_computation.1 | convolution fusion | flops 3763863552 | bytes 13369344 | tf_op jit(solution)/shard_map/dot_general | solution.py:19
  109.6 0.0 reduce-scatter.3.cloned.1.call-update
  109.6 12.4 %multiply_convert_fusion.1 = (bf16[512,896]{1,0:T(8,128)(2,1)}, bf16[512,896]{1,0:T(8,128)(2,1)}) fusion(bf16[512,896]{1,0:T(8,128)(2,1)S(1)} %copy-done.1, bf16[512,896]{1,0:T(8,128)(2,1)S(1)} %copy-done, bf16[512,4096]{1,0:T(8,128)(2,1)} %all-gather.2.cloned.1.call-done, bf16[896,4096]{1,0:T(8,128)(2,1)} %param.6), kind=kOutput, calls=%fused_computation.15 | convolution fusion | flops 3764977664 | bytes 15204352 | tf_op jit(solution)/shard_map/td,fd->tf/dot_general | solution.py:25
  122.0 44.9 %reduce-scatter.5.cloned.1.call-done = bf16[896,512]{1,0:T(8,128)(2,1)} async-done(((bf16[896,4096]{1,0:T(8,128)(2,1)}), bf16[896,512]{1,0:T(8,128)(2,1)}) %reduce-scatter.5.cloned.1.call-update) | async-done | bytes 917520 | tf_op jit(solution)/shard_map/reduce_scatter | solution.py:30
  166.9 2.7 %convert_element_type.31 = f32[896,512]{1,0:T(8,128)} convert(bf16[896,512]{1,0:T(8,128)(2,1)} %reduce-scatter.5.cloned.1.call-done) | non-fusion elementwise | flops 458752 | bytes 2752512 | tf_op jit(solution)/shard_map/convert_element_type | solution.py:32
  169.5 77.2 %reduce-scatter.3.cloned.1.call-done = bf16[128,4096]{1,0:T(8,128)(2,1)} async-done(((bf16[512,4096]{1,0:T(8,128)(2,1)}), bf16[128,4096]{1,0:T(8,128)(2,1)}) %reduce-scatter.3.cloned.1.call-update) | async-done | bytes 1048592 | tf_op jit(solution)/shard_map/reduce_scatter | solution.py:18
Async XLA Ops:
  7.2 81.9 %all-gather.2.cloned.1.call-start = ((), (), s32[]{:S(2)}) async-start(), calls=%async_computation.3 | async-start | bytes 5242880 | tf_op jit(solution)/shard_map/all_gather | solution.py:24
  7.9 159.0 %reduce-scatter.5.cloned.1.call-start = ((), (), s32[]{:S(2)}) async-start(), calls=%async_computation.4 | async-start | bytes 8257536 | tf_op jit(solution)/shard_map/reduce_scatter | solution.py:30
  98.9 1.2 copy-start
  98.9 1.5 copy-start.1
  98.9 147.8 %reduce-scatter.3.cloned.1.call-start = ((), (), s32[]{:S(2)}) async-start(), calls=%async_computation.2 | async-start | bytes 5242880 | tf_op jit(solution)/shard_map/reduce_scatter | solution.py:18
Sparse Core Ops, SparseCore 0:
  9.6 79.4 all-gather.1
  99.0 67.7 reduce-scatter.4
  169.8 76.8 reduce-scatter.2
where the time goes:
time: 255 us; the launch traced here: 253 us
  waiting for transfers between devices  204 us (80%)
  matrix products  31.5 us (12%)
  between operations  13.7 us (5%)
  other arithmetic  2.66 us (1%)
    all_gather x1, waiting for transfers between devices, body(): piece = lax.all_gather(grad_out, 'tensor', axis=0, tiled=True)  81.1 us
    reduce_scatter x1, waiting for transfers between devices, body(): lax.psum_scatter(jnp.dot(hidden_rows, down_weight, preferred_element_type...  77.2 us
    reduce_scatter x1, waiting for transfers between devices, body(): lax.psum_scatter((weight_grad * grad_scale).astype(jnp.bfloat16), 'dp', s...  44.9 us
    dot_general x1, matrix products, body(): jnp.einsum('td,fd->tf', piece, down_weight, preferred_element_type=jnp.fl...  12.4 us
    dot_general x1, matrix products, body(): jnp.einsum('tf,td->fd', hidden_rows, piece, preferred_element_type=jnp.fl...  9.85 us
    dot_general x1, matrix products, body(): jnp.dot(hidden_rows, down_weight, preferred_element_type=jnp.float32)  9.22 us
  transfers between devices with their start and end apart: 3, of which 3 were waited for; matrix products, arithmetic and copies ran while one was open for 10% of the time, Pallas kernels for 0%

commit v1 on v0

v1 whole, which is shorter than its diff:
```python
import functools
import math

import jax
import jax.numpy as jnp
from jax import lax
from jax.experimental import pallas as pl
from jax.experimental.pallas import tpu as pltpu
from jax.sharding import PartitionSpec as P

F32, BF16 = jnp.float32, jnp.bfloat16
VMEM_BYTES = 48 * 1024 * 1024


def plain_body(gate_pre, up_pre, down_weight, grad_out):
    gate_val = gate_pre.astype(F32)
    up_val = up_pre.astype(F32)
    sigmoid_gate = jax.nn.sigmoid(gate_val)
    activated = gate_val * sigmoid_gate
    hidden = (activated * up_val).astype(BF16)
    grad_scale = 1.0 / math.sqrt(hidden.shape[0] * lax.axis_size("dp"))
    ffn_out = lax.psum_scatter(
        jnp.dot(hidden, down_weight, preferred_element_type=F32).astype(BF16),
        "tensor",
        scatter_dimension=0,
        tiled=True,
    )
    piece = lax.all_gather(grad_out, "tensor", axis=0, tiled=True)
    hidden_grad = jnp.einsum("td,fd->tf", piece, down_weight, preferred_element_type=F32)
    weight_grad = jnp.einsum("tf,td->fd", hidden, piece, preferred_element_type=F32)
    grad_down = lax.psum_scatter(
        (weight_grad * grad_scale).astype(BF16), "dp", scatter_dimension=1, tiled=True
    ).astype(F32)
    grad_gate = (
        hidden_grad * up_val * sigmoid_gate * (1.0 + gate_val * (1.0 - sigmoid_gate))
    ).astype(BF16)
    grad_up = (hidden_grad * activated).astype(BF16)
    return (ffn_out, grad_gate, grad_up, grad_down)


OUTER = [(0, 1), (1, 0), (2, 3), (3, 2)]
OUTWARD = [(1, 0), (2, 3)]
INWARD = [(0, 1), (3, 2)]
MIDDLE = [(1, 2), (2, 1)]


def hidden_kernel(place, gate_ref, up_ref, hidden_ref, turned_ref):
    gate_val = gate_ref[...].astype(F32)
    hidden = gate_val * jax.nn.sigmoid(gate_val) * up_ref[...].astype(F32)
    hidden_ref[...] = hidden.astype(BF16)
    turned_ref[...] = hidden.T.astype(BF16)


def hidden_of(place, gate_pre, up_pre):
    rows, width = gate_pre.shape
    block = rows // 4
    return pl.pallas_call(
        hidden_kernel,
        grid_spec=pltpu.PrefetchScalarGridSpec(
            num_scalar_prefetch=1,
            grid=(4,),
            in_specs=[pl.BlockSpec((block, width), lambda i, place: (place[i], 0))] * 2,
            out_specs=[
                pl.BlockSpec((block, width), lambda i, place: (i, 0)),
                pl.BlockSpec((width, block), lambda i, place: (0, i)),
            ],
        ),
        out_shape=[
            jax.ShapeDtypeStruct((rows, width), BF16),
            jax.ShapeDtypeStruct((width, rows), BF16),
        ],
        cost_estimate=pl.CostEstimate(flops=10 * rows * width, bytes_accessed=8 * rows * width, transcendentals=rows * width),
        compiler_params=pltpu.CompilerParams(vmem_limit_bytes=VMEM_BYTES),
        name="hidden",
    )(place, gate_pre, up_pre)


def forward_kernel(hidden_ref, weight_ref, *out_refs):
    block = out_refs[0].shape[0]
    product = jnp.dot(hidden_ref[...], weight_ref[...], preferred_element_type=F32)
    for i, out_ref in enumerate(out_refs):
        out_ref[...] = product[i * block : (i + 1) * block].astype(BF16)


def forward_of(hidden, weight, tile=512):
    rows, width = hidden.shape
    model = weight.shape[1]
    block = rows // 4
    return pl.pallas_call(
        forward_kernel,
        grid=(model // tile,),
        in_specs=[
            pl.BlockSpec((rows, width), lambda j: (0, 0)),
            pl.BlockSpec((width, tile), lambda j: (0, j)),
        ],
        out_specs=[pl.BlockSpec((block, tile), lambda j: (0, j))] * 4,
        out_shape=[jax.ShapeDtypeStruct((block, model), BF16)] * 4,
        cost_estimate=pl.CostEstimate(
            flops=2 * rows * width * model, bytes_accessed=2 * (rows * model + width * model), transcendentals=0
        ),
        compiler_params=pltpu.CompilerParams(vmem_limit_bytes=VMEM_BYTES),
        name="forward",
    )(hidden, weight)


def gathered(edge, own, outer, mid_e, mid_m, far_e, far_m):
    return jnp.concatenate(
        [
            own[...],
            outer[...],
            jnp.where(edge, mid_e[...], mid_m[...]),
            jnp.where(edge, far_e[...], far_m[...]),
        ],
        axis=0,
    )


def weight_kernel(scale, place, turned_ref, *refs):
    out_ref = refs[6]
    piece = gathered(place[4] == 1, *refs[:6])
    product = jnp.dot(turned_ref[...], piece, preferred_element_type=F32)
    out_ref[0] = (product * scale).astype(BF16)


def weight_grad_of(place, turned, blocks, scale, odd, n_dp):
    width, rows = turned.shape
    block, columns = blocks[0].shape
    tile = columns // n_dp
    return pl.pallas_call(
        functools.partial(weight_kernel, scale),
        grid_spec=pltpu.PrefetchScalarGridSpec(
            num_scalar_prefetch=1,
            grid=(n_dp // 2,),
            in_specs=[pl.BlockSpec((width, rows), lambda i, place: (0, 0))]
            + [pl.BlockSpec((block, tile), lambda i, place: (0, jnp.bitwise_xor(place[5], 2 * i + odd)))] * 6,
            out_specs=pl.BlockSpec((1, width, tile), lambda i, place: (i, 0, 0)),
        ),
        out_shape=jax.ShapeDtypeStruct((n_dp // 2, width, tile), BF16),
        cost_estimate=pl.CostEstimate(
            flops=rows * width * columns, bytes_accessed=width * columns + 3 * rows * columns // 2, transcendentals=0
        ),
        compiler_params=pltpu.CompilerParams(vmem_limit_bytes=VMEM_BYTES),
        name="weight_grad",
    )(place, turned, *blocks)


def input_kernel(tiles, place, weight_ref, gate_ref, up_ref, *refs):
    step = pl.program_id(0)
    grad_gate_ref, grad_up_ref, total_ref = refs[-3:]
    edge = place[4] == 1
    start, part = 0, None
    for n, tile in enumerate(tiles):
        piece = gathered(edge, *refs[6 * n : 6 * n + 6])
        product = lax.dot_general(
            piece, weight_ref[:, start : start + tile], (((1,), (1,)), ((), ())), preferred_element_type=F32
        )
        part = product if part is None else part + product
        start += tile

    @pl.when(step == 0)
    def _():
        total_ref[...] = part

    @pl.when(step > 0)
    def _():
        total_ref[...] += part

    @pl.when(step == pl.num_programs(0) - 1)
    def _():
        block = total_ref.shape[0] // 4
        for i in range(4):
            rows = pl.ds(pl.multiple_of(place[i] * block, block), block)
            hidden_grad = total_ref[i * block : (i + 1) * block]
            gate_val = gate_ref[rows].astype(F32)
            up_val = up_ref[rows].astype(F32)
            s = jax.nn.sigmoid(gate_val)
            grad_gate_ref[rows] = (hidden_grad * up_val * s * (1.0 + gate_val * (1.0 - s))).astype(BF16)
            grad_up_ref[rows] = (hidden_grad * (gate_val * s)).astype(BF16)


def input_grads_of(place, weight, gate_pre, up_pre, parts, n_dp):
    rows, width = gate_pre.shape
    model = weight.shape[1]
    tiles = [blocks[0].shape[1] // n_dp for blocks in parts]
    whole = pl.BlockSpec((rows, width), lambda j, place: (0, 0))
    return pl.pallas_call(
        functools.partial(input_kernel, tiles),
        grid_spec=pltpu.PrefetchScalarGridSpec(
            num_scalar_prefetch=1,
            grid=(n_dp,),
            in_specs=[pl.BlockSpec((width, model // n_dp), lambda j, place: (0, j)), whole, whole]
            + [
                pl.BlockSpec((rows // 4, tile), lambda j, place: (0, j))
                for tile in tiles
                for _ in range(6)
            ],
            out_specs=[whole, whole],
            scratch_shapes=[pltpu.VMEM((rows, width), F32)],
        ),
        out_shape=[jax.ShapeDtypeStruct((rows, width), BF16)] * 2,
        cost_estimate=pl.CostEstimate(
            flops=2 * rows * width * model,
            bytes_accessed=2 * width * model + 3 * rows * model + 8 * rows * width,
            transcendentals=rows * width,
        ),
        compiler_params=pltpu.CompilerParams(vmem_limit_bytes=VMEM_BYTES),
        name="input_grads",
    )(place, weight, gate_pre, up_pre, *(b for blocks in parts for b in blocks))


def add(*terms):
    return functools.reduce(lambda a, b: a + b, [t.astype(F32) for t in terms])


def line_body(n_dp, n_tensor, gate_pre, up_pre, down_weight, grad_out):
    place_z = lax.axis_index("tensor")
    me = lax.axis_index("dp")
    outer = jnp.bitwise_xor(place_z, 1)
    edge = (place_z == 0) | (place_z == 3)
    other_mid = jnp.where(edge, 3 - outer, 3 - place_z)
    other_edge = jnp.where(edge, 3 - place_z, 3 - outer)
    place = jnp.stack([place_z, outer, other_mid, other_edge, edge.astype(jnp.int32), me]).astype(jnp.int32)
    rows, model = gate_pre.shape[0], grad_out.shape[1]
    scale = 1.0 / math.sqrt(rows * n_dp)

    def along(pairs):
        return lambda v: lax.ppermute(v, "tensor", pairs)

    both, outward, inward, middle = along(OUTER), along(OUTWARD), along(INWARD), along(MIDDLE)

    def flip(bit):
        return lambda v: lax.ppermute(v, "dp", [(i, i ^ bit) for i in range(n_dp)])

    flip_core, flip_x, flip_y = flip(1), flip(2), flip(4)

    share = model // n_dp
    half = share // 2
    parts = []
    for c in range(2):
        own = jnp.concatenate(
            [grad_out[:, j * share + c * half : j * share + (c + 1) * half] for j in range(n_dp)], axis=1
        )
        parts.append([own, both(own), middle(own)])
    hidden, turned = hidden_of(place, gate_pre, up_pre)
    partial = forward_of(hidden, down_weight)
    for part in parts:
        own, p1, q1 = part
        p2 = outward(q1)
        q2 = middle(p1)
        p3 = outward(q2)
        part[:] = [own, p1, p2, q1, p3, q2]

    r1 = inward(partial[3])
    r2 = inward(partial[2])
    m1 = middle(add(partial[3], r1).astype(BF16))
    m2 = middle(add(partial[2], r2).astype(BF16))
    r3 = both(add(partial[1], m1).astype(BF16))
    ffn_out = add(partial[0], r3, m2).astype(BF16)

    columns = []
    for part in parts:
        send = weight_grad_of(place, turned, part, scale, 1, n_dp)
        got = flip_core(send)
        keep = weight_grad_of(place, turned, part, scale, 0, n_dp)
        top = keep.shape[1] // 2
        x_out = add(keep[1::2, :top], got[1::2, :top]).astype(BF16)
        y_out = add(keep[2:, top:], got[2:, top:]).astype(BF16)
        x_in = flip_x(x_out)
        y_in = flip_y(y_out)
        x_then_y = flip_y(add(keep[2, :top], got[2, :top], x_in[1]).astype(BF16))
        y_then_x = flip_x(add(keep[1, top:], got[1, top:], y_in[1]).astype(BF16))
        columns.append(
            jnp.concatenate(
                [
                    add(keep[0, :top], got[0, :top], x_in[0], x_then_y),
                    add(keep[0, top:], got[0, top:], y_in[0], y_then_x),
                ],
                axis=0,
            )
        )
    grad_down = jnp.concatenate(columns, axis=1)
    grad_gate, grad_up = input_grads_of(place, down_weight, gate_pre, up_pre, parts, n_dp)
    return (ffn_out, grad_gate, grad_up, grad_down)


def solution(mesh):
    n_dp, n_tensor = mesh.shape["dp"], mesh.shape["tensor"]
    on_line = n_dp == 8 and n_tensor == 4
    return jax.shard_map(
        functools.partial(line_body, n_dp, n_tensor) if on_line else plain_body,
        mesh=mesh,
        in_specs=(
            P("dp", "tensor"),
            P("dp", "tensor"),
            P("tensor", None),
            P(("dp", "tensor"), None),
        ),
        out_specs=(
            P(("dp", "tensor"), None),
            P("dp", "tensor"),
            P("dp", "tensor"),
            P("tensor", "dp"),
        ),
        check_vma=False,
    )
```

time: 255 us -> 188 us (0.74)
  waiting for transfers between devices: 204 us -> 90 us
  starting transfers between devices: 0.12 us -> 41.2 us
  Pallas kernels: 0 us -> 33.7 us
  matrix products: 31.5 us -> 0 us
  other arithmetic: 2.66 us -> 17.2 us
  between operations: 13.7 us -> 0.97 us
    reduce_scatter x2 -> x0, waiting for transfers between devices: 122 us -> none  [the longest x1 77.2 us: body(): lax.psum_scatter(jnp.dot(hidden_rows, down_weight, preferred_element_type...]
    ppermute x0 -> x25, waiting for transfers between devices: none -> 90 us  [the longest x15 71.5 us: along(): return lambda v: lax.ppermute(v, 'tensor', pairs)]
    all_gather x1 -> x0, waiting for transfers between devices: 81.1 us -> none  [body(): piece = lax.all_gather(grad_out, 'tensor', axis=0, tiled=True)]
    ppermute x0 -> x25, starting transfers between devices: none -> 41.2 us  [the longest x15 34.1 us: along(): return lambda v: lax.ppermute(v, 'tensor', pairs)]
    pallas_call x0 -> x7, Pallas kernels: none -> 33.7 us  [the longest x1 12.9 us: input_grads_of(): pl.pallas_call(functools.partial(input_kernel, tiles), grid_spec=pltpu.Pr...]
    dot_general x3 -> x0, matrix products: 31.5 us -> none  [the longest x1 12.4 us: body(): jnp.einsum('td,fd->tf', piece, down_weight, preferred_element_type=jnp.fl...]
    convert_element_type x1 -> x8, other arithmetic: 2.66 us -> 13.2 us  [the longest x1 2.99 us: line_body(): ffn_out = add(partial[0], r3, m2).astype(BF16)]
  transfers between devices with their start and end apart: 3 -> 25, of which waited for: 3 -> 11; matrix products, arithmetic and copies ran while one was open for 10% -> 8% of each run, Pallas kernels for 0% -> 13%
where the time goes in v1:
time: 188 us; the launch traced here: 186 us
  waiting for transfers between devices  90 us (48%)
  starting transfers between devices  41.2 us (22%)
  Pallas kernels  33.7 us (18%)
  other arithmetic  17.2 us (9%)
  local copies, waits for them, and re-layouts  2.55 us (1%)
    ppermute x15, waiting for transfers between devices, along(): return lambda v: lax.ppermute(v, 'tensor', pairs)  71.5 us
    ppermute x15, starting transfers between devices, along(): return lambda v: lax.ppermute(v, 'tensor', pairs)  34.1 us
    ppermute x10, waiting for transfers between devices, flip(): return lambda v: lax.ppermute(v, 'dp', [(i, i ^ bit) for i in range(n_dp)])  18.5 us
    pallas_call x1, Pallas kernels, input_grads_of(): pl.pallas_call(functools.partial(input_kernel, tiles), grid_spec=pltpu.Pr...  12.9 us
    pallas_call x4, Pallas kernels, weight_grad_of(): pl.pallas_call(functools.partial(weight_kernel, scale), grid_spec=pltpu.P...  10.6 us
    pallas_call x1, Pallas kernels, forward_of(): pl.pallas_call(forward_kernel, grid=(model // tile,), in_specs=[pl.BlockS...  8.76 us
    ppermute x10, starting transfers between devices, flip(): return lambda v: lax.ppermute(v, 'dp', [(i, i ^ bit) for i in range(n_dp)])  7.05 us
  transfers between devices with their start and end apart: 25, of which 11 were waited for; matrix products, arithmetic and copies ran while one was open for 8% of the time, Pallas kernels for 13%

profile of v1, /device:TPU:12, one launch (start us, length us, event | category | flops | bytes accessed | tf_op | source)
XLA Modules:
  0.0 185.6 jit_solution(15312010922221945160)
XLA Ops:
  0.6 0.1 stack.31.place
  0.7 1.2 copy-done.1
  1.9 1.2 copy-done.2
  3.1 1.4 hidden.1
  4.5 0.0 copy-start.3
  4.5 8.8 %forward.1 = (bf16[128,4096]{1,0:T(8,128)(2,1)S(1)}, bf16[128,4096]{1,0:T(8,128)(2,1)S(1)}, bf16[128,4096]{1,0:T(8,128)(2,1)S(1)}, bf16[128,4096]{1,0:T(8,128)(2,1)S(1)}) custom-call(bf16[512,896]{1,0:T(8,128)(2,1)S(1)} %get-tuple-element.12.hidden_ref, bf16[896,4096]{1,0:T(8,128)(2,1)} %weight_ref.3), custom_call_target="tpu_custom_call" | custom-call | flops 3758096384 | bytes 11534336 | tf_op jit(solution)/shard_map/forward/pallas_call | solution.py:89
  13.3 1.3 collective-permute-start
  14.8 2.8 %collective-permute-start.5 = (bf16[128,2048]{1,0:T(8,128)(2,1)S(1)}, bf16[128,2048]{1,0:T(8,128)(2,1)S(1)}, u32[]{:S(2)}, u32[]{:S(2)}) collective-permute-start(bf16[128,2048]{1,0:T(8,128)(2,1)S(1)} %get-tuple-element.33.refs_0_), channel_id=1, source_target_pairs={{0,1},{1,0},{2,3},{3,2},{4,5},{5,4},{6,7},{7,6},{8,9},{9,8},{10,11... | collective-permute-start | bytes 1572872 | tf_op jit(solution)/shard_map/ppermute | solution.py:227
  17.5 0.1 collective-permute-start.10
  17.6 3.5 %collective-permute-start.6 = (bf16[128,2048]{1,0:T(8,128)(2,1)S(1)}, bf16[128,2048]{1,0:T(8,128)(2,1)S(1)}, u32[]{:S(2)}, u32[]{:S(2)}) collective-permute-start(bf16[128,2048]{1,0:T(8,128)(2,1)S(1)} %get-tuple-element.33.refs_0_), channel_id=1, source_target_pairs={{1,2},{2,1},{5,6},{6,5},{9,10},{10,9},{13,14},{14,13},{17,18},{18,... | collective-permute-start | bytes 1572872 | tf_op jit(solution)/shard_map/ppermute | solution.py:227
  21.1 2.4 %collective-permute-start.11 = (bf16[128,2048]{1,0:T(8,128)(2,1)S(1)}, bf16[128,2048]{1,0:T(8,128)(2,1)S(1)}, u32[]{:S(2)}, u32[]{:S(2)}) collective-permute-start(bf16[128,2048]{1,0:T(8,128)(2,1)S(1)} %get-tuple-element.32.refs_6_.refs_0_), channel_id=1, source_target_pairs={{1,2},{2,1},{5,6},{6,5},{9,10},{10,9},{13,14},{14,13},{17,18},{18,... | collective-permute-start | bytes 1572872 | tf_op jit(solution)/shard_map/ppermute | solution.py:227
  23.5 29.0 %collective-permute-done.5.refs_1_ = bf16[128,2048]{1,0:T(8,128)(2,1)S(1)} collective-permute-done((bf16[128,2048]{1,0:T(8,128)(2,1)S(1)}, bf16[128,2048]{1,0:T(8,128)(2,1)S(1)}, u32[]{:S(2)}, u32[]{:S(2)}) %collective-permute-start.5) | collective-permute-done | bytes 524320 | tf_op jit(solution)/shard_map/ppermute | solution.py:227
  52.5 3.5 %collective-permute-start.8 = (bf16[128,2048]{1,0:T(8,128)(2,1)S(1)}, bf16[128,2048]{1,0:T(8,128)(2,1)S(1)}, u32[]{:S(2)}, u32[]{:S(2)}) collective-permute-start(bf16[128,2048]{1,0:T(8,128)(2,1)S(1)} %collective-permute-done.5.refs_1_), channel_id=1, source_target_pairs={{1,2},{2,1},{5,6},{6,5},{9,10},{10,9},{13,14},{14,13},{17,18},{18,... | collective-permute-start | bytes 1572872 | tf_op jit(solution)/shard_map/ppermute | solution.py:227
  56.0 6.6 %collective-permute-done.10.refs_7_.refs_1_ = bf16[128,2048]{1,0:T(8,128)(2,1)S(1)} collective-permute-done((bf16[128,2048]{1,0:T(8,128)(2,1)S(1)}, bf16[128,2048]{1,0:T(8,128)(2,1)S(1)}, u32[]{:S(2)}, u32[]{:S(2)}) %collective-permute-start.10) | collective-permute-done | bytes 524320 | tf_op jit(solution)/shard_map/ppermute | solution.py:227
  62.6 3.5 %collective-permute-start.13 = (bf16[128,2048]{1,0:T(8,128)(2,1)S(1)}, bf16[128,2048]{1,0:T(8,128)(2,1)S(1)}, u32[]{:S(2)}, u32[]{:S(2)}) collective-permute-start(bf16[128,2048]{1,0:T(8,128)(2,1)S(1)} %collective-permute-done.10.refs_7_.refs_1_), channel_id=1, source_target_pairs={{1,2},{2,1},{5,6},{6,5},{9,10},{10,9},{13,14},{14,13},{17,18},{18,... | collective-permute-start | bytes 1572872 | tf_op jit(solution)/shard_map/ppermute | solution.py:227
  66.1 1.3 collective-permute-start.3
  67.4 0.0 collective-permute-done.11.refs_9_.refs_3_
  67.4 5.5 %collective-permute-start.7 = (bf16[128,2048]{1,0:T(8,128)(2,1)S(1)}, bf16[128,2048]{1,0:T(8,128)(2,1)S(1)}, u32[]{:S(2)}, u32[]{:S(2)}) collective-permute-start(bf16[128,2048]{1,0:T(8,128)(2,1)S(1)} %collective-permute-done.6.refs_3_), channel_id=1, source_target_pairs={{1,0},{2,3},{5,4},{6,7},{9,8},{10,11},{13,12},{14,15},{17,16},{18,... | collective-permute-start | bytes 1572872 | tf_op jit(solution)/shard_map/ppermute | solution.py:227
  72.9 0.0 collective-permute-done
  72.9 1.3 collective-permute-start.12
  74.2 0.0 collective-permute-done.8.refs_5_
  74.3 1.3 collective-permute-start.9
  75.6 1.7 collective-permute-done.13.refs_11_.refs_5_
  77.2 1.3 collective-permute-start.14
  78.6 1.2 add_convert_fusion.3
  79.8 16.7 %collective-permute-done.12.refs_8_.refs_2_ = bf16[128,2048]{1,0:T(8,128)(2,1)S(1)} collective-permute-done((bf16[128,2048]{1,0:T(8,128)(2,1)S(1)}, bf16[128,2048]{1,0:T(8,128)(2,1)S(1)}, u32[]{:S(2)}, u32[]{:S(2)}) %collective-permute-start.12) | collective-permute-done | bytes 524320 | tf_op jit(solution)/shard_map/ppermute | solution.py:227
  96.5 2.3 %collective-permute-start.1 = (bf16[128,4096]{1,0:T(8,128)(2,1)}, bf16[128,4096]{1,0:T(8,128)(2,1)S(1)}, u32[]{:S(2)}, u32[]{:S(2)}) collective-permute-start(bf16[128,4096]{1,0:T(8,128)(2,1)} %add_convert_fusion.3), channel_id=1, source_target_pairs={{1,2},{2,1},{5,6},{6,5},{9,10},{10,9},{13,14},{14,13},{17,18},{18,... | collective-permute-start | bytes 3145736 | tf_op jit(solution)/shard_map/ppermute | solution.py:227
  98.8 17.5 %collective-permute-done.14.refs_10_.refs_4_ = bf16[128,2048]{1,0:T(8,128)(2,1)S(1)} collective-permute-done((bf16[128,2048]{1,0:T(8,128)(2,1)S(1)}, bf16[128,2048]{1,0:T(8,128)(2,1)S(1)}, u32[]{:S(2)}, u32[]{:S(2)}) %collective-permute-start.14) | collective-permute-done | bytes 524320 | tf_op jit(solution)/shard_map/ppermute | solution.py:227
  116.3 2.7 %weight_grad.7 = bf16[4,896,256]{2,1,0:T(8,128)(2,1)S(1)} custom-call(s32[6]{0:T(128)S(1)} %stack.31.place, bf16[896,512]{1,0:T(8,128)(2,1)S(1)} %get-tuple-element.19.turned_ref, bf16[128,2048]{1,0:T(8,128)(2,1)S(1)} %get-tuple-element.32.refs_6_.refs_0_, bf16[128,2048]{1,0:T(8,128)(2,1)S(1)} %collective-permute-done.10.refs_7_.refs_1_, ...), custom_call_target="tpu_custom_call" | custom-call | flops 939524096 | bytes 3407872 | tf_op jit(solution)/shard_map/weight_grad/pallas_call | solution.py:129
  119.0 0.1 collective-permute-start.20
  119.1 0.0 collective-permute-done.7.refs_2_
  119.1 2.7 %weight_grad.5 = bf16[4,896,256]{2,1,0:T(8,128)(2,1)S(1)} custom-call(s32[6]{0:T(128)S(1)} %stack.31.place, bf16[896,512]{1,0:T(8,128)(2,1)S(1)} %get-tuple-element.19.turned_ref, bf16[128,2048]{1,0:T(8,128)(2,1)S(1)} %get-tuple-element.33.refs_0_, bf16[128,2048]{1,0:T(8,128)(2,1)S(1)} %collective-permute-done.5.refs_1_, ...), custom_call_target="tpu_custom_call" | custom-call | flops 939524096 | bytes 3407872 | tf_op jit(solution)/shard_map/weight_grad/pallas_call | solution.py:129
  121.7 0.5 collective-permute-start.15
  122.3 2.4 %add_convert_fusion.1 = bf16[128,4096]{1,0:T(8,128)(2,1)} fusion(bf16[128,4096]{1,0:T(8,128)(2,1)} %collective-permute-done.3, bf16[128,4096]{1,0:T(8,128)(2,1)S(1)} %get-tuple-element.16), kind=kLoop, calls=%fused_computation.1 | loop fusion | flops 2097152 | bytes 3145728 | tf_op jit(solution)/shard_map/convert_element_type | solution.py:256
  124.7 2.3 %collective-permute-start.4 = (bf16[128,4096]{1,0:T(8,128)(2,1)}, bf16[128,4096]{1,0:T(8,128)(2,1)}, u32[]{:S(2)}, u32[]{:S(2)}) collective-permute-start(bf16[128,4096]{1,0:T(8,128)(2,1)} %add_convert_fusion.1), channel_id=1, source_target_pairs={{1,2},{2,1},{5,6},{6,5},{9,10},{10,9},{13,14},{14,13},{17,18},{18,... | collective-permute-start | bytes 3145736 | tf_op jit(solution)/shard_map/ppermute | solution.py:227
  127.1 1.2 add_convert_fusion.2
  128.3 1.8 collective-permute-start.2
  130.1 2.7 %weight_grad.6 = bf16[4,896,256]{2,1,0:T(8,128)(2,1)S(1)} custom-call(s32[6]{0:T(128)S(1)} %stack.31.place, bf16[896,512]{1,0:T(8,128)(2,1)S(1)} %get-tuple-element.19.turned_ref, bf16[128,2048]{1,0:T(8,128)(2,1)S(1)} %get-tuple-element.32.refs_6_.refs_0_, bf16[128,2048]{1,0:T(8,128)(2,1)S(1)} %collective-permute-done.10.refs_7_.refs_1_, ...), custom_call_target="tpu_custom_call" | custom-call | flops 939524096 | bytes 3407872 | tf_op jit(solution)/shard_map/weight_grad/pallas_call | solution.py:129
  132.7 2.7 %weight_grad.4 = bf16[4,896,256]{2,1,0:T(8,128)(2,1)S(1)} custom-call(s32[6]{0:T(128)S(1)} %stack.31.place, bf16[896,512]{1,0:T(8,128)(2,1)S(1)} %get-tuple-element.19.turned_ref, bf16[128,2048]{1,0:T(8,128)(2,1)S(1)} %get-tuple-element.33.refs_0_, bf16[128,2048]{1,0:T(8,128)(2,1)S(1)} %collective-permute-done.5.refs_1_, ...), custom_call_target="tpu_custom_call" | custom-call | flops 939524096 | bytes 3407872 | tf_op jit(solution)/shard_map/weight_grad/pallas_call | solution.py:129
  135.4 12.9 %input_grads.1 = (bf16[512,896]{1,0:T(8,128)(2,1)}, bf16[512,896]{1,0:T(8,128)(2,1)}) custom-call(s32[6]{0:T(128)S(1)} %stack.31.place, bf16[896,4096]{1,0:T(8,128)(2,1)} %weight_ref.3, bf16[512,896]{1,0:T(8,128)(2,1)} %gate_ref.3, bf16[512,896]{1,0:T(8,128)(2,1)} %up_ref.3, bf16[128,2048]{1,0:T(8,128)(2,1)S(1)} %get-tuple-element.33.refs_0_, ...), custom_call_target="tpu_custom_call" | custom-call | flops 3758096384 | bytes 17301504 | tf_op jit(solution)/shard_map/input_grads/pallas_call | solution.py:186
  148.3 1.4 add_convert_fusion.5
  149.7 1.5 collective-permute-start.21
  151.2 0.5 collective-permute-start.23
  151.8 0.0 collective-permute-done.15
  151.8 1.4 add_convert_fusion.7
  153.2 0.6 collective-permute-start.16
  153.8 1.5 collective-permute-start.18
  155.3 0.0 collective-permute-done.2
  155.3 3.0 %add_convert_fusion = bf16[128,4096]{1,0:T(8,128)(2,1)} fusion(bf16[128,4096]{1,0:T(8,128)(2,1)} %collective-permute-done.4, bf16[128,4096]{1,0:T(8,128)(2,1)} %collective-permute-done.2, bf16[128,4096]{1,0:T(8,128)(2,1)S(1)} %get-tuple-element.13), kind=kLoop, calls=%fused_computation | loop fusion | flops 3145728 | bytes 4194304 | tf_op jit(solution)/shard_map/convert_element_type | solution.py:258
  158.3 4.9 %collective-permute-done.21 = bf16[2,448,256]{2,1,0:T(8,128)(2,1)S(1)} collective-permute-done((bf16[2,448,256]{2,1,0:T(8,128)(2,1)S(1)}, bf16[2,448,256]{2,1,0:T(8,128)(2,1)S(1)}, u32[]{:S(2)}, u32[]{:S(2)}) %collective-permute-start.21) | collective-permute-done | bytes 458784 | tf_op jit(solution)/shard_map/ppermute | solution.py:232
  163.2 1.5 collective-permute-done.23
  164.7 1.2 fusion.2
  165.9 0.6 collective-permute-start.22
  166.5 0.5 collective-permute-start.24
  167.1 6.0 %collective-permute-done.16 = bf16[2,448,256]{2,1,0:T(8,128)(2,1)S(1)} collective-permute-done((bf16[2,448,256]{2,1,0:T(8,128)(2,1)S(1)}, bf16[2,448,256]{2,1,0:T(8,128)(2,1)S(1)}, u32[]{:S(2)}, u32[]{:S(2)}) %collective-permute-start.16) | collective-permute-done | bytes 458784 | tf_op jit(solution)/shard_map/ppermute | solution.py:232
  173.0 1.5 collective-permute-done.18
  174.5 1.2 fusion
  175.8 0.6 collective-permute-start.17
  176.4 0.5 collective-permute-start.19
  176.9 2.5 %collective-permute-done.22 = bf16[448,256]{1,0:T(8,128)(2,1)S(1)} collective-permute-done((bf16[448,256]{1,0:T(8,128)(2,1)S(1)}, bf16[448,256]{1,0:T(8,128)(2,1)S(1)}, u32[]{:S(2)}, u32[]{:S(2)}) %collective-permute-start.22) | collective-permute-done | bytes 229408 | tf_op jit(solution)/shard_map/ppermute | solution.py:232
  179.5 1.3 bitcast_add_fusion.1
  180.7 2.1 %collective-permute-done.17 = bf16[448,256]{1,0:T(8,128)(2,1)S(1)} collective-permute-done((bf16[448,256]{1,0:T(8,128)(2,1)S(1)}, bf16[448,256]{1,0:T(8,128)(2,1)S(1)}, u32[]{:S(2)}, u32[]{:S(2)}) %collective-permute-start.17) | collective-permute-done | bytes 229408 | tf_op jit(solution)/shard_map/ppermute | solution.py:232
  182.8 1.3 bitcast_add_fusion.3
  184.1 1.5 maximum_maximum_fusion
  (21 shorter events, 0.1 us)
Async XLA Ops:
  0.7 1.2 copy-start.1
  1.9 1.2 copy-start.2
  4.5 10.1 %copy-start.3 = (bf16[128,4096]{1,0:T(8,128)(2,1)S(1)}, bf16[128,4096]{1,0:T(8,128)(2,1)}, u32[]{:S(2)}) copy-start(bf16[128,4096]{1,0:T(8,128)(2,1)} %param.7) | copy-start | bytes 3145732
  13.3 59.6 %collective-permute-start = (bf16[128,4096]{1,0:T(8,128)(2,1)S(1)}, bf16[128,4096]{1,0:T(8,128)(2,1)S(1)}, u32[]{:S(2)}, u32[]{:S(2)}) collective-permute-start(bf16[128,4096]{1,0:T(8,128)(2,1)S(1)} %get-tuple-element.15), channel_id=1, source_target_pairs={{0,1},{3,2},{4,5},{7,6},{8,9},{11,10},{12,13},{15,14},{16,17},{19,... | collective-permute-start | bytes 3145736 | tf_op jit(solution)/shard_map/ppermute | solution.py:227
  14.8 37.7 %collective-permute-start.5 = (bf16[128,2048]{1,0:T(8,128)(2,1)S(1)}, bf16[128,2048]{1,0:T(8,128)(2,1)S(1)}, u32[]{:S(2)}, u32[]{:S(2)}) collective-permute-start(bf16[128,2048]{1,0:T(8,128)(2,1)S(1)} %get-tuple-element.33.refs_0_), channel_id=1, source_target_pairs={{0,1},{1,0},{2,3},{3,2},{4,5},{5,4},{6,7},{7,6},{8,9},{9,8},{10,11... | collective-permute-start | bytes 1572872 | tf_op jit(solution)/shard_map/ppermute | solution.py:227
  17.5 45.0 %collective-permute-start.10 = (bf16[128,2048]{1,0:T(8,128)(2,1)S(1)}, bf16[128,2048]{1,0:T(8,128)(2,1)S(1)}, u32[]{:S(2)}, u32[]{:S(2)}) collective-permute-start(bf16[128,2048]{1,0:T(8,128)(2,1)S(1)} %get-tuple-element.32.refs_6_.refs_0_), channel_id=1, source_target_pairs={{0,1},{1,0},{2,3},{3,2},{4,5},{5,4},{6,7},{7,6},{8,9},{9,8},{10,11... | collective-permute-start | bytes 1572872 | tf_op jit(solution)/shard_map/ppermute | solution.py:227
  17.6 48.4 %collective-permute-start.6 = (bf16[128,2048]{1,0:T(8,128)(2,1)S(1)}, bf16[128,2048]{1,0:T(8,128)(2,1)S(1)}, u32[]{:S(2)}, u32[]{:S(2)}) collective-permute-start(bf16[128,2048]{1,0:T(8,128)(2,1)S(1)} %get-tuple-element.33.refs_0_), channel_id=1, source_target_pairs={{1,2},{2,1},{5,6},{6,5},{9,10},{10,9},{13,14},{14,13},{17,18},{18,... | collective-permute-start | bytes 1572872 | tf_op jit(solution)/shard_map/ppermute | solution.py:227
  21.1 46.3 %collective-permute-start.11 = (bf16[128,2048]{1,0:T(8,128)(2,1)S(1)}, bf16[128,2048]{1,0:T(8,128)(2,1)S(1)}, u32[]{:S(2)}, u32[]{:S(2)}) collective-permute-start(bf16[128,2048]{1,0:T(8,128)(2,1)S(1)} %get-tuple-element.32.refs_6_.refs_0_), channel_id=1, source_target_pairs={{1,2},{2,1},{5,6},{6,5},{9,10},{10,9},{13,14},{14,13},{17,18},{18,... | collective-permute-start | bytes 1572872 | tf_op jit(solution)/shard_map/ppermute | solution.py:227
  52.5 21.8 %collective-permute-start.8 = (bf16[128,2048]{1,0:T(8,128)(2,1)S(1)}, bf16[128,2048]{1,0:T(8,128)(2,1)S(1)}, u32[]{:S(2)}, u32[]{:S(2)}) collective-permute-start(bf16[128,2048]{1,0:T(8,128)(2,1)S(1)} %collective-permute-done.5.refs_1_), channel_id=1, source_target_pairs={{1,2},{2,1},{5,6},{6,5},{9,10},{10,9},{13,14},{14,13},{17,18},{18,... | collective-permute-start | bytes 1572872 | tf_op jit(solution)/shard_map/ppermute | solution.py:227
  62.6 14.7 %collective-permute-start.13 = (bf16[128,2048]{1,0:T(8,128)(2,1)S(1)}, bf16[128,2048]{1,0:T(8,128)(2,1)S(1)}, u32[]{:S(2)}, u32[]{:S(2)}) collective-permute-start(bf16[128,2048]{1,0:T(8,128)(2,1)S(1)} %collective-permute-done.10.refs_7_.refs_1_), channel_id=1, source_target_pairs={{1,2},{2,1},{5,6},{6,5},{9,10},{10,9},{13,14},{14,13},{17,18},{18,... | collective-permute-start | bytes 1572872 | tf_op jit(solution)/shard_map/ppermute | solution.py:227
  66.1 56.2 %collective-permute-start.3 = (bf16[128,4096]{1,0:T(8,128)(2,1)S(1)}, bf16[128,4096]{1,0:T(8,128)(2,1)}, u32[]{:S(2)}, u32[]{:S(2)}) collective-permute-start(bf16[128,4096]{1,0:T(8,128)(2,1)S(1)} %get-tuple-element.16), channel_id=1, source_target_pairs={{0,1},{3,2},{4,5},{7,6},{8,9},{11,10},{12,13},{15,14},{16,17},{19,... | collective-permute-start | bytes 3145736 | tf_op jit(solution)/shard_map/ppermute | solution.py:227
  67.4 51.7 %collective-permute-start.7 = (bf16[128,2048]{1,0:T(8,128)(2,1)S(1)}, bf16[128,2048]{1,0:T(8,128)(2,1)S(1)}, u32[]{:S(2)}, u32[]{:S(2)}) collective-permute-start(bf16[128,2048]{1,0:T(8,128)(2,1)S(1)} %collective-permute-done.6.refs_3_), channel_id=1, source_target_pairs={{1,0},{2,3},{5,4},{6,7},{9,8},{10,11},{13,12},{14,15},{17,16},{18,... | collective-permute-start | bytes 1572872 | tf_op jit(solution)/shard_map/ppermute | solution.py:227
  72.9 23.6 %collective-permute-start.12 = (bf16[128,2048]{1,0:T(8,128)(2,1)S(1)}, bf16[128,2048]{1,0:T(8,128)(2,1)S(1)}, u32[]{:S(2)}, u32[]{:S(2)}) collective-permute-start(bf16[128,2048]{1,0:T(8,128)(2,1)S(1)} %collective-permute-done.11.refs_9_.refs_3_), channel_id=1, source_target_pairs={{1,0},{2,3},{5,4},{6,7},{9,8},{10,11},{13,12},{14,15},{17,16},{18,... | collective-permute-start | bytes 1572872 | tf_op jit(solution)/shard_map/ppermute | solution.py:227
  74.3 44.8 %collective-permute-start.9 = (bf16[128,2048]{1,0:T(8,128)(2,1)S(1)}, bf16[128,2048]{1,0:T(8,128)(2,1)S(1)}, u32[]{:S(2)}, u32[]{:S(2)}) collective-permute-start(bf16[128,2048]{1,0:T(8,128)(2,1)S(1)} %collective-permute-done.8.refs_5_), channel_id=1, source_target_pairs={{1,0},{2,3},{5,4},{6,7},{9,8},{10,11},{13,12},{14,15},{17,16},{18,... | collective-permute-start | bytes 1572872 | tf_op jit(solution)/shard_map/ppermute | solution.py:227
  77.2 52.8 %copy-start = (bf16[128,2048]{1,0:T(8,128)(2,1)}, bf16[128,2048]{1,0:T(8,128)(2,1)S(1)}, u32[]{:S(2)}) copy-start(bf16[128,2048]{1,0:T(8,128)(2,1)S(1)} %collective-permute-done.13.refs_11_.refs_5_) | copy-start | bytes 1572868
  77.2 39.1 %collective-permute-start.14 = (bf16[128,2048]{1,0:T(8,128)(2,1)S(1)}, bf16[128,2048]{1,0:T(8,128)(2,1)S(1)}, u32[]{:S(2)}, u32[]{:S(2)}) collective-permute-start(bf16[128,2048]{1,0:T(8,128)(2,1)S(1)} %collective-permute-done.13.refs_11_.refs_5_), channel_id=1, source_target_pairs={{1,0},{2,3},{5,4},{6,7},{9,8},{10,11},{13,12},{14,15},{17,16},{18,... | collective-permute-start | bytes 1572872 | tf_op jit(solution)/shard_map/ppermute | solution.py:227
  96.5 30.6 %collective-permute-start.1 = (bf16[128,4096]{1,0:T(8,128)(2,1)}, bf16[128,4096]{1,0:T(8,128)(2,1)S(1)}, u32[]{:S(2)}, u32[]{:S(2)}) collective-permute-start(bf16[128,4096]{1,0:T(8,128)(2,1)} %add_convert_fusion.3), channel_id=1, source_target_pairs={{1,2},{2,1},{5,6},{6,5},{9,10},{10,9},{13,14},{14,13},{17,18},{18,... | collective-permute-start | bytes 3145736 | tf_op jit(solution)/shard_map/ppermute | solution.py:227
  119.0 29.3 %collective-permute-start.20 = (bf16[4,896,256]{2,1,0:T(8,128)(2,1)S(1)}, bf16[4,896,256]{2,1,0:T(8,128)(2,1)}, u32[]{:S(2)}, u32[]{:S(2)}) collective-permute-start(bf16[4,896,256]{2,1,0:T(8,128)(2,1)S(1)} %weight_grad.7), channel_id=1, source_target_pairs={{0,4},{4,0},{8,12},{12,8},{16,20},{20,16},{24,28},{28,24},{1,5},{5... | collective-permute-start | bytes 5505032 | tf_op jit(solution)/shard_map/ppermute | solution.py:232
  121.7 30.0 %collective-permute-start.15 = (bf16[4,896,256]{2,1,0:T(8,128)(2,1)S(1)}, bf16[4,896,256]{2,1,0:T(8,128)(2,1)}, u32[]{:S(2)}, u32[]{:S(2)}) collective-permute-start(bf16[4,896,256]{2,1,0:T(8,128)(2,1)S(1)} %weight_grad.5), channel_id=1, source_target_pairs={{0,4},{4,0},{8,12},{12,8},{16,20},{20,16},{24,28},{28,24},{1,5},{5... | collective-permute-start | bytes 5505032 | tf_op jit(solution)/shard_map/ppermute | solution.py:232
  124.7 29.0 %collective-permute-start.4 = (bf16[128,4096]{1,0:T(8,128)(2,1)}, bf16[128,4096]{1,0:T(8,128)(2,1)}, u32[]{:S(2)}, u32[]{:S(2)}) collective-permute-start(bf16[128,4096]{1,0:T(8,128)(2,1)} %add_convert_fusion.1), channel_id=1, source_target_pairs={{1,2},{2,1},{5,6},{6,5},{9,10},{10,9},{13,14},{14,13},{17,18},{18,... | collective-permute-start | bytes 3145736 | tf_op jit(solution)/shard_map/ppermute | solution.py:227
  128.3 27.0 %collective-permute-start.2 = (bf16[128,4096]{1,0:T(8,128)(2,1)}, bf16[128,4096]{1,0:T(8,128)(2,1)}, u32[]{:S(2)}, u32[]{:S(2)}) collective-permute-start(bf16[128,4096]{1,0:T(8,128)(2,1)} %add_convert_fusion.2), channel_id=1, source_target_pairs={{0,1},{1,0},{2,3},{3,2},{4,5},{5,4},{6,7},{7,6},{8,9},{9,8},{10,11... | collective-permute-start | bytes 3145736 | tf_op jit(solution)/shard_map/ppermute | solution.py:227
  149.7 13.5 %collective-permute-start.21 = (bf16[2,448,256]{2,1,0:T(8,128)(2,1)S(1)}, bf16[2,448,256]{2,1,0:T(8,128)(2,1)S(1)}, u32[]{:S(2)}, u32[]{:S(2)}) collective-permute-start(bf16[2,448,256]{2,1,0:T(8,128)(2,1)S(1)} %get-tuple-element.30), channel_id=1, source_target_pairs={{0,8},{4,12},{8,0},{12,4},{16,24},{20,28},{24,16},{28,20},{1,9},{5... | collective-permute-start | bytes 1376264 | tf_op jit(solution)/shard_map/ppermute | solution.py:232
  151.2 13.5 %collective-permute-start.23 = (bf16[2,448,256]{2,1,0:T(8,128)(2,1)S(1)}, bf16[2,448,256]{2,1,0:T(8,128)(2,1)S(1)}, u32[]{:S(2)}, u32[]{:S(2)}) collective-permute-start(bf16[2,448,256]{2,1,0:T(8,128)(2,1)S(1)} %get-tuple-element.31), channel_id=1, source_target_pairs={{0,16},{4,20},{8,24},{12,28},{16,0},{20,4},{24,8},{28,12},{1,17},{... | collective-permute-start | bytes 1376264 | tf_op jit(solution)/shard_map/ppermute | solution.py:232
  153.2 19.8 %collective-permute-start.16 = (bf16[2,448,256]{2,1,0:T(8,128)(2,1)S(1)}, bf16[2,448,256]{2,1,0:T(8,128)(2,1)S(1)}, u32[]{:S(2)}, u32[]{:S(2)}) collective-permute-start(bf16[2,448,256]{2,1,0:T(8,128)(2,1)S(1)} %get-tuple-element.24), channel_id=1, source_target_pairs={{0,8},{4,12},{8,0},{12,4},{16,24},{20,28},{24,16},{28,20},{1,9},{5... | collective-permute-start | bytes 1376264 | tf_op jit(solution)/shard_map/ppermute | solution.py:232
  153.8 20.7 %collective-permute-start.18 = (bf16[2,448,256]{2,1,0:T(8,128)(2,1)S(1)}, bf16[2,448,256]{2,1,0:T(8,128)(2,1)S(1)}, u32[]{:S(2)}, u32[]{:S(2)}) collective-permute-start(bf16[2,448,256]{2,1,0:T(8,128)(2,1)S(1)} %get-tuple-element.25), channel_id=1, source_target_pairs={{0,16},{4,20},{8,24},{12,28},{16,0},{20,4},{24,8},{28,12},{1,17},{... | collective-permute-start | bytes 1376264 | tf_op jit(solution)/shard_map/ppermute | solution.py:232
  165.9 13.5 %collective-permute-start.22 = (bf16[448,256]{1,0:T(8,128)(2,1)S(1)}, bf16[448,256]{1,0:T(8,128)(2,1)S(1)}, u32[]{:S(2)}, u32[]{:S(2)}) collective-permute-start(bf16[448,256]{1,0:T(8,128)(2,1)S(1)} %get-tuple-element.28), channel_id=1, source_target_pairs={{0,16},{4,20},{8,24},{12,28},{16,0},{20,4},{24,8},{28,12},{1,17},{... | collective-permute-start | bytes 688136 | tf_op jit(solution)/shard_map/ppermute | solution.py:232
  166.5 12.9 %collective-permute-start.24 = (bf16[448,256]{1,0:T(8,128)(2,1)S(1)}, bf16[448,256]{1,0:T(8,128)(2,1)S(1)}, u32[]{:S(2)}, u32[]{:S(2)}) collective-permute-start(bf16[448,256]{1,0:T(8,128)(2,1)S(1)} %get-tuple-element.29), channel_id=1, source_target_pairs={{0,8},{4,12},{8,0},{12,4},{16,24},{20,28},{24,16},{28,20},{1,9},{5... | collective-permute-start | bytes 688136 | tf_op jit(solution)/shard_map/ppermute | solution.py:232
  175.8 7.0 %collective-permute-start.17 = (bf16[448,256]{1,0:T(8,128)(2,1)S(1)}, bf16[448,256]{1,0:T(8,128)(2,1)S(1)}, u32[]{:S(2)}, u32[]{:S(2)}) collective-permute-start(bf16[448,256]{1,0:T(8,128)(2,1)S(1)} %get-tuple-element.22), channel_id=1, source_target_pairs={{0,16},{4,20},{8,24},{12,28},{16,0},{20,4},{24,8},{28,12},{1,17},{... | collective-permute-start | bytes 688136 | tf_op jit(solution)/shard_map/ppermute | solution.py:232
  176.4 6.4 %collective-permute-start.19 = (bf16[448,256]{1,0:T(8,128)(2,1)S(1)}, bf16[448,256]{1,0:T(8,128)(2,1)S(1)}, u32[]{:S(2)}, u32[]{:S(2)}) collective-permute-start(bf16[448,256]{1,0:T(8,128)(2,1)S(1)} %get-tuple-element.23), channel_id=1, source_target_pairs={{0,8},{4,12},{8,0},{12,4},{16,24},{20,28},{24,16},{28,20},{1,9},{5... | collective-permute-start | bytes 688136 | tf_op jit(solution)/shard_map/ppermute | solution.py:232

commit v2 on v0

v2 whole, which is shorter than its diff:
```python
import functools
import math

import jax
import jax.numpy as jnp
from jax import lax
from jax.experimental import pallas as pl
from jax.experimental.pallas import tpu as pltpu
from jax.sharding import PartitionSpec as P

F32, BF16 = jnp.float32, jnp.bfloat16

VMEM_BYTES = 28 * 1024 * 1024


def cost(us):
    return pl.CostEstimate(flops=int(1+us * 0.35e9), bytes_accessed=1, transcendentals=0)


def plain_body(gate_pre, up_pre, down_weight, grad_out):
    gate_val = gate_pre.astype(F32)
    up_val = up_pre.astype(F32)
    sigmoid_gate = jax.nn.sigmoid(gate_val)
    activated = gate_val * sigmoid_gate
    hidden = (activated * up_val).astype(BF16)
    grad_scale = 1.0 / math.sqrt(hidden.shape[0] * lax.axis_size("dp"))
    ffn_out = lax.psum_scatter(
        jnp.dot(hidden, down_weight, preferred_element_type=F32).astype(BF16),
        "tensor",
        scatter_dimension=0,
        tiled=True,
    )
    piece = lax.all_gather(grad_out, "tensor", axis=0, tiled=True)
    hidden_grad = jnp.einsum("td,fd->tf", piece, down_weight, preferred_element_type=F32)
    weight_grad = jnp.einsum("tf,td->fd", hidden, piece, preferred_element_type=F32)
    grad_down = lax.psum_scatter(
        (weight_grad * grad_scale).astype(BF16), "dp", scatter_dimension=1, tiled=True
    ).astype(F32)
    grad_gate = (
        hidden_grad * up_val * sigmoid_gate * (1.0 + gate_val * (1.0 - sigmoid_gate))
    ).astype(BF16)
    grad_up = (hidden_grad * activated).astype(BF16)
    return (ffn_out, grad_gate, grad_up, grad_down)


OUTER = [(0, 1), (1, 0), (2, 3), (3, 2)]
OUTWARD = [(1, 0), (2, 3)]
INWARD = [(0, 1), (3, 2)]
MIDDLE = [(1, 2), (2, 1)]


def forward_kernel(place, gate_ref, up_ref, weight_ref, turned_ref, *refs):
    out_refs, hidden_ref = refs[:4], refs[4]
    block = out_refs[0].shape[0]

    @pl.when(pl.program_id(0) == 0)
    def _():
        for i in range(4):
            rows = pl.ds(pl.multiple_of(place[i] * block, block), block)
            gate_val = gate_ref[rows].astype(F32)
            hidden = gate_val * jax.nn.sigmoid(gate_val) * up_ref[rows].astype(F32)
            hidden_ref[i * block : (i + 1) * block] = hidden.astype(BF16)
            turned_ref[:, i * block : (i + 1) * block] = hidden.T.astype(BF16)

    product = jnp.dot(hidden_ref[...], weight_ref[...], preferred_element_type=F32)
    for i, out_ref in enumerate(out_refs):
        out_ref[...] = product[i * block : (i + 1) * block].astype(BF16)


def forward_of(place, gate_pre, up_pre, weight, tile=1024):
    rows, width = gate_pre.shape
    model = weight.shape[1]
    block = rows // 4
    whole = pl.BlockSpec((rows, width), lambda j, place: (0, 0))
    return pl.pallas_call(
        forward_kernel,
        grid_spec=pltpu.PrefetchScalarGridSpec(
            num_scalar_prefetch=1,
            grid=(model // tile,),
            in_specs=[whole, whole, pl.BlockSpec((width, tile), lambda j, place: (0, j))],
            out_specs=[pl.BlockSpec((width, rows), lambda j, place: (0, 0))]
            + [pl.BlockSpec((block, tile), lambda j, place: (0, j))] * 4,
            scratch_shapes=[pltpu.VMEM((rows, width), BF16)],
        ),
        out_shape=[jax.ShapeDtypeStruct((width, rows), BF16)] + [jax.ShapeDtypeStruct((block, model), BF16)] * 4,
        cost_estimate=cost(9),
        compiler_params=pltpu.CompilerParams(vmem_limit_bytes=VMEM_BYTES),
        name="forward",
    )(place, gate_pre, up_pre, weight)


def split_kernel(tiles, in_ref, *out_refs):
    share = sum(tiles)
    for j in range(in_ref.shape[1] // share):
        start = j * share
        for out_ref, tile in zip(out_refs, tiles):
            out_ref[:, j * tile : (j + 1) * tile] = in_ref[:, start : start + tile]
            start += tile


def split(block, tiles):
    rows, columns = block.shape
    return pl.pallas_call(
        functools.partial(split_kernel, tiles),
        out_shape=[jax.ShapeDtypeStruct((rows, columns * t // sum(tiles)), BF16) for t in tiles],
        cost_estimate=cost(1),
        compiler_params=pltpu.CompilerParams(vmem_limit_bytes=VMEM_BYTES),
        name="split",
    )(block)


def weight_kernel(scale, place, turned_ref, own, outer, mid_e, mid_m, far_e, far_m, *out_refs):
    edge = place[4] == 1
    piece = jnp.concatenate(
        [own[...], outer[...], jnp.where(edge, mid_e[...], mid_m[...]), jnp.where(edge, far_e[...], far_m[...])],
        axis=0,
    )
    product = (jnp.dot(turned_ref[...], piece, preferred_element_type=F32) * scale).astype(BF16)
    for i, out_ref in enumerate(out_refs):

        @pl.when(pl.program_id(0) == i)
        def _():
            out_ref[...] = product


def weight_grad_of(place, turned, whole, far, c, scale, odd, n_dp):
    width, rows = turned.shape
    block, columns = far[0].shape
    tile = columns // n_dp
    n_parts = whole[0].shape[1] // columns

    def device(i, place):
        return jnp.bitwise_xor(place[5], 2 * i + odd)

    return pl.pallas_call(
        functools.partial(weight_kernel, scale),
        grid_spec=pltpu.PrefetchScalarGridSpec(
            num_scalar_prefetch=1,
            grid=(n_dp // 2,),
            in_specs=[pl.BlockSpec((width, rows), lambda i, place: (0, 0))]
            + [pl.BlockSpec((block, tile), lambda i, place: (0, n_parts * device(i, place) + c))] * 4
            + [pl.BlockSpec((block, tile), lambda i, place: (0, device(i, place)))] * 2,
            out_specs=[pl.BlockSpec((width, tile), lambda i, place: (0, 0))] * (n_dp // 2),
        ),
        out_shape=[jax.ShapeDtypeStruct((width, tile), BF16)] * (n_dp // 2),
        cost_estimate=cost(4),
        compiler_params=pltpu.CompilerParams(vmem_limit_bytes=VMEM_BYTES),
        name="weight_grad",
    )(place, turned, *whole, *far)


def input_kernel(n_dp, base, place, weight_ref, gate_ref, up_ref, *refs):
    step = pl.program_id(0)
    grad_gate_ref, grad_up_ref, total_ref = refs[-3:]
    edge = place[4] == 1
    if base == 0:
        pieces = [refs[0][...], refs[1][...]]
    else:
        far = [jnp.where(edge, refs[i][...], refs[i + 1][...]) for i in (2, 4)]
        pieces = [jnp.where(edge, refs[0][...], refs[1][...]), jnp.concatenate(far, axis=1)]
    part = lax.dot_general(
        weight_ref[...], jnp.concatenate(pieces, axis=0), (((1,), (1,)), ((), ())), preferred_element_type=F32
    )

    @pl.when(step == 0)
    def _():
        total_ref[...] = part

    @pl.when(step > 0)
    def _():
        total_ref[...] += part

    @pl.when(step == n_dp - 1)
    def _():
        block = refs[0].shape[0]
        for i in range(2):
            rows = pl.ds(pl.multiple_of(place[base + i] * block, block), block)
            hidden_grad = total_ref[:, i * block : (i + 1) * block].T
            gate_val = gate_ref[rows].astype(F32)
            up_val = up_ref[rows].astype(F32)
            s = jax.nn.sigmoid(gate_val)
            grad_gate_ref[rows] = (hidden_grad * up_val * s * (1.0 + gate_val * (1.0 - s))).astype(BF16)
            grad_up_ref[rows] = (hidden_grad * (gate_val * s)).astype(BF16)
            if base > 0:
                rows = pl.ds(pl.multiple_of(place[i] * block, block), block)
                grad_gate_ref[rows] = refs[6][rows]
                grad_up_ref[rows] = refs[7][rows]


def input_grads_of(place, weight, gate_pre, up_pre, blocks, n_dp, earlier=()):
    rows, width = gate_pre.shape
    model = weight.shape[1]
    base = 2 if earlier else 0
    whole = pl.BlockSpec((rows, width), lambda j, place: (0, 0))
    return pl.pallas_call(
        functools.partial(input_kernel, n_dp, base),
        grid_spec=pltpu.PrefetchScalarGridSpec(
            num_scalar_prefetch=1,
            grid=(n_dp,),
            in_specs=[pl.BlockSpec((width, model // n_dp), lambda j, place: (0, j)), whole, whole]
            + [pl.BlockSpec((rows // 4, b.shape[1] // n_dp), lambda j, place: (0, j)) for b in blocks]
            + [whole] * len(earlier),
            out_specs=[whole, whole],
            scratch_shapes=[pltpu.VMEM((width, rows // 2), F32)],
        ),
        out_shape=[jax.ShapeDtypeStruct((rows, width), BF16)] * 2,
        cost_estimate=cost(9),
        compiler_params=pltpu.CompilerParams(vmem_limit_bytes=VMEM_BYTES),
        name="input_grads",
    )(place, weight, gate_pre, up_pre, *blocks, *earlier)


def add(*terms):
    return functools.reduce(lambda a, b: a + b, [t.astype(F32) for t in terms])


def line_body(n_dp, n_tensor, gate_pre, up_pre, down_weight, grad_out):
    place_z = lax.axis_index("tensor")
    me = lax.axis_index("dp")
    outer = jnp.bitwise_xor(place_z, 1)
    edge = (place_z == 0) | (place_z == 3)
    other_mid = jnp.where(edge, 3 - outer, 3 - place_z)
    other_edge = jnp.where(edge, 3 - place_z, 3 - outer)
    place = jnp.stack([place_z, outer, other_mid, other_edge, edge.astype(jnp.int32), me]).astype(jnp.int32)
    rows, model = gate_pre.shape[0], grad_out.shape[1]
    scale = 1.0 / math.sqrt(rows * n_dp)

    def along(pairs):
        return lambda v: lax.ppermute(v, "tensor", pairs)

    both, outward, inward, middle = along(OUTER), along(OUTWARD), along(INWARD), along(MIDDLE)

    def flip(bit):
        return lambda v: lax.ppermute(v, "dp", [(i, i ^ bit) for i in range(n_dp)])

    flip_core, flip_x, flip_y = flip(1), flip(2), flip(4)

    def after(value, *done):
        return lax.optimization_barrier((value, *done))[0]

    def after(value, *done):
        return lax.optimization_barrier((value, *done))[0]

    share = model // n_dp
    half = share // 2
    p1, q1 = both(grad_out), middle(grad_out)
    turned, *partial = forward_of(place, gate_pre, up_pre, down_weight)
    p2 = outward(after(q1, partial[0]))
    p1a, p1b = split(p1, (half, half))
    q2a, q2b = middle(p1a), middle(p1b)
    r1 = inward(partial[3])
    s1 = add(partial[3], r1).astype(BF16)
    m1 = middle(s1)
    r2 = inward(after(partial[2], s1))
    early = input_grads_of(place, after(down_weight, q2a, s1), gate_pre, up_pre, [grad_out, p1], n_dp)
    p3a = outward(after(q2a, s1))
    p3b = outward(q2b)
    whole = [grad_out, p1, p2, q1]

    def weight_grad(c, far, *done):
        return weight_grad_of(place, after(turned, *done), whole, far, c, scale, 1, n_dp)

    def keep_of(c, far, *done):
        return weight_grad_of(place, after(turned, *done), whole, far, c, scale, 0, n_dp)

    top = gate_pre.shape[1] // 2

    def first(got, keep):
        x_out = jnp.stack([add(keep[i][:top], got[i][:top]).astype(BF16) for i in (1, 3)])
        y_out = jnp.stack([add(keep[i][top:], got[i][top:]).astype(BF16) for i in (2, 3)])
        return x_out, y_out

    def second(got, keep, x_in, y_in):
        x_then_y = add(keep[2][:top], got[2][:top], x_in[1]).astype(BF16)
        y_then_x = add(keep[1][top:], got[1][top:], y_in[1]).astype(BF16)
        return x_then_y, y_then_x

    def last(got, keep, x_in, y_in, x_then_y, y_then_x):
        return jnp.concatenate(
            [
                add(keep[0][:top], got[0][:top], x_in[0], x_then_y),
                add(keep[0][top:], got[0][top:], y_in[0], y_then_x),
            ],
            axis=0,
        )

    far_a, far_b = [p3a, after(q2a, q2b)], [p3b, q2b]
    send_a = weight_grad(0, far_a, early[0])
    got_a = [flip_core(v) for v in send_a]
    keep_a = keep_of(0, far_a, send_a[0])
    out_a = first(got_a, keep_a)
    in_a = flip_x(out_a[0]), flip_y(out_a[1])
    s2 = add(partial[2], after(r2, *out_a)).astype(BF16)
    m2 = middle(s2)
    send_b = weight_grad(1, [after(p3b, *out_a), q2b])
    got_b = [flip_core(v) for v in send_b]
    s3 = add(partial[1], after(m1, p3b)).astype(BF16)
    r3 = both(s3)
    on_a = second(got_a, keep_a, *after(in_a, send_b[0]))
    last_a = flip_y(on_a[0]), flip_x(on_a[1])
    keep_b = keep_of(1, far_b, *on_a)
    out_b = first(got_b, after(keep_b, s2, s3))
    in_b = flip_x(out_b[0]), flip_y(out_b[1])
    grad_gate, grad_up = input_grads_of(
        place, after(down_weight, *out_b), gate_pre, up_pre, [p2, q1, p3a, q2a, p3b, q2b], n_dp, earlier=early
    )
    on_b = second(got_b, keep_b, *after(in_b, grad_up))
    last_b = flip_y(on_b[0]), flip_x(on_b[1])
    ffn_out = add(partial[0], after(r3, *on_b), m2).astype(BF16)
    grad_down = jnp.concatenate(
        [last(got_a, keep_a, *in_a, *after(last_a, ffn_out)), last(got_b, keep_b, *in_b, *last_b)], axis=1
    )
    return (ffn_out, grad_gate, grad_up, grad_down)


def solution(mesh):
    n_dp, n_tensor = mesh.shape["dp"], mesh.shape["tensor"]
    on_line = n_dp == 8 and n_tensor == 4
    return jax.shard_map(
        functools.partial(line_body, n_dp, n_tensor) if on_line else plain_body,
        mesh=mesh,
        in_specs=(
            P("dp", "tensor"),
            P("dp", "tensor"),
            P("tensor", None),
            P(("dp", "tensor"), None),
        ),
        out_specs=(
            P(("dp", "tensor"), None),
            P("dp", "tensor"),
            P("dp", "tensor"),
            P("tensor", "dp"),
        ),
        check_vma=False,
    )
```

time: 255 us -> 133 us (0.52)
  waiting for transfers between devices: 204 us -> 49.8 us
  starting transfers between devices: 0.12 us -> 38.2 us
  Pallas kernels: 0 us -> 32.4 us
  matrix products: 31.5 us -> 0 us
  between operations: 13.7 us -> 1.05 us
  local copies, waits for them, and re-layouts: 1.38 us -> 5.57 us
    reduce_scatter x2 -> x0, waiting for transfers between devices: 122 us -> none  [the longest x1 77.2 us: body(): lax.psum_scatter(jnp.dot(hidden_rows, down_weight, preferred_element_type...]
    all_gather x1 -> x0, waiting for transfers between devices: 81.1 us -> none  [body(): piece = lax.all_gather(grad_out, 'tensor', axis=0, tiled=True)]
    ppermute x0 -> x28, waiting for transfers between devices: none -> 49.8 us  [the longest x12 35.2 us: along(): return lambda v: lax.ppermute(v, 'tensor', pairs)]
    ppermute x0 -> x28, starting transfers between devices: none -> 38.2 us  [the longest x12 26.7 us: along(): return lambda v: lax.ppermute(v, 'tensor', pairs)]
    pallas_call x0 -> x8, Pallas kernels: none -> 32.4 us  [the longest x2 13.6 us: input_grads_of(): pl.pallas_call(functools.partial(input_kernel, n_dp, base), grid_spec=plt...]
    dot_general x3 -> x0, matrix products: 31.5 us -> none  [the longest x1 12.4 us: body(): jnp.einsum('td,fd->tf', piece, down_weight, preferred_element_type=jnp.fl...]
    unnamed x4 -> x12, local copies, waits for them, and re-layouts: 1.38 us -> 5.48 us
  transfers between devices with their start and end apart: 3 -> 28, of which waited for: 3 -> 11; matrix products, arithmetic and copies ran while one was open for 10% -> 3% of each run, Pallas kernels for 0% -> 25%
where the time goes in v2:
time: 133 us; the launch traced here: 132 us
  waiting for transfers between devices  49.8 us (37%)
  starting transfers between devices  38.2 us (29%)
  Pallas kernels  32.4 us (24%)
  local copies, waits for them, and re-layouts  5.57 us (4%)
  other arithmetic  5.08 us (4%)
    ppermute x12, waiting for transfers between devices, along(): return lambda v: lax.ppermute(v, 'tensor', pairs)  35.2 us
    ppermute x12, starting transfers between devices, along(): return lambda v: lax.ppermute(v, 'tensor', pairs)  26.7 us
    ppermute x16, waiting for transfers between devices, flip(): return lambda v: lax.ppermute(v, 'dp', [(i, i ^ bit) for i in range(n_dp)])  14.7 us
    pallas_call x2, Pallas kernels, input_grads_of(): pl.pallas_call(functools.partial(input_kernel, n_dp, base), grid_spec=plt...  13.6 us
    pallas_call x4, Pallas kernels, weight_grad_of(): pl.pallas_call(functools.partial(weight_kernel, scale), grid_spec=pltpu.P...  11.8 us
    ppermute x16, starting transfers between devices, flip(): return lambda v: lax.ppermute(v, 'dp', [(i, i ^ bit) for i in range(n_dp)])  11.5 us
    pallas_call x1, Pallas kernels, forward_of(): pl.pallas_call(forward_kernel, grid_spec=pltpu.PrefetchScalarGridSpec(num...  6.94 us
    unnamed x12, local copies, waits for them, and re-layouts  5.48 us
  transfers between devices with their start and end apart: 28, of which 11 were waited for; matrix products, arithmetic and copies ran while one was open for 3% of the time, Pallas kernels for 25%

profile of v2, /device:TPU:12, one launch (start us, length us, event | category | flops | bytes accessed | tf_op | source)
XLA Modules:
  0.0 132.2 jit_solution(17229204823858641064)
XLA Ops:
  0.6 0.5 collective-permute-start.2
  1.1 4.6 %collective-permute-start.7 = (bf16[128,4096]{1,0:T(8,128)(2,1)}, bf16[128,4096]{1,0:T(8,128)(2,1)S(1)}, u32[]{:S(2)}, u32[]{:S(2)}) collective-permute-start(bf16[128,4096]{1,0:T(8,128)(2,1)} %own.7), channel_id=1, source_target_pairs={{1,2},{2,1},{5,6},{6,5},{9,10},{10,9},{13,14},{14,13},{17,18},{18,... | collective-permute-start | bytes 3145736 | tf_op jit(solution)/shard_map/ppermute | solution.py:229
  5.8 0.1 stack.67.place
  5.9 3.1 %copy-done.1 = bf16[896,4096]{1,0:T(8,128)(2,1)S(1)} copy-done((bf16[896,4096]{1,0:T(8,128)(2,1)S(1)}, bf16[896,4096]{1,0:T(8,128)(2,1)}, u32[]{:S(2)}) %copy-start.1) | copy-done | bytes 7340056
  9.0 1.2 copy-done.3
  10.1 1.2 copy-done.4
  11.3 6.9 %forward.1 = (bf16[896,512]{1,0:T(8,128)(2,1)S(1)}, bf16[128,4096]{1,0:T(8,128)(2,1)S(1)}, bf16[128,4096]{1,0:T(8,128)(2,1)S(1)}, bf16[128,4096]{1,0:T(8,128)(2,1)S(1)}, bf16[128,4096]{1,0:T(8,128)(2,1)S(1)}) custom-call(s32[6]{0:T(128)S(1)} %stack.67.place, bf16[512,896]{1,0:T(8,128)(2,1)S(1)} %copy-done.3, bf16[512,896]{1,0:T(8,128)(2,1)S(1)} %copy-done.4, ...), custom_call_target="tpu_custom_call" | custom-call | flops 3150000128 | bytes 1 | tf_op jit(solution)/shard_map/forward/pallas_call | solution.py:75
  18.3 1.4 %collective-permute-start = (bf16[128,4096]{1,0:T(8,128)(2,1)S(1)}, bf16[128,4096]{1,0:T(8,128)(2,1)S(1)}, u32[]{:S(2)}, u32[]{:S(2)}) collective-permute-start(bf16[128,4096]{1,0:T(8,128)(2,1)S(1)} %get-tuple-element.55), channel_id=1, source_target_pairs={{0,1},{3,2},{4,5},{7,6},{8,9},{11,10},{12,13},{15,14},{16,17},{19,... | collective-permute-start | bytes 3145736 | tf_op jit(solution)/shard_map/ppermute | solution.py:229
  19.7 7.2 %collective-permute-done.2.in_ref.refs_1_.outer = bf16[128,4096]{1,0:T(8,128)(2,1)S(1)} collective-permute-done((bf16[128,4096]{1,0:T(8,128)(2,1)}, bf16[128,4096]{1,0:T(8,128)(2,1)S(1)}, u32[]{:S(2)}, u32[]{:S(2)}) %collective-permute-start.2) | collective-permute-done | bytes 1048608 | tf_op jit(solution)/shard_map/ppermute | solution.py:229
  27.0 0.1 split.1
  27.0 3.5 %collective-permute-start.6 = (bf16[128,2048]{1,0:T(8,128)(2,1)S(1)}, bf16[128,2048]{1,0:T(8,128)(2,1)S(1)}, u32[]{:S(2)}, u32[]{:S(2)}) collective-permute-start(bf16[128,2048]{1,0:T(8,128)(2,1)S(1)} %get-tuple-element.59), channel_id=1, source_target_pairs={{1,2},{2,1},{5,6},{6,5},{9,10},{10,9},{13,14},{14,13},{17,18},{18,... | collective-permute-start | bytes 1572872 | tf_op jit(solution)/shard_map/ppermute | solution.py:229
  30.5 1.4 %collective-permute-start.8 = (bf16[128,4096]{1,0:T(8,128)(2,1)S(1)}, bf16[128,4096]{1,0:T(8,128)(2,1)S(1)}, u32[]{:S(2)}, u32[]{:S(2)}) collective-permute-start(bf16[128,4096]{1,0:T(8,128)(2,1)S(1)} %collective-permute-done.7.mid_m.refs_1_), channel_id=1, source_target_pairs={{1,0},{2,3},{5,4},{6,7},{9,8},{10,11},{13,12},{14,15},{17,16},{18,... | collective-permute-start | bytes 3145736 | tf_op jit(solution)/shard_map/ppermute | solution.py:229
  31.9 2.4 %collective-permute-start.3 = (bf16[128,2048]{1,0:T(8,128)(2,1)S(1)}, bf16[128,2048]{1,0:T(8,128)(2,1)S(1)}, u32[]{:S(2)}, u32[]{:S(2)}) collective-permute-start(bf16[128,2048]{1,0:T(8,128)(2,1)S(1)} %get-tuple-element.56), channel_id=1, source_target_pairs={{1,2},{2,1},{5,6},{6,5},{9,10},{10,9},{13,14},{14,13},{17,18},{18,... | collective-permute-start | bytes 1572872 | tf_op jit(solution)/shard_map/ppermute | solution.py:229
  34.3 14.0 %collective-permute-done = bf16[128,4096]{1,0:T(8,128)(2,1)S(1)} collective-permute-done((bf16[128,4096]{1,0:T(8,128)(2,1)S(1)}, bf16[128,4096]{1,0:T(8,128)(2,1)S(1)}, u32[]{:S(2)}, u32[]{:S(2)}) %collective-permute-start) | collective-permute-done | bytes 1048608 | tf_op jit(solution)/shard_map/ppermute | solution.py:229
  48.3 0.2 add_convert_fusion.3
  48.5 3.5 %collective-permute-start.1 = (bf16[128,4096]{1,0:T(8,128)(2,1)S(1)}, bf16[128,4096]{1,0:T(8,128)(2,1)S(1)}, u32[]{:S(2)}, u32[]{:S(2)}) collective-permute-start(bf16[128,4096]{1,0:T(8,128)(2,1)S(1)} %add_convert_fusion.3), channel_id=1, source_target_pairs={{1,2},{2,1},{5,6},{6,5},{9,10},{10,9},{13,14},{14,13},{17,18},{18,... | collective-permute-start | bytes 3145736 | tf_op jit(solution)/shard_map/ppermute | solution.py:229
  52.0 1.3 %collective-permute-start.9 = (bf16[128,2048]{1,0:T(8,128)(2,1)S(1)}, bf16[128,2048]{1,0:T(8,128)(2,1)S(1)}, u32[]{:S(2)}, u32[]{:S(2)}) collective-permute-start(bf16[128,2048]{1,0:T(8,128)(2,1)S(1)} %collective-permute-done.6.far_m.refs_3_), channel_id=1, source_target_pairs={{1,0},{2,3},{5,4},{6,7},{9,8},{10,11},{13,12},{14,15},{17,16},{18,... | collective-permute-start | bytes 1572872 | tf_op jit(solution)/shard_map/ppermute | solution.py:229
  53.4 1.3 %collective-permute-start.4 = (bf16[128,2048]{1,0:T(8,128)(2,1)S(1)}, bf16[128,2048]{1,0:T(8,128)(2,1)S(1)}, u32[]{:S(2)}, u32[]{:S(2)}) collective-permute-start(bf16[128,2048]{1,0:T(8,128)(2,1)S(1)} %collective-permute-done.3.far_m.refs_5_), channel_id=1, source_target_pairs={{1,0},{2,3},{5,4},{6,7},{9,8},{10,11},{13,12},{14,15},{17,16},{18,... | collective-permute-start | bytes 1572872 | tf_op jit(solution)/shard_map/ppermute | solution.py:229
  54.7 1.3 collective-permute-start.16
  56.0 5.9 %input_grads.2 = (bf16[512,896]{1,0:T(8,128)(2,1)S(1)}, bf16[512,896]{1,0:T(8,128)(2,1)S(1)}) custom-call(s32[6]{0:T(128)S(1)} %stack.67.place, bf16[896,4096]{1,0:T(8,128)(2,1)S(1)} %copy-done.2, bf16[512,896]{1,0:T(8,128)(2,1)S(1)} %copy-done.3, bf16[512,896]{1,0:T(8,128)(2,1)S(1)} %copy-done.5, bf16[128,4096]{1,0:T(8,128)(2,1)S(1)} %copy-done, ...), custom_call_target="tpu_custom_call" | custom-call | flops 3150000128 | bytes 1 | tf_op jit(solution)/shard_map/input_grads/pallas_call | solution.py:195
  62.0 3.7 %collective-permute-done.9.far_e.refs_2_ = bf16[128,2048]{1,0:T(8,128)(2,1)S(1)} collective-permute-done((bf16[128,2048]{1,0:T(8,128)(2,1)S(1)}, bf16[128,2048]{1,0:T(8,128)(2,1)S(1)}, u32[]{:S(2)}, u32[]{:S(2)}) %collective-permute-start.9) | collective-permute-done | bytes 524320 | tf_op jit(solution)/shard_map/ppermute | solution.py:229
  65.7 2.9 %weight_grad.4 = (bf16[896,256]{1,0:T(8,128)(2,1)S(1)}, bf16[896,256]{1,0:T(8,128)(2,1)S(1)}, bf16[896,256]{1,0:T(8,128)(2,1)S(1)}, bf16[896,256]{1,0:T(8,128)(2,1)S(1)}) custom-call(s32[6]{0:T(128)S(1)} %stack.67.place, bf16[896,512]{1,0:T(8,128)(2,1)S(1)} %get-tuple-element.78.turned_ref, bf16[128,4096]{1,0:T(8,128)(2,1)S(1)} %copy-done, ...), custom_call_target="tpu_custom_call" | custom-call | flops 1400000000 | bytes 1 | tf_op jit(solution)/shard_map/weight_grad/pallas_call | solution.py:135
  68.6 0.1 collective-permute-start.10
  68.7 0.5 collective-permute-start.12
  69.2 5.6 %collective-permute-done.4.far_e.refs_4_ = bf16[128,2048]{1,0:T(8,128)(2,1)S(1)} collective-permute-done((bf16[128,2048]{1,0:T(8,128)(2,1)S(1)}, bf16[128,2048]{1,0:T(8,128)(2,1)S(1)}, u32[]{:S(2)}, u32[]{:S(2)}) %collective-permute-start.4) | collective-permute-done | bytes 524320 | tf_op jit(solution)/shard_map/ppermute | solution.py:229
  74.9 0.2 add_convert_fusion.2
  75.1 2.5 %collective-permute-start.5 = (bf16[128,4096]{1,0:T(8,128)(2,1)S(1)}, bf16[128,4096]{1,0:T(8,128)(2,1)S(1)}, u32[]{:S(2)}, u32[]{:S(2)}) collective-permute-start(bf16[128,4096]{1,0:T(8,128)(2,1)S(1)} %add_convert_fusion.2), channel_id=1, source_target_pairs={{0,1},{1,0},{2,3},{3,2},{4,5},{5,4},{6,7},{7,6},{8,9},{9,8},{10,11... | collective-permute-start | bytes 3145736 | tf_op jit(solution)/shard_map/ppermute | solution.py:229
  77.7 2.9 %weight_grad.5 = (bf16[896,256]{1,0:T(8,128)(2,1)S(1)}, bf16[896,256]{1,0:T(8,128)(2,1)S(1)}, bf16[896,256]{1,0:T(8,128)(2,1)S(1)}, bf16[896,256]{1,0:T(8,128)(2,1)S(1)}) custom-call(s32[6]{0:T(128)S(1)} %stack.67.place, bf16[896,512]{1,0:T(8,128)(2,1)S(1)} %get-tuple-element.78.turned_ref, bf16[128,4096]{1,0:T(8,128)(2,1)S(1)} %copy-done, ...), custom_call_target="tpu_custom_call" | custom-call | flops 1400000000 | bytes 1 | tf_op jit(solution)/shard_map/weight_grad/pallas_call | solution.py:135
  80.6 0.1 fusion.10
  80.7 0.1 fusion.11
  80.9 0.6 collective-permute-start.14
  81.4 0.1 fusion.8
  81.6 1.6 %collective-permute-start.13 = (bf16[2,448,256]{2,1,0:T(8,128)(2,1)S(1)}, bf16[2,448,256]{2,1,0:T(8,128)(2,1)S(1)}, u32[]{:S(2)}, u32[]{:S(2)}) collective-permute-start(bf16[2,448,256]{2,1,0:T(8,128)(2,1)S(1)} %pad_maximum_fusion), channel_id=1, source_target_pairs={{0,8},{4,12},{8,0},{12,4},{16,24},{20,28},{24,16},{28,20},{1,9},{5... | collective-permute-start | bytes 1376264 | tf_op jit(solution)/shard_map/ppermute | solution.py:234
  83.1 0.2 add_convert_fusion.1
  83.4 2.9 %weight_grad.6 = (bf16[896,256]{1,0:T(8,128)(2,1)S(1)}, bf16[896,256]{1,0:T(8,128)(2,1)S(1)}, bf16[896,256]{1,0:T(8,128)(2,1)S(1)}, bf16[896,256]{1,0:T(8,128)(2,1)S(1)}) custom-call(s32[6]{0:T(128)S(1)} %stack.67.place, bf16[896,512]{1,0:T(8,128)(2,1)S(1)} %get-tuple-element.78.turned_ref, bf16[128,4096]{1,0:T(8,128)(2,1)S(1)} %copy-done, ...), custom_call_target="tpu_custom_call" | custom-call | flops 1400000000 | bytes 1 | tf_op jit(solution)/shard_map/weight_grad/pallas_call | solution.py:135
  86.3 0.1 collective-permute-start.15
  86.4 0.5 collective-permute-start.18
  86.9 6.7 %collective-permute-done.14 = bf16[2,448,256]{2,1,0:T(8,128)(2,1)S(1)} collective-permute-done((bf16[2,448,256]{2,1,0:T(8,128)(2,1)S(1)}, bf16[2,448,256]{2,1,0:T(8,128)(2,1)S(1)}, u32[]{:S(2)}, u32[]{:S(2)}) %collective-permute-start.14) | collective-permute-done | bytes 458784 | tf_op jit(solution)/shard_map/ppermute | solution.py:234
  93.6 0.4 collective-permute-done.13
  94.0 3.0 %collective-permute-start.21 = (bf16[128,4096]{1,0:T(8,128)(2,1)S(1)}, bf16[128,4096]{1,0:T(8,128)(2,1)S(1)}, u32[]{:S(2)}, u32[]{:S(2)}) collective-permute-start(bf16[128,4096]{1,0:T(8,128)(2,1)S(1)} %add_convert_fusion.1), channel_id=1, source_target_pairs={{1,2},{2,1},{5,6},{6,5},{9,10},{10,9},{13,14},{14,13},{17,18},{18,... | collective-permute-start | bytes 3145736 | tf_op jit(solution)/shard_map/ppermute | solution.py:229
  97.0 0.1 fusion.6
  97.1 0.1 fusion.7
  97.2 3.0 %weight_grad.7 = (bf16[896,256]{1,0:T(8,128)(2,1)S(1)}, bf16[896,256]{1,0:T(8,128)(2,1)S(1)}, bf16[896,256]{1,0:T(8,128)(2,1)S(1)}, bf16[896,256]{1,0:T(8,128)(2,1)S(1)}) custom-call(s32[6]{0:T(128)S(1)} %stack.67.place, bf16[896,512]{1,0:T(8,128)(2,1)S(1)} %get-tuple-element.78.turned_ref, bf16[128,4096]{1,0:T(8,128)(2,1)S(1)} %copy-done, ...), custom_call_target="tpu_custom_call" | custom-call | flops 1400000000 | bytes 1 | tf_op jit(solution)/shard_map/weight_grad/pallas_call | solution.py:135
  100.2 0.1 fusion.14
  100.3 0.1 fusion.15
  100.5 1.6 %collective-permute-start.20 = (bf16[2,448,256]{2,1,0:T(8,128)(2,1)S(1)}, bf16[2,448,256]{2,1,0:T(8,128)(2,1)S(1)}, u32[]{:S(2)}, u32[]{:S(2)}) collective-permute-start(bf16[2,448,256]{2,1,0:T(8,128)(2,1)S(1)} %pad_maximum_fusion.3), channel_id=1, source_target_pairs={{0,16},{4,20},{8,24},{12,28},{16,0},{20,4},{24,8},{28,12},{1,17},{... | collective-permute-start | bytes 1376264 | tf_op jit(solution)/shard_map/ppermute | solution.py:234
  102.0 0.1 fusion.12
  102.1 1.6 %collective-permute-start.19 = (bf16[2,448,256]{2,1,0:T(8,128)(2,1)S(1)}, bf16[2,448,256]{2,1,0:T(8,128)(2,1)S(1)}, u32[]{:S(2)}, u32[]{:S(2)}) collective-permute-start(bf16[2,448,256]{2,1,0:T(8,128)(2,1)S(1)} %pad_maximum_fusion.2), channel_id=1, source_target_pairs={{0,8},{4,12},{8,0},{12,4},{16,24},{20,28},{24,16},{28,20},{1,9},{5... | collective-permute-start | bytes 1376264 | tf_op jit(solution)/shard_map/ppermute | solution.py:234
  103.7 7.7 %input_grads.3 = (bf16[512,896]{1,0:T(8,128)(2,1)}, bf16[512,896]{1,0:T(8,128)(2,1)}) custom-call(s32[6]{0:T(128)S(1)} %stack.67.place, bf16[896,4096]{1,0:T(8,128)(2,1)S(1)} %copy-done.2, bf16[512,896]{1,0:T(8,128)(2,1)S(1)} %copy-done.3, bf16[512,896]{1,0:T(8,128)(2,1)S(1)} %copy-done.5, bf16[128,4096]{1,0:T(8,128)(2,1)S(1)} %collective-permute-done.8.mid_e.refs_0_, ...), custom_call_target="tpu_custom_call" | custom-call | flops 3150000128 | bytes 1 | tf_op jit(solution)/shard_map/input_grads/pallas_call | solution.py:195
  111.4 1.4 %collective-permute-done.20 = bf16[2,448,256]{2,1,0:T(8,128)(2,1)S(1)} collective-permute-done((bf16[2,448,256]{2,1,0:T(8,128)(2,1)S(1)}, bf16[2,448,256]{2,1,0:T(8,128)(2,1)S(1)}, u32[]{:S(2)}, u32[]{:S(2)}) %collective-permute-start.20) | collective-permute-done | bytes 458784 | tf_op jit(solution)/shard_map/ppermute | solution.py:234
  112.8 0.4 collective-permute-done.19
  113.2 1.5 %collective-permute-start.24 = (bf16[448,256]{1,0:T(8,128)(2,1)S(1)}, bf16[448,256]{1,0:T(8,128)(2,1)S(1)}, u32[]{:S(2)}, u32[]{:S(2)}) collective-permute-start(bf16[448,256]{1,0:T(8,128)(2,1)S(1)} %fusion.6), channel_id=1, source_target_pairs={{0,8},{4,12},{8,0},{12,4},{16,24},{20,28},{24,16},{28,20},{1,9},{5... | collective-permute-start | bytes 688136 | tf_op jit(solution)/shard_map/ppermute | solution.py:234
  114.7 0.1 fusion.4
  114.8 0.1 fusion.5
  114.9 1.6 %collective-permute-start.23 = (bf16[448,256]{1,0:T(8,128)(2,1)S(1)}, bf16[448,256]{1,0:T(8,128)(2,1)S(1)}, u32[]{:S(2)}, u32[]{:S(2)}) collective-permute-start(bf16[448,256]{1,0:T(8,128)(2,1)S(1)} %fusion.7), channel_id=1, source_target_pairs={{0,16},{4,20},{8,24},{12,28},{16,0},{20,4},{24,8},{28,12},{1,17},{... | collective-permute-start | bytes 688136 | tf_op jit(solution)/shard_map/ppermute | solution.py:234
  116.5 4.6 %collective-permute-done.21 = bf16[128,4096]{1,0:T(8,128)(2,1)S(1)} collective-permute-done((bf16[128,4096]{1,0:T(8,128)(2,1)S(1)}, bf16[128,4096]{1,0:T(8,128)(2,1)S(1)}, u32[]{:S(2)}, u32[]{:S(2)}) %collective-permute-start.21) | collective-permute-done | bytes 1048608 | tf_op jit(solution)/shard_map/ppermute | solution.py:229
  121.1 1.5 %collective-permute-start.27 = (bf16[448,256]{1,0:T(8,128)(2,1)S(1)}, bf16[448,256]{1,0:T(8,128)(2,1)S(1)}, u32[]{:S(2)}, u32[]{:S(2)}) collective-permute-start(bf16[448,256]{1,0:T(8,128)(2,1)S(1)} %fusion.4), channel_id=1, source_target_pairs={{0,8},{4,12},{8,0},{12,4},{16,24},{20,28},{24,16},{28,20},{1,9},{5... | collective-permute-start | bytes 688136 | tf_op jit(solution)/shard_map/ppermute | solution.py:234
  122.5 1.4 %add_convert_fusion = bf16[128,4096]{1,0:T(8,128)(2,1)} fusion(bf16[128,4096]{1,0:T(8,128)(2,1)S(1)} %collective-permute-done.21, bf16[128,4096]{1,0:T(8,128)(2,1)S(1)} %collective-permute-done.5, bf16[128,4096]{1,0:T(8,128)(2,1)S(1)} %get-tuple-element.53), kind=kLoop, calls=%fused_computation | loop fusion | flops 3145728 | bytes 4194304 | tf_op jit(solution)/shard_map/convert_element_type | solution.py:309
  124.0 0.5 collective-permute-start.26
  124.5 0.2 fusion.3
  124.7 3.1 %collective-permute-done.27 = bf16[448,256]{1,0:T(8,128)(2,1)S(1)} collective-permute-done((bf16[448,256]{1,0:T(8,128)(2,1)S(1)}, bf16[448,256]{1,0:T(8,128)(2,1)S(1)}, u32[]{:S(2)}, u32[]{:S(2)}) %collective-permute-start.27) | collective-permute-done | bytes 229408 | tf_op jit(solution)/shard_map/ppermute | solution.py:234
  127.8 2.7 %collective-permute-done.26 = bf16[448,256]{1,0:T(8,128)(2,1)S(1)} collective-permute-done((bf16[448,256]{1,0:T(8,128)(2,1)S(1)}, bf16[448,256]{1,0:T(8,128)(2,1)S(1)}, u32[]{:S(2)}, u32[]{:S(2)}) %collective-permute-start.26) | collective-permute-done | bytes 229408 | tf_op jit(solution)/shard_map/ppermute | solution.py:234
  130.5 0.2 fusion.1
  130.7 1.5 %maximum_maximum_fusion = f32[896,512]{1,0:T(8,128)} fusion(f32[448,256]{1,0:T(8,128)S(1)} %get-tuple-element.105, f32[448,256]{1,0:T(8,128)S(1)} %get-tuple-element.104, f32[448,256]{1,0:T(8,128)S(1)} %get-tuple-element.103, f32[448,256]{1,0:T(8,128)S(1)} %get-tuple-element.102), kind=kLoop, calls=%fused_computation.4 | loop fusion | flops 1376256 | bytes 3670016 | tf_op jit(solution)/shard_map/concatenate | solution.py:310
  (34 shorter events, 0.3 us)
Async XLA Ops:
  0.6 26.3 %collective-permute-start.2 = (bf16[128,4096]{1,0:T(8,128)(2,1)}, bf16[128,4096]{1,0:T(8,128)(2,1)S(1)}, u32[]{:S(2)}, u32[]{:S(2)}) collective-permute-start(bf16[128,4096]{1,0:T(8,128)(2,1)} %own.7), channel_id=1, source_target_pairs={{0,1},{1,0},{2,3},{3,2},{4,5},{5,4},{6,7},{7,6},{8,9},{9,8},{10,11... | collective-permute-start | bytes 3145736 | tf_op jit(solution)/shard_map/ppermute | solution.py:229
  1.1 29.4 %collective-permute-start.7 = (bf16[128,4096]{1,0:T(8,128)(2,1)}, bf16[128,4096]{1,0:T(8,128)(2,1)S(1)}, u32[]{:S(2)}, u32[]{:S(2)}) collective-permute-start(bf16[128,4096]{1,0:T(8,128)(2,1)} %own.7), channel_id=1, source_target_pairs={{1,2},{2,1},{5,6},{6,5},{9,10},{10,9},{13,14},{14,13},{17,18},{18,... | collective-permute-start | bytes 3145736 | tf_op jit(solution)/shard_map/ppermute | solution.py:229
  5.9 3.1 %copy-start.1 = (bf16[896,4096]{1,0:T(8,128)(2,1)S(1)}, bf16[896,4096]{1,0:T(8,128)(2,1)}, u32[]{:S(2)}) copy-start(bf16[896,4096]{1,0:T(8,128)(2,1)} %weight_ref.3) | copy-start | bytes 22020100
  9.0 1.2 copy-start.3
  10.1 1.2 copy-start.4
  11.3 44.7 %copy-start.2 = (bf16[896,4096]{1,0:T(8,128)(2,1)S(1)}, bf16[896,4096]{1,0:T(8,128)(2,1)}, u32[]{:S(2)}) copy-start(bf16[896,4096]{1,0:T(8,128)(2,1)} %weight_ref.3) | copy-start | bytes 22020100
  18.3 37.7 %copy-start = (bf16[128,4096]{1,0:T(8,128)(2,1)S(1)}, bf16[128,4096]{1,0:T(8,128)(2,1)}, u32[]{:S(2)}) copy-start(bf16[128,4096]{1,0:T(8,128)(2,1)} %own.7) | copy-start | bytes 3145732
  18.3 37.7 %copy-start.5 = (bf16[512,896]{1,0:T(8,128)(2,1)S(1)}, bf16[512,896]{1,0:T(8,128)(2,1)}, u32[]{:S(2)}) copy-start(bf16[512,896]{1,0:T(8,128)(2,1)} %up_ref.5) | copy-start | bytes 2752516
  18.3 30.0 %collective-permute-start = (bf16[128,4096]{1,0:T(8,128)(2,1)S(1)}, bf16[128,4096]{1,0:T(8,128)(2,1)S(1)}, u32[]{:S(2)}, u32[]{:S(2)}) collective-permute-start(bf16[128,4096]{1,0:T(8,128)(2,1)S(1)} %get-tuple-element.55), channel_id=1, source_target_pairs={{0,1},{3,2},{4,5},{7,6},{8,9},{11,10},{12,13},{15,14},{16,17},{19,... | collective-permute-start | bytes 3145736 | tf_op jit(solution)/shard_map/ppermute | solution.py:229
  27.0 25.0 %collective-permute-start.6 = (bf16[128,2048]{1,0:T(8,128)(2,1)S(1)}, bf16[128,2048]{1,0:T(8,128)(2,1)S(1)}, u32[]{:S(2)}, u32[]{:S(2)}) collective-permute-start(bf16[128,2048]{1,0:T(8,128)(2,1)S(1)} %get-tuple-element.59), channel_id=1, source_target_pairs={{1,2},{2,1},{5,6},{6,5},{9,10},{10,9},{13,14},{14,13},{17,18},{18,... | collective-permute-start | bytes 1572872 | tf_op jit(solution)/shard_map/ppermute | solution.py:229
  30.5 35.2 %collective-permute-start.8 = (bf16[128,4096]{1,0:T(8,128)(2,1)S(1)}, bf16[128,4096]{1,0:T(8,128)(2,1)S(1)}, u32[]{:S(2)}, u32[]{:S(2)}) collective-permute-start(bf16[128,4096]{1,0:T(8,128)(2,1)S(1)} %collective-permute-done.7.mid_m.refs_1_), channel_id=1, source_target_pairs={{1,0},{2,3},{5,4},{6,7},{9,8},{10,11},{13,12},{14,15},{17,16},{18,... | collective-permute-start | bytes 3145736 | tf_op jit(solution)/shard_map/ppermute | solution.py:229
  31.9 21.5 %collective-permute-start.3 = (bf16[128,2048]{1,0:T(8,128)(2,1)S(1)}, bf16[128,2048]{1,0:T(8,128)(2,1)S(1)}, u32[]{:S(2)}, u32[]{:S(2)}) collective-permute-start(bf16[128,2048]{1,0:T(8,128)(2,1)S(1)} %get-tuple-element.56), channel_id=1, source_target_pairs={{1,2},{2,1},{5,6},{6,5},{9,10},{10,9},{13,14},{14,13},{17,18},{18,... | collective-permute-start | bytes 1572872 | tf_op jit(solution)/shard_map/ppermute | solution.py:229
  48.5 26.3 %collective-permute-start.1 = (bf16[128,4096]{1,0:T(8,128)(2,1)S(1)}, bf16[128,4096]{1,0:T(8,128)(2,1)S(1)}, u32[]{:S(2)}, u32[]{:S(2)}) collective-permute-start(bf16[128,4096]{1,0:T(8,128)(2,1)S(1)} %add_convert_fusion.3), channel_id=1, source_target_pairs={{1,2},{2,1},{5,6},{6,5},{9,10},{10,9},{13,14},{14,13},{17,18},{18,... | collective-permute-start | bytes 3145736 | tf_op jit(solution)/shard_map/ppermute | solution.py:229
  52.0 13.7 %collective-permute-start.9 = (bf16[128,2048]{1,0:T(8,128)(2,1)S(1)}, bf16[128,2048]{1,0:T(8,128)(2,1)S(1)}, u32[]{:S(2)}, u32[]{:S(2)}) collective-permute-start(bf16[128,2048]{1,0:T(8,128)(2,1)S(1)} %collective-permute-done.6.far_m.refs_3_), channel_id=1, source_target_pairs={{1,0},{2,3},{5,4},{6,7},{9,8},{10,11},{13,12},{14,15},{17,16},{18,... | collective-permute-start | bytes 1572872 | tf_op jit(solution)/shard_map/ppermute | solution.py:229
  53.4 21.5 %collective-permute-start.4 = (bf16[128,2048]{1,0:T(8,128)(2,1)S(1)}, bf16[128,2048]{1,0:T(8,128)(2,1)S(1)}, u32[]{:S(2)}, u32[]{:S(2)}) collective-permute-start(bf16[128,2048]{1,0:T(8,128)(2,1)S(1)} %collective-permute-done.3.far_m.refs_5_), channel_id=1, source_target_pairs={{1,0},{2,3},{5,4},{6,7},{9,8},{10,11},{13,12},{14,15},{17,16},{18,... | collective-permute-start | bytes 1572872 | tf_op jit(solution)/shard_map/ppermute | solution.py:229
  54.7 28.4 %collective-permute-start.16 = (bf16[128,4096]{1,0:T(8,128)(2,1)S(1)}, bf16[128,4096]{1,0:T(8,128)(2,1)S(1)}, u32[]{:S(2)}, u32[]{:S(2)}) collective-permute-start(bf16[128,4096]{1,0:T(8,128)(2,1)S(1)} %get-tuple-element.85), channel_id=1, source_target_pairs={{0,1},{3,2},{4,5},{7,6},{8,9},{11,10},{12,13},{15,14},{16,17},{19,... | collective-permute-start | bytes 3145736 | tf_op jit(solution)/shard_map/ppermute | solution.py:229
  68.6 12.0 %collective-permute-start.10 = (bf16[896,256]{1,0:T(8,128)(2,1)S(1)}, bf16[896,256]{1,0:T(8,128)(2,1)S(1)}, u32[]{:S(2)}, u32[]{:S(2)}) collective-permute-start(bf16[896,256]{1,0:T(8,128)(2,1)S(1)} %get-tuple-element.69), channel_id=1, source_target_pairs={{0,4},{4,0},{8,12},{12,8},{16,20},{20,16},{24,28},{28,24},{1,5},{5... | collective-permute-start | bytes 1376264 | tf_op jit(solution)/shard_map/ppermute | solution.py:234
  68.7 12.0 %collective-permute-start.12 = (bf16[896,256]{1,0:T(8,128)(2,1)S(1)}, bf16[896,256]{1,0:T(8,128)(2,1)S(1)}, u32[]{:S(2)}, u32[]{:S(2)}) collective-permute-start(bf16[896,256]{1,0:T(8,128)(2,1)S(1)} %get-tuple-element.73), channel_id=1, source_target_pairs={{0,4},{4,0},{8,12},{12,8},{16,20},{20,16},{24,28},{28,24},{1,5},{5... | collective-permute-start | bytes 1376264 | tf_op jit(solution)/shard_map/ppermute | solution.py:234
  74.9 6.6 %collective-permute-start.11 = (bf16[896,256]{1,0:T(8,128)(2,1)S(1)}, bf16[896,256]{1,0:T(8,128)(2,1)S(1)}, u32[]{:S(2)}, u32[]{:S(2)}) collective-permute-start(bf16[896,256]{1,0:T(8,128)(2,1)S(1)} %get-tuple-element.71), channel_id=1, source_target_pairs={{0,4},{4,0},{8,12},{12,8},{16,20},{20,16},{24,28},{28,24},{1,5},{5... | collective-permute-start | bytes 1376264 | tf_op jit(solution)/shard_map/ppermute | solution.py:234
  75.1 39.7 %collective-permute-start.5 = (bf16[128,4096]{1,0:T(8,128)(2,1)S(1)}, bf16[128,4096]{1,0:T(8,128)(2,1)S(1)}, u32[]{:S(2)}, u32[]{:S(2)}) collective-permute-start(bf16[128,4096]{1,0:T(8,128)(2,1)S(1)} %add_convert_fusion.2), channel_id=1, source_target_pairs={{0,1},{1,0},{2,3},{3,2},{4,5},{5,4},{6,7},{7,6},{8,9},{9,8},{10,11... | collective-permute-start | bytes 3145736 | tf_op jit(solution)/shard_map/ppermute | solution.py:229
  80.9 12.7 %collective-permute-start.14 = (bf16[2,448,256]{2,1,0:T(8,128)(2,1)S(1)}, bf16[2,448,256]{2,1,0:T(8,128)(2,1)S(1)}, u32[]{:S(2)}, u32[]{:S(2)}) collective-permute-start(bf16[2,448,256]{2,1,0:T(8,128)(2,1)S(1)} %pad_maximum_fusion.1), channel_id=1, source_target_pairs={{0,16},{4,20},{8,24},{12,28},{16,0},{20,4},{24,8},{28,12},{1,17},{... | collective-permute-start | bytes 1376264 | tf_op jit(solution)/shard_map/ppermute | solution.py:234
  81.6 12.4 %collective-permute-start.13 = (bf16[2,448,256]{2,1,0:T(8,128)(2,1)S(1)}, bf16[2,448,256]{2,1,0:T(8,128)(2,1)S(1)}, u32[]{:S(2)}, u32[]{:S(2)}) collective-permute-start(bf16[2,448,256]{2,1,0:T(8,128)(2,1)S(1)} %pad_maximum_fusion), channel_id=1, source_target_pairs={{0,8},{4,12},{8,0},{12,4},{16,24},{20,28},{24,16},{28,20},{1,9},{5... | collective-permute-start | bytes 1376264 | tf_op jit(solution)/shard_map/ppermute | solution.py:234
  86.3 13.9 %collective-permute-start.15 = (bf16[896,256]{1,0:T(8,128)(2,1)S(1)}, bf16[896,256]{1,0:T(8,128)(2,1)S(1)}, u32[]{:S(2)}, u32[]{:S(2)}) collective-permute-start(bf16[896,256]{1,0:T(8,128)(2,1)S(1)} %get-tuple-element.80), channel_id=1, source_target_pairs={{0,4},{4,0},{8,12},{12,8},{16,20},{20,16},{24,28},{28,24},{1,5},{5... | collective-permute-start | bytes 1376264 | tf_op jit(solution)/shard_map/ppermute | solution.py:234
  86.4 13.9 %collective-permute-start.18 = (bf16[896,256]{1,0:T(8,128)(2,1)S(1)}, bf16[896,256]{1,0:T(8,128)(2,1)S(1)}, u32[]{:S(2)}, u32[]{:S(2)}) collective-permute-start(bf16[896,256]{1,0:T(8,128)(2,1)S(1)} %get-tuple-element.90), channel_id=1, source_target_pairs={{0,4},{4,0},{8,12},{12,8},{16,20},{20,16},{24,28},{28,24},{1,5},{5... | collective-permute-start | bytes 1376264 | tf_op jit(solution)/shard_map/ppermute | solution.py:234
  93.6 8.4 %collective-permute-start.17 = (bf16[896,256]{1,0:T(8,128)(2,1)S(1)}, bf16[896,256]{1,0:T(8,128)(2,1)S(1)}, u32[]{:S(2)}, u32[]{:S(2)}) collective-permute-start(bf16[896,256]{1,0:T(8,128)(2,1)S(1)} %get-tuple-element.88), channel_id=1, source_target_pairs={{0,4},{4,0},{8,12},{12,8},{16,20},{20,16},{24,28},{28,24},{1,5},{5... | collective-permute-start | bytes 1376264 | tf_op jit(solution)/shard_map/ppermute | solution.py:234
  94.0 27.1 %collective-permute-start.21 = (bf16[128,4096]{1,0:T(8,128)(2,1)S(1)}, bf16[128,4096]{1,0:T(8,128)(2,1)S(1)}, u32[]{:S(2)}, u32[]{:S(2)}) collective-permute-start(bf16[128,4096]{1,0:T(8,128)(2,1)S(1)} %add_convert_fusion.1), channel_id=1, source_target_pairs={{1,2},{2,1},{5,6},{6,5},{9,10},{10,9},{13,14},{14,13},{17,18},{18,... | collective-permute-start | bytes 3145736 | tf_op jit(solution)/shard_map/ppermute | solution.py:229
  100.5 12.3 %collective-permute-start.20 = (bf16[2,448,256]{2,1,0:T(8,128)(2,1)S(1)}, bf16[2,448,256]{2,1,0:T(8,128)(2,1)S(1)}, u32[]{:S(2)}, u32[]{:S(2)}) collective-permute-start(bf16[2,448,256]{2,1,0:T(8,128)(2,1)S(1)} %pad_maximum_fusion.3), channel_id=1, source_target_pairs={{0,16},{4,20},{8,24},{12,28},{16,0},{20,4},{24,8},{28,12},{1,17},{... | collective-permute-start | bytes 1376264 | tf_op jit(solution)/shard_map/ppermute | solution.py:234
  102.1 11.0 %collective-permute-start.19 = (bf16[2,448,256]{2,1,0:T(8,128)(2,1)S(1)}, bf16[2,448,256]{2,1,0:T(8,128)(2,1)S(1)}, u32[]{:S(2)}, u32[]{:S(2)}) collective-permute-start(bf16[2,448,256]{2,1,0:T(8,128)(2,1)S(1)} %pad_maximum_fusion.2), channel_id=1, source_target_pairs={{0,8},{4,12},{8,0},{12,4},{16,24},{20,28},{24,16},{28,20},{1,9},{5... | collective-permute-start | bytes 1376264 | tf_op jit(solution)/shard_map/ppermute | solution.py:234
  103.7 20.8 %collective-permute-start.22 = (bf16[896,256]{1,0:T(8,128)(2,1)S(1)}, bf16[896,256]{1,0:T(8,128)(2,1)S(1)}, u32[]{:S(2)}, u32[]{:S(2)}) collective-permute-start(bf16[896,256]{1,0:T(8,128)(2,1)S(1)} %get-tuple-element.66), channel_id=1, source_target_pairs={{0,4},{4,0},{8,12},{12,8},{16,20},{20,16},{24,28},{28,24},{1,5},{5... | collective-permute-start | bytes 1376264 | tf_op jit(solution)/shard_map/ppermute | solution.py:234
  112.8 12.0 %collective-permute-start.25 = (bf16[896,256]{1,0:T(8,128)(2,1)S(1)}, bf16[896,256]{1,0:T(8,128)(2,1)S(1)}, u32[]{:S(2)}, u32[]{:S(2)}) collective-permute-start(bf16[896,256]{1,0:T(8,128)(2,1)S(1)} %get-tuple-element.75), channel_id=1, source_target_pairs={{0,4},{4,0},{8,12},{12,8},{16,20},{20,16},{24,28},{28,24},{1,5},{5... | collective-permute-start | bytes 1376264 | tf_op jit(solution)/shard_map/ppermute | solution.py:234
  113.2 10.8 %collective-permute-start.24 = (bf16[448,256]{1,0:T(8,128)(2,1)S(1)}, bf16[448,256]{1,0:T(8,128)(2,1)S(1)}, u32[]{:S(2)}, u32[]{:S(2)}) collective-permute-start(bf16[448,256]{1,0:T(8,128)(2,1)S(1)} %fusion.6), channel_id=1, source_target_pairs={{0,8},{4,12},{8,0},{12,4},{16,24},{20,28},{24,16},{28,20},{1,9},{5... | collective-permute-start | bytes 688136 | tf_op jit(solution)/shard_map/ppermute | solution.py:234
  114.9 9.6 %collective-permute-start.23 = (bf16[448,256]{1,0:T(8,128)(2,1)S(1)}, bf16[448,256]{1,0:T(8,128)(2,1)S(1)}, u32[]{:S(2)}, u32[]{:S(2)}) collective-permute-start(bf16[448,256]{1,0:T(8,128)(2,1)S(1)} %fusion.7), channel_id=1, source_target_pairs={{0,16},{4,20},{8,24},{12,28},{16,0},{20,4},{24,8},{28,12},{1,17},{... | collective-permute-start | bytes 688136 | tf_op jit(solution)/shard_map/ppermute | solution.py:234
  121.1 6.8 %collective-permute-start.27 = (bf16[448,256]{1,0:T(8,128)(2,1)S(1)}, bf16[448,256]{1,0:T(8,128)(2,1)S(1)}, u32[]{:S(2)}, u32[]{:S(2)}) collective-permute-start(bf16[448,256]{1,0:T(8,128)(2,1)S(1)} %fusion.4), channel_id=1, source_target_pairs={{0,8},{4,12},{8,0},{12,4},{16,24},{20,28},{24,16},{28,20},{1,9},{5... | collective-permute-start | bytes 688136 | tf_op jit(solution)/shard_map/ppermute | solution.py:234
  124.0 6.5 %collective-permute-start.26 = (bf16[448,256]{1,0:T(8,128)(2,1)S(1)}, bf16[448,256]{1,0:T(8,128)(2,1)S(1)}, u32[]{:S(2)}, u32[]{:S(2)}) collective-permute-start(bf16[448,256]{1,0:T(8,128)(2,1)S(1)} %fusion.5), channel_id=1, source_target_pairs={{0,16},{4,20},{8,24},{12,28},{16,0},{20,4},{24,8},{28,12},{1,17},{... | collective-permute-start | bytes 688136 | tf_op jit(solution)/shard_map/ppermute | solution.py:234

commit v3 on v2

--- a/solution.py
+++ b/solution.py
@@ -14,7 +14,7 @@
 
 
 def cost(us):
-    return pl.CostEstimate(flops=int(1+us * 0.35e9), bytes_accessed=1, transcendentals=0)
+    return pl.CostEstimate(flops=int(us * 0.35e9), bytes_accessed=1, transcendentals=0)
 
 
 def plain_body(gate_pre, up_pre, down_weight, grad_out):
@@ -123,30 +123,33 @@
             out_ref[...] = product
 
 
-def weight_grad_of(place, turned, whole, far, c, scale, odd, n_dp):
+def weight_grad_of(place, turned, whole, far, c, scale, cores, n_dp):
     width, rows = turned.shape
     block, columns = far[0].shape
     tile = columns // n_dp
     n_parts = whole[0].shape[1] // columns
-
-    def device(i, place):
-        return jnp.bitwise_xor(place[5], 2 * i + odd)
-
-    return pl.pallas_call(
+    n_out = n_dp // 2
+
+    def device(j, place):
+        core = cores[0] if len(cores) == 1 else jnp.where(j < n_out, cores[0], cores[1])
+        return jnp.bitwise_xor(place[5], 2 * lax.rem(j, n_out) + core)
+
+    outs = pl.pallas_call(
         functools.partial(weight_kernel, scale),
         grid_spec=pltpu.PrefetchScalarGridSpec(
             num_scalar_prefetch=1,
-            grid=(n_dp // 2,),
-            in_specs=[pl.BlockSpec((width, rows), lambda i, place: (0, 0))]
-            + [pl.BlockSpec((block, tile), lambda i, place: (0, n_parts * device(i, place) + c))] * 4
-            + [pl.BlockSpec((block, tile), lambda i, place: (0, device(i, place)))] * 2,
-            out_specs=[pl.BlockSpec((width, tile), lambda i, place: (0, 0))] * (n_dp // 2),
-        ),
-        out_shape=[jax.ShapeDtypeStruct((width, tile), BF16)] * (n_dp // 2),
+            grid=(n_out * len(cores),),
+            in_specs=[pl.BlockSpec((width, rows), lambda j, place: (0, 0))]
+            + [pl.BlockSpec((block, tile), lambda j, place: (0, n_parts * device(j, place) + c))] * 4
+            + [pl.BlockSpec((block, tile), lambda j, place: (0, device(j, place)))] * 2,
+            out_specs=[pl.BlockSpec((width, tile), lambda j, place: (0, 0))] * (n_out * len(cores)),
+        ),
+        out_shape=[jax.ShapeDtypeStruct((width, tile), BF16)] * (n_out * len(cores)),
         cost_estimate=cost(4),
         compiler_params=pltpu.CompilerParams(vmem_limit_bytes=VMEM_BYTES),
         name="weight_grad",
     )(place, turned, *whole, *far)
+    return [outs[k * n_out : (k + 1) * n_out] for k in range(len(cores))]
 
 
 def input_kernel(n_dp, base, place, weight_ref, gate_ref, up_ref, *refs):
@@ -238,30 +241,21 @@
     def after(value, *done):
         return lax.optimization_barrier((value, *done))[0]
 
-    def after(value, *done):
-        return lax.optimization_barrier((value, *done))[0]
-
     share = model // n_dp
     half = share // 2
     p1, q1 = both(grad_out), middle(grad_out)
     turned, *partial = forward_of(place, gate_pre, up_pre, down_weight)
     p2 = outward(after(q1, partial[0]))
-    p1a, p1b = split(p1, (half, half))
-    q2a, q2b = middle(p1a), middle(p1b)
+    q2 = middle(after(p1, partial[0]))
     r1 = inward(partial[3])
     s1 = add(partial[3], r1).astype(BF16)
+    q2a, q2b = split(q2, (half, half))
     m1 = middle(s1)
     r2 = inward(after(partial[2], s1))
     early = input_grads_of(place, after(down_weight, q2a, s1), gate_pre, up_pre, [grad_out, p1], n_dp)
     p3a = outward(after(q2a, s1))
     p3b = outward(q2b)
     whole = [grad_out, p1, p2, q1]
-
-    def weight_grad(c, far, *done):
-        return weight_grad_of(place, after(turned, *done), whole, far, c, scale, 1, n_dp)
-
-    def keep_of(c, far, *done):
-        return weight_grad_of(place, after(turned, *done), whole, far, c, scale, 0, n_dp)
 
     top = gate_pre.shape[1] // 2
 
@@ -284,23 +278,26 @@
             axis=0,
         )
 
+    def flip_cores(send):
+        pairs = [flip_core(jnp.stack(send[i : i + 2])) for i in range(0, len(send), 2)]
+        return [pair[k] for pair in pairs for k in range(2)]
+
     far_a, far_b = [p3a, after(q2a, q2b)], [p3b, q2b]
-    send_a = weight_grad(0, far_a, early[0])
-    got_a = [flip_core(v) for v in send_a]
-    keep_a = keep_of(0, far_a, send_a[0])
+    send_a, keep_a = weight_grad_of(place, after(turned, early[0]), whole, far_a, 0, scale, (1, 0), n_dp)
+    got_a = flip_cores(send_a)
     out_a = first(got_a, keep_a)
     in_a = flip_x(out_a[0]), flip_y(out_a[1])
-    s2 = add(partial[2], after(r2, *out_a)).astype(BF16)
+    (send_b,) = weight_grad_of(place, turned, whole, [after(p3b, *out_a), q2b], 1, scale, (1,), n_dp)
+    got_b = flip_cores(send_b)
+    s2 = add(partial[2], after(r2, send_b[0])).astype(BF16)
     m2 = middle(s2)
-    send_b = weight_grad(1, [after(p3b, *out_a), q2b])
-    got_b = [flip_core(v) for v in send_b]
     s3 = add(partial[1], after(m1, p3b)).astype(BF16)
     r3 = both(s3)
-    on_a = second(got_a, keep_a, *after(in_a, send_b[0]))
-    last_a = flip_y(on_a[0]), flip_x(on_a[1])
-    keep_b = keep_of(1, far_b, *on_a)
+    (keep_b,) = weight_grad_of(place, after(turned, send_b[0]), whole, far_b, 1, scale, (0,), n_dp)
     out_b = first(got_b, after(keep_b, s2, s3))
     in_b = flip_x(out_b[0]), flip_y(out_b[1])
+    on_a = second(got_a, keep_a, *after(in_a, *out_b))
+    last_a = flip_y(on_a[0]), flip_x(on_a[1])
     grad_gate, grad_up = input_grads_of(
         place, after(down_weight, *out_b), gate_pre, up_pre, [p2, q1, p3a, q2a, p3b, q2b], n_dp, earlier=early
     )

time: 133 us -> 119 us (0.89)
  waiting for transfers between devices: 49.8 us -> 35.9 us
    ppermute x16 -> x12, waiting for transfers between devices: 14.7 us -> 2 us  [flip(): return lambda v: lax.ppermute(v, 'dp', [(i, i ^ bit) for i in range(n_dp)])]
    ppermute x16 -> x12, starting transfers between devices: 11.5 us -> 9.81 us  [flip(): return lambda v: lax.ppermute(v, 'dp', [(i, i ^ bit) for i in range(n_dp)])]
    ppermute x12 -> x11, waiting for transfers between devices: 35.2 us -> 33.9 us  [along(): return lambda v: lax.ppermute(v, 'tensor', pairs)]
    ppermute x12 -> x11, starting transfers between devices: 26.7 us -> 27.7 us  [along(): return lambda v: lax.ppermute(v, 'tensor', pairs)]
    pallas_call x4 -> x3, Pallas kernels: 11.8 us -> 11.5 us  [weight_grad_of(): pl.pallas_call(functools.partial(weight_kernel, scale), grid_spec=pltpu.P...]
    unnamed x12 -> x14, local copies, waits for them, and re-layouts: 5.48 us -> 5.48 us
  transfers between devices with their start and end apart: 28 -> 23, of which waited for: 11 -> 8; matrix products, arithmetic and copies ran while one was open for 3% -> 3% of each run, Pallas kernels for 25% -> 27%
where the time goes in v3:
time: 119 us; the launch traced here: 118 us
  starting transfers between devices  37.5 us (32%)
  waiting for transfers between devices  35.9 us (30%)
  Pallas kernels  32.2 us (27%)
  local copies, waits for them, and re-layouts  5.57 us (5%)
  other arithmetic  5.44 us (5%)
    ppermute x11, waiting for transfers between devices, along(): return lambda v: lax.ppermute(v, 'tensor', pairs)  33.9 us
    ppermute x11, starting transfers between devices, along(): return lambda v: lax.ppermute(v, 'tensor', pairs)  27.7 us
    pallas_call x2, Pallas kernels, input_grads_of(): pl.pallas_call(functools.partial(input_kernel, n_dp, base), grid_spec=plt...  13.6 us
    pallas_call x3, Pallas kernels, weight_grad_of(): pl.pallas_call(functools.partial(weight_kernel, scale), grid_spec=pltpu.P...  11.5 us
    ppermute x12, starting transfers between devices, flip(): return lambda v: lax.ppermute(v, 'dp', [(i, i ^ bit) for i in range(n_dp)])  9.81 us
    pallas_call x1, Pallas kernels, forward_of(): pl.pallas_call(forward_kernel, grid_spec=pltpu.PrefetchScalarGridSpec(num...  6.94 us
    unnamed x14, local copies, waits for them, and re-layouts  5.48 us
  transfers between devices with their start and end apart: 23, of which 8 were waited for; matrix products, arithmetic and copies ran while one was open for 3% of the time, Pallas kernels for 27%

profile of v3, /device:TPU:12, one launch (start us, length us, event | category | flops | bytes accessed | tf_op | source)
XLA Modules:
  0.0 117.7 jit_solution(239116990911397917)
XLA Ops:
  0.6 0.5 collective-permute-start.2
  1.1 4.6 %collective-permute-start.6 = (bf16[128,4096]{1,0:T(8,128)(2,1)}, bf16[128,4096]{1,0:T(8,128)(2,1)S(1)}, u32[]{:S(2)}, u32[]{:S(2)}) collective-permute-start(bf16[128,4096]{1,0:T(8,128)(2,1)} %own.5), channel_id=1, source_target_pairs={{1,2},{2,1},{5,6},{6,5},{9,10},{10,9},{13,14},{14,13},{17,18},{18,... | collective-permute-start | bytes 3145736 | tf_op jit(solution)/shard_map/ppermute | solution.py:232
  5.8 0.1 stack.103.place
  5.9 3.1 %copy-done.1 = bf16[896,4096]{1,0:T(8,128)(2,1)S(1)} copy-done((bf16[896,4096]{1,0:T(8,128)(2,1)S(1)}, bf16[896,4096]{1,0:T(8,128)(2,1)}, u32[]{:S(2)}) %copy-start.1) | copy-done | bytes 7340056
  9.0 1.2 %copy-done.3 = bf16[512,896]{1,0:T(8,128)(2,1)S(1)} copy-done((bf16[512,896]{1,0:T(8,128)(2,1)S(1)}, bf16[512,896]{1,0:T(8,128)(2,1)}, u32[]{:S(2)}) %copy-start.3) | copy-done | bytes 917528
  10.1 1.2 %copy-done.5 = bf16[512,896]{1,0:T(8,128)(2,1)S(1)} copy-done((bf16[512,896]{1,0:T(8,128)(2,1)S(1)}, bf16[512,896]{1,0:T(8,128)(2,1)}, u32[]{:S(2)}) %copy-start.5) | copy-done | bytes 917528
  11.3 6.9 %forward.1 = (bf16[896,512]{1,0:T(8,128)(2,1)S(1)}, bf16[128,4096]{1,0:T(8,128)(2,1)S(1)}, bf16[128,4096]{1,0:T(8,128)(2,1)S(1)}, bf16[128,4096]{1,0:T(8,128)(2,1)S(1)}, bf16[128,4096]{1,0:T(8,128)(2,1)S(1)}) custom-call(s32[6]{0:T(128)S(1)} %stack.103.place, bf16[512,896]{1,0:T(8,128)(2,1)S(1)} %copy-done.3, bf16[512,896]{1,0:T(8,128)(2,1)S(1)} %copy-done.5, ...), custom_call_target="tpu_custom_call" | custom-call | flops 3150000128 | bytes 1 | tf_op jit(solution)/shard_map/forward/pallas_call | solution.py:75
  18.3 1.3 %collective-permute-start = (bf16[128,4096]{1,0:T(8,128)(2,1)S(1)}, bf16[128,4096]{1,0:T(8,128)(2,1)S(1)}, u32[]{:S(2)}, u32[]{:S(2)}) collective-permute-start(bf16[128,4096]{1,0:T(8,128)(2,1)S(1)} %get-tuple-element.55), channel_id=1, source_target_pairs={{0,1},{3,2},{4,5},{7,6},{8,9},{11,10},{12,13},{15,14},{16,17},{19,... | collective-permute-start | bytes 3145736 | tf_op jit(solution)/shard_map/ppermute | solution.py:232
  19.6 7.4 %collective-permute-done.2.refs_1_.outer = bf16[128,4096]{1,0:T(8,128)(2,1)S(1)} collective-permute-done((bf16[128,4096]{1,0:T(8,128)(2,1)}, bf16[128,4096]{1,0:T(8,128)(2,1)S(1)}, u32[]{:S(2)}, u32[]{:S(2)}) %collective-permute-start.2) | collective-permute-done | bytes 1048608 | tf_op jit(solution)/shard_map/ppermute | solution.py:232
  27.0 3.7 %collective-permute-start.3 = (bf16[128,4096]{1,0:T(8,128)(2,1)S(1)}, bf16[128,4096]{1,0:T(8,128)(2,1)S(1)}, u32[]{:S(2)}, u32[]{:S(2)}) collective-permute-start(bf16[128,4096]{1,0:T(8,128)(2,1)S(1)} %collective-permute-done.2.refs_1_.outer), channel_id=1, source_target_pairs={{1,2},{2,1},{5,6},{6,5},{9,10},{10,9},{13,14},{14,13},{17,18},{18,... | collective-permute-start | bytes 3145736 | tf_op jit(solution)/shard_map/ppermute | solution.py:232
  30.7 0.0 collective-permute-done.6.mid_m.refs_1_
  30.7 1.4 %collective-permute-start.7 = (bf16[128,4096]{1,0:T(8,128)(2,1)S(1)}, bf16[128,4096]{1,0:T(8,128)(2,1)S(1)}, u32[]{:S(2)}, u32[]{:S(2)}) collective-permute-start(bf16[128,4096]{1,0:T(8,128)(2,1)S(1)} %collective-permute-done.6.mid_m.refs_1_), channel_id=1, source_target_pairs={{1,0},{2,3},{5,4},{6,7},{9,8},{10,11},{13,12},{14,15},{17,16},{18,... | collective-permute-start | bytes 3145736 | tf_op jit(solution)/shard_map/ppermute | solution.py:232
  32.1 16.2 %collective-permute-done = bf16[128,4096]{1,0:T(8,128)(2,1)S(1)} collective-permute-done((bf16[128,4096]{1,0:T(8,128)(2,1)S(1)}, bf16[128,4096]{1,0:T(8,128)(2,1)S(1)}, u32[]{:S(2)}, u32[]{:S(2)}) %collective-permute-start) | collective-permute-done | bytes 1048608 | tf_op jit(solution)/shard_map/ppermute | solution.py:232
  48.3 0.2 add_convert_fusion.3
  48.5 3.5 %collective-permute-start.1 = (bf16[128,4096]{1,0:T(8,128)(2,1)S(1)}, bf16[128,4096]{1,0:T(8,128)(2,1)S(1)}, u32[]{:S(2)}, u32[]{:S(2)}) collective-permute-start(bf16[128,4096]{1,0:T(8,128)(2,1)S(1)} %add_convert_fusion.3), channel_id=1, source_target_pairs={{1,2},{2,1},{5,6},{6,5},{9,10},{10,9},{13,14},{14,13},{17,18},{18,... | collective-permute-start | bytes 3145736 | tf_op jit(solution)/shard_map/ppermute | solution.py:232
  52.0 0.0 collective-permute-done.3.in_ref
  52.0 0.1 split.1
  52.2 1.3 %collective-permute-start.8 = (bf16[128,2048]{1,0:T(8,128)(2,1)S(1)}, bf16[128,2048]{1,0:T(8,128)(2,1)S(1)}, u32[]{:S(2)}, u32[]{:S(2)}) collective-permute-start(bf16[128,2048]{1,0:T(8,128)(2,1)S(1)} %get-tuple-element.65.far_m.refs_3_), channel_id=1, source_target_pairs={{1,0},{2,3},{5,4},{6,7},{9,8},{10,11},{13,12},{14,15},{17,16},{18,... | collective-permute-start | bytes 1572872 | tf_op jit(solution)/shard_map/ppermute | solution.py:232
  53.5 1.3 %collective-permute-start.12 = (bf16[128,4096]{1,0:T(8,128)(2,1)S(1)}, bf16[128,4096]{1,0:T(8,128)(2,1)S(1)}, u32[]{:S(2)}, u32[]{:S(2)}) collective-permute-start(bf16[128,4096]{1,0:T(8,128)(2,1)S(1)} %get-tuple-element.83), channel_id=1, source_target_pairs={{0,1},{3,2},{4,5},{7,6},{8,9},{11,10},{12,13},{15,14},{16,17},{19,... | collective-permute-start | bytes 3145736 | tf_op jit(solution)/shard_map/ppermute | solution.py:232
  54.8 4.6 %collective-permute-start.4 = (bf16[128,2048]{1,0:T(8,128)(2,1)S(1)}, bf16[128,2048]{1,0:T(8,128)(2,1)S(1)}, u32[]{:S(2)}, u32[]{:S(2)}) collective-permute-start(bf16[128,2048]{1,0:T(8,128)(2,1)S(1)} %get-tuple-element.57.far_m.refs_5_), channel_id=1, source_target_pairs={{1,0},{2,3},{5,4},{6,7},{9,8},{10,11},{13,12},{14,15},{17,16},{18,... | collective-permute-start | bytes 1572872 | tf_op jit(solution)/shard_map/ppermute | solution.py:232
  59.5 6.0 %input_grads.2 = (bf16[512,896]{1,0:T(8,128)(2,1)S(1)}, bf16[512,896]{1,0:T(8,128)(2,1)S(1)}) custom-call(s32[6]{0:T(128)S(1)} %stack.103.place, bf16[896,4096]{1,0:T(8,128)(2,1)S(1)} %copy-done.2, bf16[512,896]{1,0:T(8,128)(2,1)S(1)} %copy-done.4, bf16[512,896]{1,0:T(8,128)(2,1)S(1)} %copy-done.6, bf16[128,4096]{1,0:T(8,128)(2,1)S(1)} %copy-done, ...), custom_call_target="tpu_custom_call" | custom-call | flops 3150000128 | bytes 1 | tf_op jit(solution)/shard_map/input_grads/pallas_call | solution.py:198
  65.4 0.4 collective-permute-done.8.far_e.refs_2_
  65.8 5.6 %weight_grad.3 = (bf16[896,256]{1,0:T(8,128)(2,1)S(1)}, bf16[896,256]{1,0:T(8,128)(2,1)S(1)}, bf16[896,256]{1,0:T(8,128)(2,1)S(1)}, bf16[896,256]{1,0:T(8,128)(2...) custom-call(s32[6]{0:T(128)S(1)} %stack.103.place, ...), custom_call_target="tpu_custom_call" | custom-call | flops 1400000000 | bytes 1 | tf_op jit(solution)/shard_map/weight_grad/pallas_call | solution.py:137
  71.4 0.1 pad_maximum_fusion.1
  71.5 0.1 collective-permute-start.10
  71.6 0.1 pad_maximum_fusion
  71.7 0.6 collective-permute-start.9
  72.3 2.2 %collective-permute-done.1 = bf16[128,4096]{1,0:T(8,128)(2,1)S(1)} collective-permute-done((bf16[128,4096]{1,0:T(8,128)(2,1)S(1)}, bf16[128,4096]{1,0:T(8,128)(2,1)S(1)}, u32[]{:S(2)}, u32[]{:S(2)}) %collective-permute-start.1) | collective-permute-done | bytes 1048608 | tf_op jit(solution)/shard_map/ppermute | solution.py:232
  74.5 0.5 collective-permute-done.4.far_e.refs_4_
  75.0 0.2 add_convert_fusion.2
  75.2 2.5 %collective-permute-start.5 = (bf16[128,4096]{1,0:T(8,128)(2,1)S(1)}, bf16[128,4096]{1,0:T(8,128)(2,1)S(1)}, u32[]{:S(2)}, u32[]{:S(2)}) collective-permute-start(bf16[128,4096]{1,0:T(8,128)(2,1)S(1)} %add_convert_fusion.2), channel_id=1, source_target_pairs={{0,1},{1,0},{2,3},{3,2},{4,5},{5,4},{6,7},{7,6},{8,9},{9,8},{10,11... | collective-permute-start | bytes 3145736 | tf_op jit(solution)/shard_map/ppermute | solution.py:232
  77.8 0.0 collective-permute-done.10
  77.8 0.2 fusion.19
  78.0 0.6 collective-permute-start.18
  78.6 0.1 fusion.16
  78.7 1.6 %collective-permute-start.17 = (bf16[2,448,256]{2,1,0:T(8,128)(2,1)S(1)}, bf16[2,448,256]{2,1,0:T(8,128)(2,1)S(1)}, u32[]{:S(2)}, u32[]{:S(2)}) collective-permute-start(bf16[2,448,256]{2,1,0:T(8,128)(2,1)S(1)} %pad_maximum_fusion.4), channel_id=1, source_target_pairs={{0,8},{4,12},{8,0},{12,4},{16,24},{20,28},{24,16},{28,20},{1,9},{5... | collective-permute-start | bytes 1376264 | tf_op jit(solution)/shard_map/ppermute | solution.py:237
  80.3 3.0 %weight_grad.4 = (bf16[896,256]{1,0:T(8,128)(2,1)S(1)}, bf16[896,256]{1,0:T(8,128)(2,1)S(1)}, bf16[896,256]{1,0:T(8,128)(2,1)S(1)}, bf16[896,256]{1,0:T(8,128)(2,1)S(1)}) custom-call(s32[6]{0:T(128)S(1)} %stack.103.place, bf16[896,512]{1,0:T(8,128)(2,1)S(1)} %get-tuple-element.75.turned_ref, bf16[128,4096]{1,0:T(8,128)(2,1)S(1)} %copy-done, ...), custom_call_target="tpu_custom_call" | custom-call | flops 1400000000 | bytes 1 | tf_op jit(solution)/shard_map/weight_grad/pallas_call | solution.py:137
  83.2 0.1 pad_maximum_fusion.2
  83.3 0.1 collective-permute-start.11
  83.4 0.1 pad_maximum_fusion.3
  83.5 0.6 collective-permute-start.13
  84.1 0.2 add_convert_fusion.1
  84.3 2.9 %weight_grad.5 = (bf16[896,256]{1,0:T(8,128)(2,1)S(1)}, bf16[896,256]{1,0:T(8,128)(2,1)S(1)}, bf16[896,256]{1,0:T(8,128)(2,1)S(1)}, bf16[896,256]{1,0:T(8,128)(2,1)S(1)}) custom-call(s32[6]{0:T(128)S(1)} %stack.103.place, bf16[896,512]{1,0:T(8,128)(2,1)S(1)} %get-tuple-element.75.turned_ref, bf16[128,4096]{1,0:T(8,128)(2,1)S(1)} %copy-done, ...), custom_call_target="tpu_custom_call" | custom-call | flops 1400000000 | bytes 1 | tf_op jit(solution)/shard_map/weight_grad/pallas_call | solution.py:137
  87.3 2.9 %collective-permute-start.16 = (bf16[128,4096]{1,0:T(8,128)(2,1)S(1)}, bf16[128,4096]{1,0:T(8,128)(2,1)S(1)}, u32[]{:S(2)}, u32[]{:S(2)}) collective-permute-start(bf16[128,4096]{1,0:T(8,128)(2,1)S(1)} %add_convert_fusion.1), channel_id=1, source_target_pairs={{1,2},{2,1},{5,6},{6,5},{9,10},{10,9},{13,14},{14,13},{17,18},{18,... | collective-permute-start | bytes 3145736 | tf_op jit(solution)/shard_map/ppermute | solution.py:232
  90.2 0.2 fusion.23
  90.4 1.6 %collective-permute-start.15 = (bf16[2,448,256]{2,1,0:T(8,128)(2,1)S(1)}, bf16[2,448,256]{2,1,0:T(8,128)(2,1)S(1)}, u32[]{:S(2)}, u32[]{:S(2)}) collective-permute-start(bf16[2,448,256]{2,1,0:T(8,128)(2,1)S(1)} %pad_maximum_fusion.7), channel_id=1, source_target_pairs={{0,16},{4,20},{8,24},{12,28},{16,0},{20,4},{24,8},{28,12},{1,17},{... | collective-permute-start | bytes 1376264 | tf_op jit(solution)/shard_map/ppermute | solution.py:237
  92.0 0.1 fusion.20
  92.1 0.6 collective-permute-start.14
  92.7 0.1 fusion.3
  92.8 1.6 %collective-permute-start.20 = (bf16[448,256]{1,0:T(8,128)(2,1)S(1)}, bf16[448,256]{1,0:T(8,128)(2,1)S(1)}, u32[]{:S(2)}, u32[]{:S(2)}) collective-permute-start(bf16[448,256]{1,0:T(8,128)(2,1)S(1)} %fusion.3), channel_id=1, source_target_pairs={{0,8},{4,12},{8,0},{12,4},{16,24},{20,28},{24,16},{28,20},{1,9},{5... | collective-permute-start | bytes 688136 | tf_op jit(solution)/shard_map/ppermute | solution.py:237
  94.4 0.1 fusion.4
  94.5 7.7 %input_grads.3 = (bf16[512,896]{1,0:T(8,128)(2,1)}, bf16[512,896]{1,0:T(8,128)(2,1)}) custom-call(s32[6]{0:T(128)S(1)} %stack.103.place, bf16[896,4096]{1,0:T(8,128)(2,1)S(1)} %copy-done.2, bf16[512,896]{1,0:T(8,128)(2,1)S(1)} %copy-done.4, bf16[512,896]{1,0:T(8,128)(2,1)S(1)} %copy-done.6, bf16[128,4096]{1,0:T(8,128)(2,1)S(1)} %collective-permute-done.7.mid_e.refs_0_, ...), custom_call_target="tpu_custom_call" | custom-call | flops 3150000128 | bytes 1 | tf_op jit(solution)/shard_map/input_grads/pallas_call | solution.py:198
  102.2 0.5 collective-permute-done.15
  102.7 1.5 %collective-permute-start.19 = (bf16[448,256]{1,0:T(8,128)(2,1)S(1)}, bf16[448,256]{1,0:T(8,128)(2,1)S(1)}, u32[]{:S(2)}, u32[]{:S(2)}) collective-permute-start(bf16[448,256]{1,0:T(8,128)(2,1)S(1)} %fusion.4), channel_id=1, source_target_pairs={{0,16},{4,20},{8,24},{12,28},{16,0},{20,4},{24,8},{28,12},{1,17},{... | collective-permute-start | bytes 688136 | tf_op jit(solution)/shard_map/ppermute | solution.py:237
  104.2 1.5 %collective-permute-done.14 = bf16[2,448,256]{2,1,0:T(8,128)(2,1)S(1)} collective-permute-done((bf16[2,448,256]{2,1,0:T(8,128)(2,1)S(1)}, bf16[2,448,256]{2,1,0:T(8,128)(2,1)S(1)}, u32[]{:S(2)}, u32[]{:S(2)}) %collective-permute-start.14) | collective-permute-done | bytes 458784 | tf_op jit(solution)/shard_map/ppermute | solution.py:237
  105.7 0.1 fusion.6
  105.8 0.6 collective-permute-start.22
  106.4 0.1 fusion.7
  106.5 0.6 collective-permute-start.21
  107.0 7.2 %collective-permute-done.16 = bf16[128,4096]{1,0:T(8,128)(2,1)S(1)} collective-permute-done((bf16[128,4096]{1,0:T(8,128)(2,1)S(1)}, bf16[128,4096]{1,0:T(8,128)(2,1)S(1)}, u32[]{:S(2)}, u32[]{:S(2)}) %collective-permute-start.16) | collective-permute-done | bytes 1048608 | tf_op jit(solution)/shard_map/ppermute | solution.py:232
  114.2 1.4 %add_convert_fusion = bf16[128,4096]{1,0:T(8,128)(2,1)} fusion(bf16[128,4096]{1,0:T(8,128)(2,1)S(1)} %collective-permute-done.16, bf16[128,4096]{1,0:T(8,128)(2,1)S(1)} %collective-permute-done.5, bf16[128,4096]{1,0:T(8,128)(2,1)S(1)} %get-tuple-element.53), kind=kLoop, calls=%fused_computation | loop fusion | flops 3145728 | bytes 4194304 | tf_op jit(solution)/shard_map/convert_element_type | solution.py:306
  115.7 0.2 fusion.5
  115.9 0.2 fusion.1
  116.2 1.5 %maximum_maximum_fusion = f32[896,512]{1,0:T(8,128)} fusion(f32[448,256]{1,0:T(8,128)S(1)} %get-tuple-element.104, f32[448,256]{1,0:T(8,128)S(1)} %get-tuple-element.103, f32[448,256]{1,0:T(8,128)S(1)} %get-tuple-element.102, f32[448,256]{1,0:T(8,128)S(1)} %get-tuple-element.101), kind=kLoop, calls=%fused_computation.4 | loop fusion | flops 1376256 | bytes 3670016 | tf_op jit(solution)/shard_map/concatenate | solution.py:307
  (27 shorter events, 0.2 us)
Async XLA Ops:
  0.6 26.3 %collective-permute-start.2 = (bf16[128,4096]{1,0:T(8,128)(2,1)}, bf16[128,4096]{1,0:T(8,128)(2,1)S(1)}, u32[]{:S(2)}, u32[]{:S(2)}) collective-permute-start(bf16[128,4096]{1,0:T(8,128)(2,1)} %own.5), channel_id=1, source_target_pairs={{0,1},{1,0},{2,3},{3,2},{4,5},{5,4},{6,7},{7,6},{8,9},{9,8},{10,11... | collective-permute-start | bytes 3145736 | tf_op jit(solution)/shard_map/ppermute | solution.py:232
  1.1 29.6 %collective-permute-start.6 = (bf16[128,4096]{1,0:T(8,128)(2,1)}, bf16[128,4096]{1,0:T(8,128)(2,1)S(1)}, u32[]{:S(2)}, u32[]{:S(2)}) collective-permute-start(bf16[128,4096]{1,0:T(8,128)(2,1)} %own.5), channel_id=1, source_target_pairs={{1,2},{2,1},{5,6},{6,5},{9,10},{10,9},{13,14},{14,13},{17,18},{18,... | collective-permute-start | bytes 3145736 | tf_op jit(solution)/shard_map/ppermute | solution.py:232
  5.9 3.1 %copy-start.1 = (bf16[896,4096]{1,0:T(8,128)(2,1)S(1)}, bf16[896,4096]{1,0:T(8,128)(2,1)}, u32[]{:S(2)}) copy-start(bf16[896,4096]{1,0:T(8,128)(2,1)} %weight_ref.3) | copy-start | bytes 22020100
  9.0 1.2 %copy-start.3 = (bf16[512,896]{1,0:T(8,128)(2,1)S(1)}, bf16[512,896]{1,0:T(8,128)(2,1)}, u32[]{:S(2)}) copy-start(bf16[512,896]{1,0:T(8,128)(2,1)} %gate_ref.5) | copy-start | bytes 2752516
  10.1 1.2 %copy-start.5 = (bf16[512,896]{1,0:T(8,128)(2,1)S(1)}, bf16[512,896]{1,0:T(8,128)(2,1)}, u32[]{:S(2)}) copy-start(bf16[512,896]{1,0:T(8,128)(2,1)} %up_ref.5) | copy-start | bytes 2752516
  11.3 48.1 %copy-start.2 = (bf16[896,4096]{1,0:T(8,128)(2,1)S(1)}, bf16[896,4096]{1,0:T(8,128)(2,1)}, u32[]{:S(2)}) copy-start(bf16[896,4096]{1,0:T(8,128)(2,1)} %weight_ref.3) | copy-start | bytes 22020100
  18.3 30.0 %collective-permute-start = (bf16[128,4096]{1,0:T(8,128)(2,1)S(1)}, bf16[128,4096]{1,0:T(8,128)(2,1)S(1)}, u32[]{:S(2)}, u32[]{:S(2)}) collective-permute-start(bf16[128,4096]{1,0:T(8,128)(2,1)S(1)} %get-tuple-element.55), channel_id=1, source_target_pairs={{0,1},{3,2},{4,5},{7,6},{8,9},{11,10},{12,13},{15,14},{16,17},{19,... | collective-permute-start | bytes 3145736 | tf_op jit(solution)/shard_map/ppermute | solution.py:232
  27.0 32.5 %copy-start = (bf16[128,4096]{1,0:T(8,128)(2,1)S(1)}, bf16[128,4096]{1,0:T(8,128)(2,1)}, u32[]{:S(2)}) copy-start(bf16[128,4096]{1,0:T(8,128)(2,1)} %own.5) | copy-start | bytes 3145732
  27.0 32.5 %copy-start.4 = (bf16[512,896]{1,0:T(8,128)(2,1)S(1)}, bf16[512,896]{1,0:T(8,128)(2,1)}, u32[]{:S(2)}) copy-start(bf16[512,896]{1,0:T(8,128)(2,1)} %gate_ref.5) | copy-start | bytes 2752516
  27.0 32.5 %copy-start.6 = (bf16[512,896]{1,0:T(8,128)(2,1)S(1)}, bf16[512,896]{1,0:T(8,128)(2,1)}, u32[]{:S(2)}) copy-start(bf16[512,896]{1,0:T(8,128)(2,1)} %up_ref.5) | copy-start | bytes 2752516
  27.0 25.1 %collective-permute-start.3 = (bf16[128,4096]{1,0:T(8,128)(2,1)S(1)}, bf16[128,4096]{1,0:T(8,128)(2,1)S(1)}, u32[]{:S(2)}, u32[]{:S(2)}) collective-permute-start(bf16[128,4096]{1,0:T(8,128)(2,1)S(1)} %collective-permute-done.2.refs_1_.outer), channel_id=1, source_target_pairs={{1,2},{2,1},{5,6},{6,5},{9,10},{10,9},{13,14},{14,13},{17,18},{18,... | collective-permute-start | bytes 3145736 | tf_op jit(solution)/shard_map/ppermute | solution.py:232
  30.7 34.7 %collective-permute-start.7 = (bf16[128,4096]{1,0:T(8,128)(2,1)S(1)}, bf16[128,4096]{1,0:T(8,128)(2,1)S(1)}, u32[]{:S(2)}, u32[]{:S(2)}) collective-permute-start(bf16[128,4096]{1,0:T(8,128)(2,1)S(1)} %collective-permute-done.6.mid_m.refs_1_), channel_id=1, source_target_pairs={{1,0},{2,3},{5,4},{6,7},{9,8},{10,11},{13,12},{14,15},{17,16},{18,... | collective-permute-start | bytes 3145736 | tf_op jit(solution)/shard_map/ppermute | solution.py:232
  48.5 25.9 %collective-permute-start.1 = (bf16[128,4096]{1,0:T(8,128)(2,1)S(1)}, bf16[128,4096]{1,0:T(8,128)(2,1)S(1)}, u32[]{:S(2)}, u32[]{:S(2)}) collective-permute-start(bf16[128,4096]{1,0:T(8,128)(2,1)S(1)} %add_convert_fusion.3), channel_id=1, source_target_pairs={{1,2},{2,1},{5,6},{6,5},{9,10},{10,9},{13,14},{14,13},{17,18},{18,... | collective-permute-start | bytes 3145736 | tf_op jit(solution)/shard_map/ppermute | solution.py:232
  52.2 13.7 %collective-permute-start.8 = (bf16[128,2048]{1,0:T(8,128)(2,1)S(1)}, bf16[128,2048]{1,0:T(8,128)(2,1)S(1)}, u32[]{:S(2)}, u32[]{:S(2)}) collective-permute-start(bf16[128,2048]{1,0:T(8,128)(2,1)S(1)} %get-tuple-element.65.far_m.refs_3_), channel_id=1, source_target_pairs={{1,0},{2,3},{5,4},{6,7},{9,8},{10,11},{13,12},{14,15},{17,16},{18,... | collective-permute-start | bytes 1572872 | tf_op jit(solution)/shard_map/ppermute | solution.py:232
  53.5 29.7 %collective-permute-start.12 = (bf16[128,4096]{1,0:T(8,128)(2,1)S(1)}, bf16[128,4096]{1,0:T(8,128)(2,1)S(1)}, u32[]{:S(2)}, u32[]{:S(2)}) collective-permute-start(bf16[128,4096]{1,0:T(8,128)(2,1)S(1)} %get-tuple-element.83), channel_id=1, source_target_pairs={{0,1},{3,2},{4,5},{7,6},{8,9},{11,10},{12,13},{15,14},{16,17},{19,... | collective-permute-start | bytes 3145736 | tf_op jit(solution)/shard_map/ppermute | solution.py:232
  54.8 20.2 %collective-permute-start.4 = (bf16[128,2048]{1,0:T(8,128)(2,1)S(1)}, bf16[128,2048]{1,0:T(8,128)(2,1)S(1)}, u32[]{:S(2)}, u32[]{:S(2)}) collective-permute-start(bf16[128,2048]{1,0:T(8,128)(2,1)S(1)} %get-tuple-element.57.far_m.refs_5_), channel_id=1, source_target_pairs={{1,0},{2,3},{5,4},{6,7},{9,8},{10,11},{13,12},{14,15},{17,16},{18,... | collective-permute-start | bytes 1572872 | tf_op jit(solution)/shard_map/ppermute | solution.py:232
  71.5 6.3 %collective-permute-start.10 = (bf16[2,896,256]{2,1,0:T(8,128)(2,1)S(1)}, bf16[2,896,256]{2,1,0:T(8,128)(2,1)S(1)}, u32[]{:S(2)}, u32[]{:S(2)}) collective-permute-start(bf16[2,896,256]{2,1,0:T(8,128)(2,1)S(1)} %pad_maximum_fusion.1), channel_id=1, source_target_pairs={{0,4},{4,0},{8,12},{12,8},{16,20},{20,16},{24,28},{28,24},{1,5},{5... | collective-permute-start | bytes 2752520 | tf_op jit(solution)/shard_map/ppermute | solution.py:237
  71.7 6.9 %collective-permute-start.9 = (bf16[2,896,256]{2,1,0:T(8,128)(2,1)S(1)}, bf16[2,896,256]{2,1,0:T(8,128)(2,1)S(1)}, u32[]{:S(2)}, u32[]{:S(2)}) collective-permute-start(bf16[2,896,256]{2,1,0:T(8,128)(2,1)S(1)} %pad_maximum_fusion), channel_id=1, source_target_pairs={{0,4},{4,0},{8,12},{12,8},{16,20},{20,16},{24,28},{28,24},{1,5},{5... | collective-permute-start | bytes 2752520 | tf_op jit(solution)/shard_map/ppermute | solution.py:237
  75.2 31.2 %collective-permute-start.5 = (bf16[128,4096]{1,0:T(8,128)(2,1)S(1)}, bf16[128,4096]{1,0:T(8,128)(2,1)S(1)}, u32[]{:S(2)}, u32[]{:S(2)}) collective-permute-start(bf16[128,4096]{1,0:T(8,128)(2,1)S(1)} %add_convert_fusion.2), channel_id=1, source_target_pairs={{0,1},{1,0},{2,3},{3,2},{4,5},{5,4},{6,7},{7,6},{8,9},{9,8},{10,11... | collective-permute-start | bytes 3145736 | tf_op jit(solution)/shard_map/ppermute | solution.py:232
  78.0 14.1 %collective-permute-start.18 = (bf16[2,448,256]{2,1,0:T(8,128)(2,1)S(1)}, bf16[2,448,256]{2,1,0:T(8,128)(2,1)S(1)}, u32[]{:S(2)}, u32[]{:S(2)}) collective-permute-start(bf16[2,448,256]{2,1,0:T(8,128)(2,1)S(1)} %pad_maximum_fusion.5), channel_id=1, source_target_pairs={{0,16},{4,20},{8,24},{12,28},{16,0},{20,4},{24,8},{28,12},{1,17},{... | collective-permute-start | bytes 1376264 | tf_op jit(solution)/shard_map/ppermute | solution.py:237
  78.7 14.0 %collective-permute-start.17 = (bf16[2,448,256]{2,1,0:T(8,128)(2,1)S(1)}, bf16[2,448,256]{2,1,0:T(8,128)(2,1)S(1)}, u32[]{:S(2)}, u32[]{:S(2)}) collective-permute-start(bf16[2,448,256]{2,1,0:T(8,128)(2,1)S(1)} %pad_maximum_fusion.4), channel_id=1, source_target_pairs={{0,8},{4,12},{8,0},{12,4},{16,24},{20,28},{24,16},{28,20},{1,9},{5... | collective-permute-start | bytes 1376264 | tf_op jit(solution)/shard_map/ppermute | solution.py:237
  83.3 3.9 %collective-permute-start.11 = (bf16[2,896,256]{2,1,0:T(8,128)(2,1)S(1)}, bf16[2,896,256]{2,1,0:T(8,128)(2,1)S(1)}, u32[]{:S(2)}, u32[]{:S(2)}) collective-permute-start(bf16[2,896,256]{2,1,0:T(8,128)(2,1)S(1)} %pad_maximum_fusion.2), channel_id=1, source_target_pairs={{0,4},{4,0},{8,12},{12,8},{16,20},{20,16},{24,28},{28,24},{1,5},{5... | collective-permute-start | bytes 2752520 | tf_op jit(solution)/shard_map/ppermute | solution.py:237
  83.5 6.9 %collective-permute-start.13 = (bf16[2,896,256]{2,1,0:T(8,128)(2,1)S(1)}, bf16[2,896,256]{2,1,0:T(8,128)(2,1)S(1)}, u32[]{:S(2)}, u32[]{:S(2)}) collective-permute-start(bf16[2,896,256]{2,1,0:T(8,128)(2,1)S(1)} %pad_maximum_fusion.3), channel_id=1, source_target_pairs={{0,4},{4,0},{8,12},{12,8},{16,20},{20,16},{24,28},{28,24},{1,5},{5... | collective-permute-start | bytes 2752520 | tf_op jit(solution)/shard_map/ppermute | solution.py:237
  87.3 27.0 %collective-permute-start.16 = (bf16[128,4096]{1,0:T(8,128)(2,1)S(1)}, bf16[128,4096]{1,0:T(8,128)(2,1)S(1)}, u32[]{:S(2)}, u32[]{:S(2)}) collective-permute-start(bf16[128,4096]{1,0:T(8,128)(2,1)S(1)} %add_convert_fusion.1), channel_id=1, source_target_pairs={{1,2},{2,1},{5,6},{6,5},{9,10},{10,9},{13,14},{14,13},{17,18},{18,... | collective-permute-start | bytes 3145736 | tf_op jit(solution)/shard_map/ppermute | solution.py:232
  90.4 12.2 %collective-permute-start.15 = (bf16[2,448,256]{2,1,0:T(8,128)(2,1)S(1)}, bf16[2,448,256]{2,1,0:T(8,128)(2,1)S(1)}, u32[]{:S(2)}, u32[]{:S(2)}) collective-permute-start(bf16[2,448,256]{2,1,0:T(8,128)(2,1)S(1)} %pad_maximum_fusion.7), channel_id=1, source_target_pairs={{0,16},{4,20},{8,24},{12,28},{16,0},{20,4},{24,8},{28,12},{1,17},{... | collective-permute-start | bytes 1376264 | tf_op jit(solution)/shard_map/ppermute | solution.py:237
  92.1 13.5 %collective-permute-start.14 = (bf16[2,448,256]{2,1,0:T(8,128)(2,1)S(1)}, bf16[2,448,256]{2,1,0:T(8,128)(2,1)S(1)}, u32[]{:S(2)}, u32[]{:S(2)}) collective-permute-start(bf16[2,448,256]{2,1,0:T(8,128)(2,1)S(1)} %pad_maximum_fusion.6), channel_id=1, source_target_pairs={{0,8},{4,12},{8,0},{12,4},{16,24},{20,28},{24,16},{28,20},{1,9},{5... | collective-permute-start | bytes 1376264 | tf_op jit(solution)/shard_map/ppermute | solution.py:237
  92.8 22.9 %collective-permute-start.20 = (bf16[448,256]{1,0:T(8,128)(2,1)S(1)}, bf16[448,256]{1,0:T(8,128)(2,1)S(1)}, u32[]{:S(2)}, u32[]{:S(2)}) collective-permute-start(bf16[448,256]{1,0:T(8,128)(2,1)S(1)} %fusion.3), channel_id=1, source_target_pairs={{0,8},{4,12},{8,0},{12,4},{16,24},{20,28},{24,16},{28,20},{1,9},{5... | collective-permute-start | bytes 688136 | tf_op jit(solution)/shard_map/ppermute | solution.py:237
  102.7 13.0 %collective-permute-start.19 = (bf16[448,256]{1,0:T(8,128)(2,1)S(1)}, bf16[448,256]{1,0:T(8,128)(2,1)S(1)}, u32[]{:S(2)}, u32[]{:S(2)}) collective-permute-start(bf16[448,256]{1,0:T(8,128)(2,1)S(1)} %fusion.4), channel_id=1, source_target_pairs={{0,16},{4,20},{8,24},{12,28},{16,0},{20,4},{24,8},{28,12},{1,17},{... | collective-permute-start | bytes 688136 | tf_op jit(solution)/shard_map/ppermute | solution.py:237
  105.8 10.2 %collective-permute-start.22 = (bf16[448,256]{1,0:T(8,128)(2,1)S(1)}, bf16[448,256]{1,0:T(8,128)(2,1)S(1)}, u32[]{:S(2)}, u32[]{:S(2)}) collective-permute-start(bf16[448,256]{1,0:T(8,128)(2,1)S(1)} %fusion.6), channel_id=1, source_target_pairs={{0,8},{4,12},{8,0},{12,4},{16,24},{20,28},{24,16},{28,20},{1,9},{5... | collective-permute-start | bytes 688136 | tf_op jit(solution)/shard_map/ppermute | solution.py:237
  106.5 9.5 %collective-permute-start.21 = (bf16[448,256]{1,0:T(8,128)(2,1)S(1)}, bf16[448,256]{1,0:T(8,128)(2,1)S(1)}, u32[]{:S(2)}, u32[]{:S(2)}) collective-permute-start(bf16[448,256]{1,0:T(8,128)(2,1)S(1)} %fusion.7), channel_id=1, source_target_pairs={{0,16},{4,20},{8,24},{12,28},{16,0},{20,4},{24,8},{28,12},{1,17},{... | collective-permute-start | bytes 688136 | tf_op jit(solution)/shard_map/ppermute | solution.py:237

commit v4 on v3

--- a/solution.py
+++ b/solution.py
@@ -291,7 +291,7 @@
     got_b = flip_cores(send_b)
     s2 = add(partial[2], after(r2, send_b[0])).astype(BF16)
     m2 = middle(s2)
-    s3 = add(partial[1], after(m1, p3b)).astype(BF16)
+    s3 = add(partial[1], m1).astype(BF16)
     r3 = both(s3)
     (keep_b,) = weight_grad_of(place, after(turned, send_b[0]), whole, far_b, 1, scale, (0,), n_dp)
     out_b = first(got_b, after(keep_b, s2, s3))

time: 119 us -> 116 us (0.975); the launches traced: 118 us -> 116 us
  starting transfers between devices: 37.5 us -> 35.5 us
    ppermute x11, starting transfers between devices: 27.7 us -> 25 us  [along(): return lambda v: lax.ppermute(v, 'tensor', pairs)]
  transfers between devices with their start and end apart: 23 -> 23, of which waited for: 8 -> 7; matrix products, arithmetic and copies ran while one was open for 3% -> 3% of each run, Pallas kernels for 27% -> 28%
where the time goes in v4:
time: 116 us
  waiting for transfers between devices  36.1 us (31%)
  starting transfers between devices  35.5 us (31%)
  Pallas kernels  32.2 us (28%)
  local copies, waits for them, and re-layouts  5.57 us (5%)
  other arithmetic  5.42 us (5%)
    ppermute x11, waiting for transfers between devices, along(): return lambda v: lax.ppermute(v, 'tensor', pairs)  33.9 us
    ppermute x11, starting transfers between devices, along(): return lambda v: lax.ppermute(v, 'tensor', pairs)  25 us
    pallas_call x2, Pallas kernels, input_grads_of(): pl.pallas_call(functools.partial(input_kernel, n_dp, base), grid_spec=plt...  13.6 us
    pallas_call x3, Pallas kernels, weight_grad_of(): pl.pallas_call(functools.partial(weight_kernel, scale), grid_spec=pltpu.P...  11.5 us
    ppermute x12, starting transfers between devices, flip(): return lambda v: lax.ppermute(v, 'dp', [(i, i ^ bit) for i in range(n_dp)])  10.5 us
    pallas_call x1, Pallas kernels, forward_of(): pl.pallas_call(forward_kernel, grid_spec=pltpu.PrefetchScalarGridSpec(num...  6.94 us
    unnamed x14, local copies, waits for them, and re-layouts  5.48 us
  transfers between devices with their start and end apart: 23, of which 7 were waited for; matrix products, arithmetic and copies ran while one was open for 3% of the time, Pallas kernels for 28%

profile of v4, /device:TPU:12, one launch (start us, length us, event | category | flops | bytes accessed | tf_op | source)
XLA Modules:
  0.0 115.9 jit_solution(14863509975251878067)
XLA Ops:
  0.6 0.5 collective-permute-start.3
  1.1 4.6 %collective-permute-start.4 = (bf16[128,4096]{1,0:T(8,128)(2,1)}, bf16[128,4096]{1,0:T(8,128)(2,1)S(1)}, u32[]{:S(2)}, u32[]{:S(2)}) collective-permute-start(bf16[128,4096]{1,0:T(8,128)(2,1)} %own.5), channel_id=1, source_target_pairs={{1,2},{2,1},{5,6},{6,5},{9,10},{10,9},{13,14},{14,13},{17,18},{18,... | collective-permute-start | bytes 3145736 | tf_op jit(solution)/shard_map/ppermute | solution.py:232
  5.8 0.1 stack.103.place
  5.9 3.1 %copy-done.1 = bf16[896,4096]{1,0:T(8,128)(2,1)S(1)} copy-done((bf16[896,4096]{1,0:T(8,128)(2,1)S(1)}, bf16[896,4096]{1,0:T(8,128)(2,1)}, u32[]{:S(2)}) %copy-start.1) | copy-done | bytes 7340056
  9.0 1.2 %copy-done.3 = bf16[512,896]{1,0:T(8,128)(2,1)S(1)} copy-done((bf16[512,896]{1,0:T(8,128)(2,1)S(1)}, bf16[512,896]{1,0:T(8,128)(2,1)}, u32[]{:S(2)}) %copy-start.3) | copy-done | bytes 917528
  10.1 1.2 %copy-done.5 = bf16[512,896]{1,0:T(8,128)(2,1)S(1)} copy-done((bf16[512,896]{1,0:T(8,128)(2,1)S(1)}, bf16[512,896]{1,0:T(8,128)(2,1)}, u32[]{:S(2)}) %copy-start.5) | copy-done | bytes 917528
  11.3 6.9 %forward.1 = (bf16[896,512]{1,0:T(8,128)(2,1)S(1)}, bf16[128,4096]{1,0:T(8,128)(2,1)S(1)}, bf16[128,4096]{1,0:T(8,128)(2,1)S(1)}, bf16[128,4096]{1,0:T(8,128)(2,1)S(1)}, bf16[128,4096]{1,0:T(8,128)(2,1)S(1)}) custom-call(s32[6]{0:T(128)S(1)} %stack.103.place, bf16[512,896]{1,0:T(8,128)(2,1)S(1)} %copy-done.3, bf16[512,896]{1,0:T(8,128)(2,1)S(1)} %copy-done.5, ...), custom_call_target="tpu_custom_call" | custom-call | flops 3150000128 | bytes 1 | tf_op jit(solution)/shard_map/forward/pallas_call | solution.py:75
  18.3 1.3 %collective-permute-start = (bf16[128,4096]{1,0:T(8,128)(2,1)S(1)}, bf16[128,4096]{1,0:T(8,128)(2,1)S(1)}, u32[]{:S(2)}, u32[]{:S(2)}) collective-permute-start(bf16[128,4096]{1,0:T(8,128)(2,1)S(1)} %get-tuple-element.54), channel_id=1, source_target_pairs={{0,1},{3,2},{4,5},{7,6},{8,9},{11,10},{12,13},{15,14},{16,17},{19,... | collective-permute-start | bytes 3145736 | tf_op jit(solution)/shard_map/ppermute | solution.py:232
  19.6 7.4 %collective-permute-done.3.refs_1_.outer = bf16[128,4096]{1,0:T(8,128)(2,1)S(1)} collective-permute-done((bf16[128,4096]{1,0:T(8,128)(2,1)}, bf16[128,4096]{1,0:T(8,128)(2,1)S(1)}, u32[]{:S(2)}, u32[]{:S(2)}) %collective-permute-start.3) | collective-permute-done | bytes 1048608 | tf_op jit(solution)/shard_map/ppermute | solution.py:232
  27.0 3.7 %collective-permute-start.6 = (bf16[128,4096]{1,0:T(8,128)(2,1)S(1)}, bf16[128,4096]{1,0:T(8,128)(2,1)S(1)}, u32[]{:S(2)}, u32[]{:S(2)}) collective-permute-start(bf16[128,4096]{1,0:T(8,128)(2,1)S(1)} %collective-permute-done.3.refs_1_.outer), channel_id=1, source_target_pairs={{1,2},{2,1},{5,6},{6,5},{9,10},{10,9},{13,14},{14,13},{17,18},{18,... | collective-permute-start | bytes 3145736 | tf_op jit(solution)/shard_map/ppermute | solution.py:232
  30.7 1.4 %collective-permute-start.5 = (bf16[128,4096]{1,0:T(8,128)(2,1)S(1)}, bf16[128,4096]{1,0:T(8,128)(2,1)S(1)}, u32[]{:S(2)}, u32[]{:S(2)}) collective-permute-start(bf16[128,4096]{1,0:T(8,128)(2,1)S(1)} %collective-permute-done.4.mid_m.refs_1_), channel_id=1, source_target_pairs={{1,0},{2,3},{5,4},{6,7},{9,8},{10,11},{13,12},{14,15},{17,16},{18,... | collective-permute-start | bytes 3145736 | tf_op jit(solution)/shard_map/ppermute | solution.py:232
  32.1 16.2 %collective-permute-done = bf16[128,4096]{1,0:T(8,128)(2,1)S(1)} collective-permute-done((bf16[128,4096]{1,0:T(8,128)(2,1)S(1)}, bf16[128,4096]{1,0:T(8,128)(2,1)S(1)}, u32[]{:S(2)}, u32[]{:S(2)}) %collective-permute-start) | collective-permute-done | bytes 1048608 | tf_op jit(solution)/shard_map/ppermute | solution.py:232
  48.3 0.2 add_convert_fusion.3
  48.5 3.5 %collective-permute-start.1 = (bf16[128,4096]{1,0:T(8,128)(2,1)S(1)}, bf16[128,4096]{1,0:T(8,128)(2,1)S(1)}, u32[]{:S(2)}, u32[]{:S(2)}) collective-permute-start(bf16[128,4096]{1,0:T(8,128)(2,1)S(1)} %add_convert_fusion.3), channel_id=1, source_target_pairs={{1,2},{2,1},{5,6},{6,5},{9,10},{10,9},{13,14},{14,13},{17,18},{18,... | collective-permute-start | bytes 3145736 | tf_op jit(solution)/shard_map/ppermute | solution.py:232
  52.0 0.0 collective-permute-done.6.in_ref
  52.0 0.1 split.1
  52.2 1.3 %collective-permute-start.8 = (bf16[128,2048]{1,0:T(8,128)(2,1)S(1)}, bf16[128,2048]{1,0:T(8,128)(2,1)S(1)}, u32[]{:S(2)}, u32[]{:S(2)}) collective-permute-start(bf16[128,2048]{1,0:T(8,128)(2,1)S(1)} %get-tuple-element.63.far_m.refs_3_), channel_id=1, source_target_pairs={{1,0},{2,3},{5,4},{6,7},{9,8},{10,11},{13,12},{14,15},{17,16},{18,... | collective-permute-start | bytes 1572872 | tf_op jit(solution)/shard_map/ppermute | solution.py:232
  53.5 1.3 %collective-permute-start.12 = (bf16[128,4096]{1,0:T(8,128)(2,1)S(1)}, bf16[128,4096]{1,0:T(8,128)(2,1)S(1)}, u32[]{:S(2)}, u32[]{:S(2)}) collective-permute-start(bf16[128,4096]{1,0:T(8,128)(2,1)S(1)} %get-tuple-element.81), channel_id=1, source_target_pairs={{0,1},{3,2},{4,5},{7,6},{8,9},{11,10},{12,13},{15,14},{16,17},{19,... | collective-permute-start | bytes 3145736 | tf_op jit(solution)/shard_map/ppermute | solution.py:232
  54.8 5.9 %input_grads.2 = (bf16[512,896]{1,0:T(8,128)(2,1)S(1)}, bf16[512,896]{1,0:T(8,128)(2,1)S(1)}) custom-call(s32[6]{0:T(128)S(1)} %stack.103.place, bf16[896,4096]{1,0:T(8,128)(2,1)S(1)} %copy-done.2, bf16[512,896]{1,0:T(8,128)(2,1)S(1)} %copy-done.4, bf16[512,896]{1,0:T(8,128)(2,1)S(1)} %copy-done.6, bf16[128,4096]{1,0:T(8,128)(2,1)S(1)} %copy-done, ...), custom_call_target="tpu_custom_call" | custom-call | flops 3150000128 | bytes 1 | tf_op jit(solution)/shard_map/input_grads/pallas_call | solution.py:198
  60.8 4.7 %collective-permute-start.7 = (bf16[128,2048]{1,0:T(8,128)(2,1)S(1)}, bf16[128,2048]{1,0:T(8,128)(2,1)S(1)}, u32[]{:S(2)}, u32[]{:S(2)}) collective-permute-start(bf16[128,2048]{1,0:T(8,128)(2,1)S(1)} %get-tuple-element.58.far_m.refs_5_), channel_id=1, source_target_pairs={{1,0},{2,3},{5,4},{6,7},{9,8},{10,11},{13,12},{14,15},{17,16},{18,... | collective-permute-start | bytes 1572872 | tf_op jit(solution)/shard_map/ppermute | solution.py:232
  65.4 0.0 collective-permute-done.8.far_e.refs_2_
  65.4 5.6 %weight_grad.3 = (bf16[896,256]{1,0:T(8,128)(2,1)S(1)}, bf16[896,256]{1,0:T(8,128)(2,1)S(1)}, bf16[896,256]{1,0:T(8,128)(2,1)S(1)}, bf16[896,256]{1,0:T(8,128)(2...) custom-call(s32[6]{0:T(128)S(1)} %stack.103.place, ...), custom_call_target="tpu_custom_call" | custom-call | flops 1400000000 | bytes 1 | tf_op jit(solution)/shard_map/weight_grad/pallas_call | solution.py:137
  71.1 0.1 pad_maximum_fusion.1
  71.2 0.1 collective-permute-start.10
  71.2 0.1 pad_maximum_fusion
  71.3 0.6 collective-permute-start.9
  71.9 2.6 %collective-permute-done.1 = bf16[128,4096]{1,0:T(8,128)(2,1)S(1)} collective-permute-done((bf16[128,4096]{1,0:T(8,128)(2,1)S(1)}, bf16[128,4096]{1,0:T(8,128)(2,1)S(1)}, u32[]{:S(2)}, u32[]{:S(2)}) %collective-permute-start.1) | collective-permute-done | bytes 1048608 | tf_op jit(solution)/shard_map/ppermute | solution.py:232
  74.5 0.2 add_convert_fusion.2
  74.7 0.1 collective-permute-start.2
  74.8 0.2 fusion.19
  75.0 0.6 collective-permute-start.18
  75.6 0.0 collective-permute-done.9
  75.6 0.1 fusion.16
  75.7 1.6 %collective-permute-start.17 = (bf16[2,448,256]{2,1,0:T(8,128)(2,1)S(1)}, bf16[2,448,256]{2,1,0:T(8,128)(2,1)S(1)}, u32[]{:S(2)}, u32[]{:S(2)}) collective-permute-start(bf16[2,448,256]{2,1,0:T(8,128)(2,1)S(1)} %pad_maximum_fusion.4), channel_id=1, source_target_pairs={{0,8},{4,12},{8,0},{12,4},{16,24},{20,28},{24,16},{28,20},{1,9},{5... | collective-permute-start | bytes 1376264 | tf_op jit(solution)/shard_map/ppermute | solution.py:237
  77.3 3.0 %weight_grad.4 = (bf16[896,256]{1,0:T(8,128)(2,1)S(1)}, bf16[896,256]{1,0:T(8,128)(2,1)S(1)}, bf16[896,256]{1,0:T(8,128)(2,1)S(1)}, bf16[896,256]{1,0:T(8,128)(2,1)S(1)}) custom-call(s32[6]{0:T(128)S(1)} %stack.103.place, bf16[896,512]{1,0:T(8,128)(2,1)S(1)} %get-tuple-element.73.turned_ref, bf16[128,4096]{1,0:T(8,128)(2,1)S(1)} %copy-done, ...), custom_call_target="tpu_custom_call" | custom-call | flops 1400000000 | bytes 1 | tf_op jit(solution)/shard_map/weight_grad/pallas_call | solution.py:137
  80.2 1.2 %collective-permute-done.12 = bf16[128,4096]{1,0:T(8,128)(2,1)S(1)} collective-permute-done((bf16[128,4096]{1,0:T(8,128)(2,1)S(1)}, bf16[128,4096]{1,0:T(8,128)(2,1)S(1)}, u32[]{:S(2)}, u32[]{:S(2)}) %collective-permute-start.12) | collective-permute-done | bytes 1048608 | tf_op jit(solution)/shard_map/ppermute | solution.py:232
  81.5 0.1 pad_maximum_fusion.2
  81.6 0.1 collective-permute-start.11
  81.6 0.1 pad_maximum_fusion.3
  81.7 0.6 collective-permute-start.13
  82.3 0.2 add_convert_fusion.1
  82.6 2.9 %weight_grad.5 = (bf16[896,256]{1,0:T(8,128)(2,1)S(1)}, bf16[896,256]{1,0:T(8,128)(2,1)S(1)}, bf16[896,256]{1,0:T(8,128)(2,1)S(1)}, bf16[896,256]{1,0:T(8,128)(2,1)S(1)}) custom-call(s32[6]{0:T(128)S(1)} %stack.103.place, bf16[896,512]{1,0:T(8,128)(2,1)S(1)} %get-tuple-element.73.turned_ref, bf16[128,4096]{1,0:T(8,128)(2,1)S(1)} %copy-done, ...), custom_call_target="tpu_custom_call" | custom-call | flops 1400000000 | bytes 1 | tf_op jit(solution)/shard_map/weight_grad/pallas_call | solution.py:137
  85.5 2.7 %collective-permute-start.16 = (bf16[128,4096]{1,0:T(8,128)(2,1)S(1)}, bf16[128,4096]{1,0:T(8,128)(2,1)S(1)}, u32[]{:S(2)}, u32[]{:S(2)}) collective-permute-start(bf16[128,4096]{1,0:T(8,128)(2,1)S(1)} %add_convert_fusion.1), channel_id=1, source_target_pairs={{1,2},{2,1},{5,6},{6,5},{9,10},{10,9},{13,14},{14,13},{17,18},{18,... | collective-permute-start | bytes 3145736 | tf_op jit(solution)/shard_map/ppermute | solution.py:232
  88.2 0.2 fusion.23
  88.5 1.3 %collective-permute-start.15 = (bf16[2,448,256]{2,1,0:T(8,128)(2,1)S(1)}, bf16[2,448,256]{2,1,0:T(8,128)(2,1)S(1)}, u32[]{:S(2)}, u32[]{:S(2)}) collective-permute-start(bf16[2,448,256]{2,1,0:T(8,128)(2,1)S(1)} %pad_maximum_fusion.7), channel_id=1, source_target_pairs={{0,16},{4,20},{8,24},{12,28},{16,0},{20,4},{24,8},{28,12},{1,17},{... | collective-permute-start | bytes 1376264 | tf_op jit(solution)/shard_map/ppermute | solution.py:237
  89.8 0.1 fusion.20
  89.9 0.8 collective-permute-start.14
  90.7 0.1 fusion.3
  90.8 1.3 %collective-permute-start.20 = (bf16[448,256]{1,0:T(8,128)(2,1)S(1)}, bf16[448,256]{1,0:T(8,128)(2,1)S(1)}, u32[]{:S(2)}, u32[]{:S(2)}) collective-permute-start(bf16[448,256]{1,0:T(8,128)(2,1)S(1)} %fusion.3), channel_id=1, source_target_pairs={{0,8},{4,12},{8,0},{12,4},{16,24},{20,28},{24,16},{28,20},{1,9},{5... | collective-permute-start | bytes 688136 | tf_op jit(solution)/shard_map/ppermute | solution.py:237
  92.2 0.1 fusion.4
  92.3 7.7 %input_grads.3 = (bf16[512,896]{1,0:T(8,128)(2,1)}, bf16[512,896]{1,0:T(8,128)(2,1)}) custom-call(s32[6]{0:T(128)S(1)} %stack.103.place, bf16[896,4096]{1,0:T(8,128)(2,1)S(1)} %copy-done.2, bf16[512,896]{1,0:T(8,128)(2,1)S(1)} %copy-done.4, bf16[512,896]{1,0:T(8,128)(2,1)S(1)} %copy-done.6, bf16[128,4096]{1,0:T(8,128)(2,1)S(1)} %collective-permute-done.5.mid_e.refs_0_, ...), custom_call_target="tpu_custom_call" | custom-call | flops 3150000128 | bytes 1 | tf_op jit(solution)/shard_map/input_grads/pallas_call | solution.py:198
  99.9 0.8 collective-permute-done.15
  100.7 1.3 %collective-permute-start.19 = (bf16[448,256]{1,0:T(8,128)(2,1)S(1)}, bf16[448,256]{1,0:T(8,128)(2,1)S(1)}, u32[]{:S(2)}, u32[]{:S(2)}) collective-permute-start(bf16[448,256]{1,0:T(8,128)(2,1)S(1)} %fusion.4), channel_id=1, source_target_pairs={{0,16},{4,20},{8,24},{12,28},{16,0},{20,4},{24,8},{28,12},{1,17},{... | collective-permute-start | bytes 688136 | tf_op jit(solution)/shard_map/ppermute | solution.py:237
  102.0 1.5 %collective-permute-done.14 = bf16[2,448,256]{2,1,0:T(8,128)(2,1)S(1)} collective-permute-done((bf16[2,448,256]{2,1,0:T(8,128)(2,1)S(1)}, bf16[2,448,256]{2,1,0:T(8,128)(2,1)S(1)}, u32[]{:S(2)}, u32[]{:S(2)}) %collective-permute-start.14) | collective-permute-done | bytes 458784 | tf_op jit(solution)/shard_map/ppermute | solution.py:237
  103.4 0.1 fusion.6
  103.5 0.8 collective-permute-start.22
  104.3 0.1 fusion.7
  104.4 1.6 %collective-permute-start.21 = (bf16[448,256]{1,0:T(8,128)(2,1)S(1)}, bf16[448,256]{1,0:T(8,128)(2,1)S(1)}, u32[]{:S(2)}, u32[]{:S(2)}) collective-permute-start(bf16[448,256]{1,0:T(8,128)(2,1)S(1)} %fusion.7), channel_id=1, source_target_pairs={{0,16},{4,20},{8,24},{12,28},{16,0},{20,4},{24,8},{28,12},{1,17},{... | collective-permute-start | bytes 688136 | tf_op jit(solution)/shard_map/ppermute | solution.py:237
  106.0 6.5 %collective-permute-done.16 = bf16[128,4096]{1,0:T(8,128)(2,1)S(1)} collective-permute-done((bf16[128,4096]{1,0:T(8,128)(2,1)S(1)}, bf16[128,4096]{1,0:T(8,128)(2,1)S(1)}, u32[]{:S(2)}, u32[]{:S(2)}) %collective-permute-start.16) | collective-permute-done | bytes 1048608 | tf_op jit(solution)/shard_map/ppermute | solution.py:232
  112.5 1.4 %add_convert_fusion = bf16[128,4096]{1,0:T(8,128)(2,1)} fusion(bf16[128,4096]{1,0:T(8,128)(2,1)S(1)} %collective-permute-done.16, bf16[128,4096]{1,0:T(8,128)(2,1)S(1)} %collective-permute-done.2, bf16[128,4096]{1,0:T(8,128)(2,1)S(1)} %get-tuple-element.52), kind=kLoop, calls=%fused_computation | loop fusion | flops 3145728 | bytes 4194304 | tf_op jit(solution)/shard_map/convert_element_type | solution.py:306
  113.9 0.0 collective-permute-done.20
  114.0 0.2 fusion.5
  114.2 0.2 fusion.1
  114.4 1.5 %maximum_maximum_fusion = f32[896,512]{1,0:T(8,128)} fusion(f32[448,256]{1,0:T(8,128)S(1)} %get-tuple-element.102, f32[448,256]{1,0:T(8,128)S(1)} %get-tuple-element.101, f32[448,256]{1,0:T(8,128)S(1)} %get-tuple-element.100, f32[448,256]{1,0:T(8,128)S(1)} %get-tuple-element.99), kind=kLoop, calls=%fused_computation.4 | loop fusion | flops 1376256 | bytes 3670016 | tf_op jit(solution)/shard_map/concatenate | solution.py:307
  (27 shorter events, 0.2 us)
Async XLA Ops:
  0.6 26.3 %collective-permute-start.3 = (bf16[128,4096]{1,0:T(8,128)(2,1)}, bf16[128,4096]{1,0:T(8,128)(2,1)S(1)}, u32[]{:S(2)}, u32[]{:S(2)}) collective-permute-start(bf16[128,4096]{1,0:T(8,128)(2,1)} %own.5), channel_id=1, source_target_pairs={{0,1},{1,0},{2,3},{3,2},{4,5},{5,4},{6,7},{7,6},{8,9},{9,8},{10,11... | collective-permute-start | bytes 3145736 | tf_op jit(solution)/shard_map/ppermute | solution.py:232
  1.1 29.6 %collective-permute-start.4 = (bf16[128,4096]{1,0:T(8,128)(2,1)}, bf16[128,4096]{1,0:T(8,128)(2,1)S(1)}, u32[]{:S(2)}, u32[]{:S(2)}) collective-permute-start(bf16[128,4096]{1,0:T(8,128)(2,1)} %own.5), channel_id=1, source_target_pairs={{1,2},{2,1},{5,6},{6,5},{9,10},{10,9},{13,14},{14,13},{17,18},{18,... | collective-permute-start | bytes 3145736 | tf_op jit(solution)/shard_map/ppermute | solution.py:232
  5.9 3.1 %copy-start.1 = (bf16[896,4096]{1,0:T(8,128)(2,1)S(1)}, bf16[896,4096]{1,0:T(8,128)(2,1)}, u32[]{:S(2)}) copy-start(bf16[896,4096]{1,0:T(8,128)(2,1)} %weight_ref.3) | copy-start | bytes 22020100
  9.0 1.2 %copy-start.3 = (bf16[512,896]{1,0:T(8,128)(2,1)S(1)}, bf16[512,896]{1,0:T(8,128)(2,1)}, u32[]{:S(2)}) copy-start(bf16[512,896]{1,0:T(8,128)(2,1)} %gate_ref.5) | copy-start | bytes 2752516
  10.1 1.2 %copy-start.5 = (bf16[512,896]{1,0:T(8,128)(2,1)S(1)}, bf16[512,896]{1,0:T(8,128)(2,1)}, u32[]{:S(2)}) copy-start(bf16[512,896]{1,0:T(8,128)(2,1)} %up_ref.5) | copy-start | bytes 2752516
  11.3 43.5 %copy-start.2 = (bf16[896,4096]{1,0:T(8,128)(2,1)S(1)}, bf16[896,4096]{1,0:T(8,128)(2,1)}, u32[]{:S(2)}) copy-start(bf16[896,4096]{1,0:T(8,128)(2,1)} %weight_ref.3) | copy-start | bytes 22020100
  18.3 30.0 %collective-permute-start = (bf16[128,4096]{1,0:T(8,128)(2,1)S(1)}, bf16[128,4096]{1,0:T(8,128)(2,1)S(1)}, u32[]{:S(2)}, u32[]{:S(2)}) collective-permute-start(bf16[128,4096]{1,0:T(8,128)(2,1)S(1)} %get-tuple-element.54), channel_id=1, source_target_pairs={{0,1},{3,2},{4,5},{7,6},{8,9},{11,10},{12,13},{15,14},{16,17},{19,... | collective-permute-start | bytes 3145736 | tf_op jit(solution)/shard_map/ppermute | solution.py:232
  27.0 27.8 %copy-start = (bf16[128,4096]{1,0:T(8,128)(2,1)S(1)}, bf16[128,4096]{1,0:T(8,128)(2,1)}, u32[]{:S(2)}) copy-start(bf16[128,4096]{1,0:T(8,128)(2,1)} %own.5) | copy-start | bytes 3145732
  27.0 27.9 %copy-start.4 = (bf16[512,896]{1,0:T(8,128)(2,1)S(1)}, bf16[512,896]{1,0:T(8,128)(2,1)}, u32[]{:S(2)}) copy-start(bf16[512,896]{1,0:T(8,128)(2,1)} %gate_ref.5) | copy-start | bytes 2752516
  27.0 27.9 %copy-start.6 = (bf16[512,896]{1,0:T(8,128)(2,1)S(1)}, bf16[512,896]{1,0:T(8,128)(2,1)}, u32[]{:S(2)}) copy-start(bf16[512,896]{1,0:T(8,128)(2,1)} %up_ref.5) | copy-start | bytes 2752516
  27.0 25.1 %collective-permute-start.6 = (bf16[128,4096]{1,0:T(8,128)(2,1)S(1)}, bf16[128,4096]{1,0:T(8,128)(2,1)S(1)}, u32[]{:S(2)}, u32[]{:S(2)}) collective-permute-start(bf16[128,4096]{1,0:T(8,128)(2,1)S(1)} %collective-permute-done.3.refs_1_.outer), channel_id=1, source_target_pairs={{1,2},{2,1},{5,6},{6,5},{9,10},{10,9},{13,14},{14,13},{17,18},{18,... | collective-permute-start | bytes 3145736 | tf_op jit(solution)/shard_map/ppermute | solution.py:232
  30.7 34.7 %collective-permute-start.5 = (bf16[128,4096]{1,0:T(8,128)(2,1)S(1)}, bf16[128,4096]{1,0:T(8,128)(2,1)S(1)}, u32[]{:S(2)}, u32[]{:S(2)}) collective-permute-start(bf16[128,4096]{1,0:T(8,128)(2,1)S(1)} %collective-permute-done.4.mid_m.refs_1_), channel_id=1, source_target_pairs={{1,0},{2,3},{5,4},{6,7},{9,8},{10,11},{13,12},{14,15},{17,16},{18,... | collective-permute-start | bytes 3145736 | tf_op jit(solution)/shard_map/ppermute | solution.py:232
  48.5 25.9 %collective-permute-start.1 = (bf16[128,4096]{1,0:T(8,128)(2,1)S(1)}, bf16[128,4096]{1,0:T(8,128)(2,1)S(1)}, u32[]{:S(2)}, u32[]{:S(2)}) collective-permute-start(bf16[128,4096]{1,0:T(8,128)(2,1)S(1)} %add_convert_fusion.3), channel_id=1, source_target_pairs={{1,2},{2,1},{5,6},{6,5},{9,10},{10,9},{13,14},{14,13},{17,18},{18,... | collective-permute-start | bytes 3145736 | tf_op jit(solution)/shard_map/ppermute | solution.py:232
  52.2 13.3 %collective-permute-start.8 = (bf16[128,2048]{1,0:T(8,128)(2,1)S(1)}, bf16[128,2048]{1,0:T(8,128)(2,1)S(1)}, u32[]{:S(2)}, u32[]{:S(2)}) collective-permute-start(bf16[128,2048]{1,0:T(8,128)(2,1)S(1)} %get-tuple-element.63.far_m.refs_3_), channel_id=1, source_target_pairs={{1,0},{2,3},{5,4},{6,7},{9,8},{10,11},{13,12},{14,15},{17,16},{18,... | collective-permute-start | bytes 1572872 | tf_op jit(solution)/shard_map/ppermute | solution.py:232
  53.5 28.0 %collective-permute-start.12 = (bf16[128,4096]{1,0:T(8,128)(2,1)S(1)}, bf16[128,4096]{1,0:T(8,128)(2,1)S(1)}, u32[]{:S(2)}, u32[]{:S(2)}) collective-permute-start(bf16[128,4096]{1,0:T(8,128)(2,1)S(1)} %get-tuple-element.81), channel_id=1, source_target_pairs={{0,1},{3,2},{4,5},{7,6},{8,9},{11,10},{12,13},{15,14},{16,17},{19,... | collective-permute-start | bytes 3145736 | tf_op jit(solution)/shard_map/ppermute | solution.py:232
  60.8 16.5 %collective-permute-start.7 = (bf16[128,2048]{1,0:T(8,128)(2,1)S(1)}, bf16[128,2048]{1,0:T(8,128)(2,1)S(1)}, u32[]{:S(2)}, u32[]{:S(2)}) collective-permute-start(bf16[128,2048]{1,0:T(8,128)(2,1)S(1)} %get-tuple-element.58.far_m.refs_5_), channel_id=1, source_target_pairs={{1,0},{2,3},{5,4},{6,7},{9,8},{10,11},{13,12},{14,15},{17,16},{18,... | collective-permute-start | bytes 1572872 | tf_op jit(solution)/shard_map/ppermute | solution.py:232
  71.2 3.6 %collective-permute-start.10 = (bf16[2,896,256]{2,1,0:T(8,128)(2,1)S(1)}, bf16[2,896,256]{2,1,0:T(8,128)(2,1)S(1)}, u32[]{:S(2)}, u32[]{:S(2)}) collective-permute-start(bf16[2,896,256]{2,1,0:T(8,128)(2,1)S(1)} %pad_maximum_fusion.1), channel_id=1, source_target_pairs={{0,4},{4,0},{8,12},{12,8},{16,20},{20,16},{24,28},{28,24},{1,5},{5... | collective-permute-start | bytes 2752520 | tf_op jit(solution)/shard_map/ppermute | solution.py:237
  71.3 4.3 %collective-permute-start.9 = (bf16[2,896,256]{2,1,0:T(8,128)(2,1)S(1)}, bf16[2,896,256]{2,1,0:T(8,128)(2,1)S(1)}, u32[]{:S(2)}, u32[]{:S(2)}) collective-permute-start(bf16[2,896,256]{2,1,0:T(8,128)(2,1)S(1)} %pad_maximum_fusion), channel_id=1, source_target_pairs={{0,4},{4,0},{8,12},{12,8},{16,20},{20,16},{24,28},{28,24},{1,5},{5... | collective-permute-start | bytes 2752520 | tf_op jit(solution)/shard_map/ppermute | solution.py:237
  74.7 29.7 %collective-permute-start.2 = (bf16[128,4096]{1,0:T(8,128)(2,1)S(1)}, bf16[128,4096]{1,0:T(8,128)(2,1)S(1)}, u32[]{:S(2)}, u32[]{:S(2)}) collective-permute-start(bf16[128,4096]{1,0:T(8,128)(2,1)S(1)} %add_convert_fusion.2), channel_id=1, source_target_pairs={{0,1},{1,0},{2,3},{3,2},{4,5},{5,4},{6,7},{7,6},{8,9},{9,8},{10,11... | collective-permute-start | bytes 3145736 | tf_op jit(solution)/shard_map/ppermute | solution.py:232
  75.0 14.9 %collective-permute-start.18 = (bf16[2,448,256]{2,1,0:T(8,128)(2,1)S(1)}, bf16[2,448,256]{2,1,0:T(8,128)(2,1)S(1)}, u32[]{:S(2)}, u32[]{:S(2)}) collective-permute-start(bf16[2,448,256]{2,1,0:T(8,128)(2,1)S(1)} %pad_maximum_fusion.5), channel_id=1, source_target_pairs={{0,16},{4,20},{8,24},{12,28},{16,0},{20,4},{24,8},{28,12},{1,17},{... | collective-permute-start | bytes 1376264 | tf_op jit(solution)/shard_map/ppermute | solution.py:237
  75.7 15.0 %collective-permute-start.17 = (bf16[2,448,256]{2,1,0:T(8,128)(2,1)S(1)}, bf16[2,448,256]{2,1,0:T(8,128)(2,1)S(1)}, u32[]{:S(2)}, u32[]{:S(2)}) collective-permute-start(bf16[2,448,256]{2,1,0:T(8,128)(2,1)S(1)} %pad_maximum_fusion.4), channel_id=1, source_target_pairs={{0,8},{4,12},{8,0},{12,4},{16,24},{20,28},{24,16},{28,20},{1,9},{5... | collective-permute-start | bytes 1376264 | tf_op jit(solution)/shard_map/ppermute | solution.py:237
  81.6 3.9 %collective-permute-start.11 = (bf16[2,896,256]{2,1,0:T(8,128)(2,1)S(1)}, bf16[2,896,256]{2,1,0:T(8,128)(2,1)S(1)}, u32[]{:S(2)}, u32[]{:S(2)}) collective-permute-start(bf16[2,896,256]{2,1,0:T(8,128)(2,1)S(1)} %pad_maximum_fusion.2), channel_id=1, source_target_pairs={{0,4},{4,0},{8,12},{12,8},{16,20},{20,16},{24,28},{28,24},{1,5},{5... | collective-permute-start | bytes 2752520 | tf_op jit(solution)/shard_map/ppermute | solution.py:237
  81.7 6.7 %collective-permute-start.13 = (bf16[2,896,256]{2,1,0:T(8,128)(2,1)S(1)}, bf16[2,896,256]{2,1,0:T(8,128)(2,1)S(1)}, u32[]{:S(2)}, u32[]{:S(2)}) collective-permute-start(bf16[2,896,256]{2,1,0:T(8,128)(2,1)S(1)} %pad_maximum_fusion.3), channel_id=1, source_target_pairs={{0,4},{4,0},{8,12},{12,8},{16,20},{20,16},{24,28},{28,24},{1,5},{5... | collective-permute-start | bytes 2752520 | tf_op jit(solution)/shard_map/ppermute | solution.py:237
  85.5 27.0 %collective-permute-start.16 = (bf16[128,4096]{1,0:T(8,128)(2,1)S(1)}, bf16[128,4096]{1,0:T(8,128)(2,1)S(1)}, u32[]{:S(2)}, u32[]{:S(2)}) collective-permute-start(bf16[128,4096]{1,0:T(8,128)(2,1)S(1)} %add_convert_fusion.1), channel_id=1, source_target_pairs={{1,2},{2,1},{5,6},{6,5},{9,10},{10,9},{13,14},{14,13},{17,18},{18,... | collective-permute-start | bytes 3145736 | tf_op jit(solution)/shard_map/ppermute | solution.py:232
  88.5 12.2 %collective-permute-start.15 = (bf16[2,448,256]{2,1,0:T(8,128)(2,1)S(1)}, bf16[2,448,256]{2,1,0:T(8,128)(2,1)S(1)}, u32[]{:S(2)}, u32[]{:S(2)}) collective-permute-start(bf16[2,448,256]{2,1,0:T(8,128)(2,1)S(1)} %pad_maximum_fusion.7), channel_id=1, source_target_pairs={{0,16},{4,20},{8,24},{12,28},{16,0},{20,4},{24,8},{28,12},{1,17},{... | collective-permute-start | bytes 1376264 | tf_op jit(solution)/shard_map/ppermute | solution.py:237
  89.9 13.5 %collective-permute-start.14 = (bf16[2,448,256]{2,1,0:T(8,128)(2,1)S(1)}, bf16[2,448,256]{2,1,0:T(8,128)(2,1)S(1)}, u32[]{:S(2)}, u32[]{:S(2)}) collective-permute-start(bf16[2,448,256]{2,1,0:T(8,128)(2,1)S(1)} %pad_maximum_fusion.6), channel_id=1, source_target_pairs={{0,8},{4,12},{8,0},{12,4},{16,24},{20,28},{24,16},{28,20},{1,9},{5... | collective-permute-start | bytes 1376264 | tf_op jit(solution)/shard_map/ppermute | solution.py:237
  90.8 23.1 %collective-permute-start.20 = (bf16[448,256]{1,0:T(8,128)(2,1)S(1)}, bf16[448,256]{1,0:T(8,128)(2,1)S(1)}, u32[]{:S(2)}, u32[]{:S(2)}) collective-permute-start(bf16[448,256]{1,0:T(8,128)(2,1)S(1)} %fusion.3), channel_id=1, source_target_pairs={{0,8},{4,12},{8,0},{12,4},{16,24},{20,28},{24,16},{28,20},{1,9},{5... | collective-permute-start | bytes 688136 | tf_op jit(solution)/shard_map/ppermute | solution.py:237
  100.7 13.2 %collective-permute-start.19 = (bf16[448,256]{1,0:T(8,128)(2,1)S(1)}, bf16[448,256]{1,0:T(8,128)(2,1)S(1)}, u32[]{:S(2)}, u32[]{:S(2)}) collective-permute-start(bf16[448,256]{1,0:T(8,128)(2,1)S(1)} %fusion.4), channel_id=1, source_target_pairs={{0,16},{4,20},{8,24},{12,28},{16,0},{20,4},{24,8},{28,12},{1,17},{... | collective-permute-start | bytes 688136 | tf_op jit(solution)/shard_map/ppermute | solution.py:237
  103.5 10.6 %collective-permute-start.22 = (bf16[448,256]{1,0:T(8,128)(2,1)S(1)}, bf16[448,256]{1,0:T(8,128)(2,1)S(1)}, u32[]{:S(2)}, u32[]{:S(2)}) collective-permute-start(bf16[448,256]{1,0:T(8,128)(2,1)S(1)} %fusion.6), channel_id=1, source_target_pairs={{0,8},{4,12},{8,0},{12,4},{16,24},{20,28},{24,16},{28,20},{1,9},{5... | collective-permute-start | bytes 688136 | tf_op jit(solution)/shard_map/ppermute | solution.py:237
  104.4 9.7 %collective-permute-start.21 = (bf16[448,256]{1,0:T(8,128)(2,1)S(1)}, bf16[448,256]{1,0:T(8,128)(2,1)S(1)}, u32[]{:S(2)}, u32[]{:S(2)}) collective-permute-start(bf16[448,256]{1,0:T(8,128)(2,1)S(1)} %fusion.7), channel_id=1, source_target_pairs={{0,16},{4,20},{8,24},{12,28},{16,0},{20,4},{24,8},{28,12},{1,17},{... | collective-permute-start | bytes 688136 | tf_op jit(solution)/shard_map/ppermute | solution.py:237
